TPU v7x, 32 devices: a whole 2x2x4 slice. The times are simulated.
32 devices in a mesh: ep: 16 (over z, y, x), tp: 2 (over core).
Axes of the slice: x: 2, y: 2, z: 4, core: 2. Of those that a mesh axis runs over, the one named last changes fastest.
Arguments:
- tokens: bfloat16 [16384, 1024], P('ep'), may hold values from -6 to 6
- gain_attn: bfloat16 [1024], replicated, may hold values from 0.5 to 1.5
- query_weight_matrix: bfloat16 [1024, 1024], P(None, 'tp'), may hold values from -0.75 to 0.75
- key_value_weight: bfloat16 [1024, 1024], P(None, 'tp'), may hold values from -0.75 to 0.75
- w_out: bfloat16 [1024, 1024], P('tp'), may hold values from -0.75 to 0.75
- gain_ffn: bfloat16 [1024], replicated, may hold values from 0.5 to 1.5
- w_router: bfloat16 [1024, 16], replicated, may hold values from -0.09375 to 0.09375
- w_gate_up: bfloat16 [16, 2, 1024, 512], P('ep', None, None, 'tp'), may hold values from -0.1875 to 0.1875
- w_down: bfloat16 [16, 512, 1024], P('ep', 'tp'), may hold values from -6 to 6
- routes: int32 [16384, 8], P(('ep', 'tp')), may hold values from 0 to 15, all different within a row; in each aligned block of 512 rows (0 to 511, 512 to 1023, ...) at most 384 rows name the same one
- doc_lengths: int32 [16, 4], P('ep'), may hold values from 1 to 768, 1024 in all within a row
- valid_mask: int32 [16384], P('ep'), may hold values from 0 to 1, as said below
- cotangent: bfloat16 [16384, 1024], P('ep'), may hold values from -6 to 6
Outputs:
- layer_out: bfloat16 [16384, 1024], P('ep')
- grad_tokens: float32 [16384, 1024], P('ep')
- grad_gain_attn: float32 [1024], replicated
- grad_w_query: float32 [1024, 1024], P(None, 'tp')
- grad_w_kv: float32 [1024, 1024], P(None, 'tp')
- grad_w_out: float32 [1024, 1024], P('tp')
- grad_gain_ffn: float32 [1024], replicated
- grad_w_router: float32 [1024, 16], replicated
- grad_w_gate_up: float32 [16, 2, 1024, 512], P('ep', None, None, 'tp')
- grad_w_down: float32 [16, 512, 1024], P('ep', 'tp')
- rms_stats: float32 [3], replicated
Inputs may be any that keep to these rules, and one draw needn't show every extreme that they name: `routes`: each row names 8 different experts. Within the 512 rows of one device (aligned blocks, in order) no expert is named by more than 384 rows, and in some device an expert is named by exactly 384. `doc_lengths`: the 4 lengths of a row sum to 1024; the largest of each row is exactly 768. `valid_mask`: the first token of every sequence is real.
All inputs are finite; a program needn't handle non-finite values.
Results may differ from a plain program's by a relative error of at most 0.024.
Values may be sent and summed in bfloat16 or wider, within the bound.
No kernel may reach another device: no remote copies, remote signals or barrier semaphores. Data moves between devices by JAX's collectives and lax.ppermute only.
A program may use at most 320 MiB of HBM per device.

v0:
```python
import math

import jax
import jax.numpy as jnp
from jax import lax
from jax.sharding import PartitionSpec as P

MODEL_WIDTH = 1024
QUERY_HEADS = 16
KEY_VALUE_HEADS = 8
HEAD_SIZE = 64
TOPK = 8
SEQUENCE_LENGTH = 1024
WINDOW = 1024


ATTN_SCALE = 0.015625
RESID_SCALE = 0.22
NORM_EPS = 1e-06
ROPE_BASE = 10000.0
MASKED = -1e30
highest_precision = lax.Precision.HIGHEST


def norm_rows(values):
    factor = lax.rsqrt(jnp.mean(values * values, axis=-1, keepdims=True) + NORM_EPS)
    return (values * factor, factor)


def norm_back(normed, factor, norm_gain, upstream):
    scaled_up = upstream * norm_gain
    gain_grad = jnp.sum(upstream * normed, axis=0)
    centered = scaled_up - normed * jnp.mean(scaled_up * normed, axis=-1, keepdims=True)
    return (factor * centered, gain_grad)


def doc_layout(doc_lengths):
    places = jnp.arange(SEQUENCE_LENGTH, dtype=jnp.int32)
    doc_ends = jnp.cumsum(doc_lengths, axis=1)
    passed = (places[None, :, None] >= doc_ends[:, None, :]).astype(jnp.int32)
    doc_ids = jnp.sum(passed, axis=2)
    offsets = places[None, :] - jnp.sum(passed * doc_lengths[:, None, :], axis=2)
    frequencies = jnp.exp(
        jnp.arange(HEAD_SIZE // 2, dtype=jnp.float32) * (-2.0 * math.log(ROPE_BASE) / HEAD_SIZE)
    )
    angles = offsets.reshape(-1).astype(jnp.float32)[:, None] * frequencies[None, :]
    return (doc_ids.reshape(-1), jnp.cos(angles), jnp.sin(angles))


def rotate(values, cosine_table, sine_table):
    half_width = values.shape[-1] // 2
    front_half = values[..., :half_width]
    back_half = values[..., half_width:]
    return jnp.concatenate(
        [
            front_half * cosine_table - back_half * sine_table,
            back_half * cosine_table + front_half * sine_table,
        ],
        axis=-1,
    )


def rotate_back(upstream, cosine_table, sine_table):
    half_width = upstream.shape[-1] // 2
    front_half = upstream[..., :half_width]
    back_half = upstream[..., half_width:]
    return jnp.concatenate(
        [
            front_half * cosine_table + back_half * sine_table,
            back_half * cosine_table - front_half * sine_table,
        ],
        axis=-1,
    )


def block_allowed(doc_ids, valid_mask, row_begin, key_begin, block_rows):
    query_places = row_begin - key_begin + jnp.arange(block_rows, dtype=jnp.int32)
    key_places = jnp.arange(SEQUENCE_LENGTH, dtype=jnp.int32)
    query_docs = lax.dynamic_slice_in_dim(doc_ids, row_begin, block_rows)
    key_live = valid_mask > 0
    same_doc = query_docs[:, None] == doc_ids[None, :]
    causal = key_places[None, :] <= query_places[:, None]
    within = query_places[:, None] - key_places[None, :] < WINDOW
    usable = key_live[None, :] | (key_places[None, :] == query_places[:, None])
    return same_doc & causal & within & usable


def block_scores(query_block, key_block, allowed):
    raw_scores = jnp.einsum(
        "qngd,knd->ngqk", query_block, key_block, preferred_element_type=jnp.float32
    )
    return jnp.where(allowed, raw_scores * ATTN_SCALE, MASKED)


def expert_forward(arrived, gate_up_all):
    gate_up_pre = jnp.einsum(
        "rnd,ncdf->rncf", arrived, gate_up_all, preferred_element_type=jnp.float32
    )
    gate_pre = gate_up_pre[:, :, 0]
    up_pre = gate_up_pre[:, :, 1]
    gate_sigmoid = jax.nn.sigmoid(gate_pre)
    hidden = (gate_pre * gate_sigmoid * up_pre).astype(jnp.bfloat16)
    return (gate_pre, up_pre, gate_sigmoid, hidden)


def on_device(
    tokens,
    gain_attn,
    query_weight_matrix,
    key_value_weight,
    w_out,
    gain_ffn,
    w_router,
    w_gate_up,
    w_down,
    routes,
    doc_lengths,
    valid_mask,
    cotangent,
):
    group_rows = tokens.shape[0]
    share_rows = routes.shape[0]
    experts = w_router.shape[1]
    capacity = min(share_rows, max(2, 3 * share_rows * TOPK // (2 * experts)))
    share_begin = lax.axis_index("tp") * share_rows
    block_rows = min(512, SEQUENCE_LENGTH)
    blocks = group_rows // block_rows
    per_sequence = SEQUENCE_LENGTH // block_rows
    width_q = query_weight_matrix.shape[1]
    kv_heads = key_value_weight.shape[1] // (2 * HEAD_SIZE)
    queries_per_key_head = QUERY_HEADS // KEY_VALUE_HEADS
    floats = tokens.astype(jnp.float32)
    gain_a = gain_attn.astype(jnp.float32)
    normed_a, factor_a = norm_rows(floats)
    attn_in = (normed_a * gain_a).astype(jnp.bfloat16)
    w_qkv = jnp.concatenate([query_weight_matrix, key_value_weight], axis=1)
    projected = jnp.dot(attn_in, w_qkv, preferred_element_type=jnp.float32)
    query_before_rotation = projected[:, :width_q].reshape(
        group_rows, kv_heads, queries_per_key_head, HEAD_SIZE
    )
    key_value_rows = projected[:, width_q:].reshape(group_rows, kv_heads, 2, HEAD_SIZE)
    doc_ids, cosine_table, sine_table = doc_layout(doc_lengths)
    query_rot = rotate(
        query_before_rotation, cosine_table[:, None, None, :], sine_table[:, None, None, :]
    ).astype(jnp.bfloat16)
    key_rot = rotate(
        key_value_rows[:, :, 0], cosine_table[:, None, :], sine_table[:, None, :]
    ).astype(jnp.bfloat16)
    value_rows = key_value_rows[:, :, 1].astype(jnp.bfloat16)

    def block_parts(block_index):
        row_begin = block_index * block_rows
        key_begin = block_index // per_sequence * SEQUENCE_LENGTH
        allowed = block_allowed(doc_ids, valid_mask, row_begin, key_begin, block_rows)
        query_block = lax.dynamic_slice_in_dim(query_rot, row_begin, block_rows)
        return (row_begin, allowed, query_block, key_rot, value_rows)

    def forward_block(block_index):
        row_begin, allowed, query_block, key_block, value_block = block_parts(block_index)
        scores = block_scores(query_block, key_block, allowed)
        row_max = jnp.max(scores, axis=-1, keepdims=True)
        weight = jnp.exp(scores - row_max)
        row_total = jnp.sum(weight, axis=-1, keepdims=True)
        attn_probs = (weight / row_total).astype(jnp.bfloat16)
        mixed_rows = jnp.einsum(
            "ngqk,knd->qngd", attn_probs, value_block, preferred_element_type=jnp.float32
        )
        return (
            mixed_rows.astype(jnp.bfloat16).reshape(block_rows, width_q),
            (row_max + jnp.log(row_total))[..., 0],
        )

    block_ids = jnp.arange(blocks, dtype=jnp.int32)
    mixed_blocks, log_totals = lax.map(forward_block, block_ids)
    heads_out = mixed_blocks.reshape(group_rows, width_q)
    attn_full = lax.psum(jnp.dot(heads_out, w_out, preferred_element_type=jnp.float32), "tp")
    middle = floats + RESID_SCALE * attn_full
    mid_share = lax.dynamic_slice_in_dim(middle, share_begin, share_rows)
    attn_share = lax.dynamic_slice_in_dim(attn_full, share_begin, share_rows)
    gain_f = gain_ffn.astype(jnp.float32)
    normed_f, factor_f = norm_rows(mid_share)
    ffn_in = (normed_f * gain_f).astype(jnp.bfloat16)
    logits = jnp.dot(ffn_in, w_router, preferred_element_type=jnp.float32)
    pick_table = (routes[:, :, None] == jnp.arange(experts, dtype=jnp.int32)[None, None, :]).astype(
        jnp.int32
    )
    pick_float = pick_table.astype(jnp.float32)
    picked_logits = jnp.sum(pick_float * logits[:, None, :], axis=2)
    logit_max = jnp.max(picked_logits, axis=1, keepdims=True)
    gate_weight = jnp.exp(picked_logits - logit_max)
    gate_probs = gate_weight / jnp.sum(gate_weight, axis=1, keepdims=True)
    chosen = jnp.sum(pick_table, axis=1)
    before = jnp.cumsum(chosen, axis=0) - chosen
    slot_rank = jnp.sum(pick_table * before[:, None, :], axis=2)
    slot_index = (slot_rank * experts + routes).reshape(-1)
    outgoing = (
        jnp.zeros((capacity * experts, MODEL_WIDTH), jnp.bfloat16)
        .at[slot_index]
        .set(jnp.repeat(ffn_in, TOPK, axis=0))
    )
    arrived = lax.all_to_all(
        outgoing.reshape(capacity, experts, MODEL_WIDTH),
        "ep",
        split_axis=1,
        concat_axis=0,
        tiled=True,
    )
    gate_up_all, down_all = (
        lax.all_gather(w_gate_up, "tp", axis=3, tiled=True),
        lax.all_gather(w_down, "tp", axis=1, tiled=True),
    )
    gate_pre, up_pre, gate_sigmoid, hidden = expert_forward(arrived, gate_up_all)
    expert_rows = jnp.einsum(
        "rnf,nfd->rnd", hidden, down_all, preferred_element_type=jnp.float32
    ).astype(jnp.bfloat16)
    returned = lax.all_to_all(expert_rows, "ep", split_axis=0, concat_axis=1, tiled=True)
    picked_out = jnp.take(
        returned.reshape(capacity * experts, MODEL_WIDTH), slot_index, axis=0
    ).reshape(share_rows, TOPK, MODEL_WIDTH)
    moe_share = jnp.sum(gate_probs[:, :, None] * picked_out.astype(jnp.float32), axis=1)
    out_share = mid_share + RESID_SCALE * moe_share
    moe_full = lax.all_gather(moe_share.astype(jnp.bfloat16), "tp", axis=0, tiled=True).astype(
        moe_share.dtype
    )
    layer_out = (middle + RESID_SCALE * moe_full).astype(jnp.bfloat16)
    live_rows = lax.dynamic_slice_in_dim(valid_mask, share_begin, share_rows).astype(jnp.float32)

    def masked_square(values):
        return jnp.sum(live_rows * jnp.sum(values * values, axis=1))

    stats_part = jnp.stack(
        [
            masked_square(out_share),
            masked_square(RESID_SCALE * attn_share),
            masked_square(RESID_SCALE * moe_share),
            jnp.sum(live_rows),
        ]
    )
    grad_out = cotangent.astype(jnp.float32)
    grad_moe = RESID_SCALE * lax.dynamic_slice_in_dim(grad_out, share_begin, share_rows)
    grad_gates = jnp.sum(grad_moe[:, None, :] * picked_out.astype(jnp.float32), axis=2)
    grad_picked = (gate_probs[:, :, None] * grad_moe[:, None, :]).astype(jnp.bfloat16)
    grad_outgoing = (
        jnp.zeros((capacity * experts, MODEL_WIDTH), jnp.bfloat16)
        .at[slot_index]
        .set(grad_picked.reshape(share_rows * TOPK, MODEL_WIDTH))
    )
    grad_arrived = lax.all_to_all(
        grad_outgoing.reshape(capacity, experts, MODEL_WIDTH),
        "ep",
        split_axis=1,
        concat_axis=0,
        tiled=True,
    )
    grad_hidden = jnp.einsum(
        "rnd,nfd->rnf", grad_arrived, down_all, preferred_element_type=jnp.float32
    )
    grad_down_all = jnp.einsum(
        "rnf,rnd->nfd", hidden, grad_arrived, preferred_element_type=jnp.float32
    )
    grad_gate = grad_hidden * up_pre * gate_sigmoid * (1.0 + gate_pre * (1.0 - gate_sigmoid))
    grad_up = grad_hidden * gate_pre * gate_sigmoid
    grad_gate_up = jnp.stack([grad_gate, grad_up], axis=2).astype(jnp.bfloat16)
    grad_gate_up_all = jnp.einsum(
        "rnd,rncf->ncdf", arrived, grad_gate_up, preferred_element_type=jnp.float32
    )
    grad_rows_expert = jnp.einsum(
        "rncf,ncdf->rnd", grad_gate_up, gate_up_all, preferred_element_type=jnp.float32
    ).astype(jnp.bfloat16)
    grad_returned = lax.all_to_all(grad_rows_expert, "ep", split_axis=0, concat_axis=1, tiled=True)
    grad_w_gate_up, grad_w_down = (
        lax.psum_scatter(
            grad_gate_up_all.astype(jnp.bfloat16), "tp", scatter_dimension=3, tiled=True
        ).astype(jnp.float32),
        lax.psum_scatter(
            grad_down_all.astype(jnp.bfloat16), "tp", scatter_dimension=1, tiled=True
        ).astype(jnp.float32),
    )
    grad_slots = jnp.take(
        grad_returned.reshape(capacity * experts, MODEL_WIDTH), slot_index, axis=0
    ).reshape(share_rows, TOPK, MODEL_WIDTH)
    grad_ffn_in = jnp.sum(grad_slots.astype(jnp.float32), axis=1)
    grad_sel = gate_probs * (grad_gates - jnp.sum(gate_probs * grad_gates, axis=1, keepdims=True))
    grad_logits = jnp.sum(grad_sel[:, :, None] * pick_float, axis=1)
    ffn_float = ffn_in.astype(jnp.float32)
    router_part = lax.dot_general(
        ffn_float, grad_logits, (((0,), (0,)), ((), ())), precision=highest_precision
    )
    grad_ffn_in = grad_ffn_in + lax.dot_general(
        grad_logits,
        w_router.astype(jnp.float32),
        (((1,), (1,)), ((), ())),
        precision=highest_precision,
    )
    grad_mid_moe, gain_f_part = norm_back(normed_f, factor_f, gain_f, grad_ffn_in)
    grad_mid_rows, gain_f_all, router_all, stats_all = (
        lax.all_gather(grad_mid_moe.astype(jnp.bfloat16), "tp", axis=0, tiled=True).astype(
            grad_mid_moe.dtype
        ),
        lax.all_gather(gain_f_part[None].astype(jnp.bfloat16), "tp", axis=0, tiled=True).astype(
            jnp.float32
        ),
        lax.all_gather(router_part[None].astype(jnp.bfloat16), "tp", axis=0, tiled=True).astype(
            jnp.float32
        ),
        lax.all_gather(stats_part[None].astype(jnp.bfloat16), "tp", axis=0, tiled=True).astype(
            jnp.float32
        ),
    )
    grad_middle = grad_out + grad_mid_rows
    grad_attn = (RESID_SCALE * grad_middle).astype(jnp.bfloat16)
    grad_heads = lax.dot_general(
        grad_attn, w_out, (((1,), (1,)), ((), ())), preferred_element_type=jnp.float32
    ).astype(jnp.bfloat16)
    grad_w_out = lax.dot_general(
        heads_out, grad_attn, (((0,), (0,)), ((), ())), preferred_element_type=jnp.float32
    )
    grad_heads = grad_heads.reshape(group_rows, kv_heads, queries_per_key_head, HEAD_SIZE)

    def backward_block(block_index):
        row_begin, allowed, query_block, key_block, value_block = block_parts(block_index)
        grad_block = lax.dynamic_slice_in_dim(grad_heads, row_begin, block_rows)
        lse_block = lax.dynamic_index_in_dim(log_totals, block_index, 0, keepdims=False)
        scores = block_scores(query_block, key_block, allowed)
        attn_probs = jnp.exp(scores - lse_block[..., None])
        grad_probs = jnp.einsum(
            "qngd,knd->ngqk", grad_block, value_block, preferred_element_type=jnp.float32
        )
        grad_value = jnp.einsum(
            "ngqk,qngd->knd",
            attn_probs.astype(jnp.bfloat16),
            grad_block,
            preferred_element_type=jnp.float32,
        )
        row_shift = jnp.sum(attn_probs * grad_probs, axis=-1, keepdims=True)
        grad_scores = (attn_probs * (grad_probs - row_shift)).astype(jnp.bfloat16)
        grad_query = (
            jnp.einsum("ngqk,knd->qngd", grad_scores, key_block, preferred_element_type=jnp.float32)
            * ATTN_SCALE
        )
        grad_key = (
            jnp.einsum(
                "ngqk,qngd->knd", grad_scores, query_block, preferred_element_type=jnp.float32
            )
            * ATTN_SCALE
        )
        return (grad_query, grad_key, grad_value)

    grad_query, grad_key, grad_value = lax.map(backward_block, block_ids)
    grad_query = grad_query.reshape(group_rows, kv_heads, queries_per_key_head, HEAD_SIZE)
    sequences = blocks // per_sequence
    grad_key = jnp.sum(
        grad_key.reshape(sequences, per_sequence, SEQUENCE_LENGTH, kv_heads, HEAD_SIZE), axis=1
    ).reshape(group_rows, kv_heads, HEAD_SIZE)
    grad_value = jnp.sum(
        grad_value.reshape(sequences, per_sequence, SEQUENCE_LENGTH, kv_heads, HEAD_SIZE), axis=1
    ).reshape(group_rows, kv_heads, HEAD_SIZE)
    grad_query_pre = rotate_back(
        grad_query, cosine_table[:, None, None, :], sine_table[:, None, None, :]
    )
    grad_key_pre = rotate_back(grad_key, cosine_table[:, None, :], sine_table[:, None, :])
    grad_kv = jnp.stack([grad_key_pre, grad_value], axis=2).reshape(
        group_rows, 2 * kv_heads * HEAD_SIZE
    )
    grad_proj = jnp.concatenate(
        [grad_query_pre.reshape(group_rows, width_q), grad_kv], axis=1
    ).astype(jnp.bfloat16)
    grad_attn_in = lax.psum(
        lax.dot_general(
            grad_proj, w_qkv, (((1,), (1,)), ((), ())), preferred_element_type=jnp.float32
        ).astype(jnp.bfloat16),
        "tp",
    ).astype(jnp.float32)
    grad_w_qkv = lax.dot_general(
        attn_in, grad_proj, (((0,), (0,)), ((), ())), preferred_element_type=jnp.float32
    )
    grad_from_norm, gain_a_grad = norm_back(normed_a, factor_a, gain_a, grad_attn_in)
    grad_tokens = grad_middle + grad_from_norm
    qkv_sum, out_sum, gain_a_sum, gain_f_sum, router_sum, stats_sum = (
        lax.psum(grad_w_qkv.astype(jnp.bfloat16), "ep").astype(jnp.float32),
        lax.psum(grad_w_out.astype(jnp.bfloat16), "ep").astype(jnp.float32),
        lax.psum(gain_a_grad.astype(jnp.bfloat16), "ep").astype(jnp.float32),
        lax.psum(jnp.sum(gain_f_all, axis=0).astype(jnp.bfloat16), "ep").astype(jnp.float32),
        lax.psum(jnp.sum(router_all, axis=0).astype(jnp.bfloat16), "ep").astype(jnp.float32),
        lax.psum(jnp.sum(stats_all, axis=0).astype(jnp.bfloat16), "ep").astype(jnp.float32),
    )
    rms_stats = jnp.sqrt(stats_sum[:3] / (stats_sum[3] * MODEL_WIDTH))
    return (
        layer_out,
        grad_tokens,
        gain_a_sum,
        qkv_sum[:, :width_q],
        qkv_sum[:, width_q:],
        out_sum,
        gain_f_sum,
        router_sum,
        grad_w_gate_up,
        grad_w_down,
        rms_stats,
    )


def solution(mesh):
    return jax.shard_map(
        on_device,
        mesh=mesh,
        in_specs=(
            P("ep", None),
            P(),
            P(None, "tp"),
            P(None, "tp"),
            P("tp", None),
            P(),
            P(),
            P("ep", None, None, "tp"),
            P("ep", "tp", None),
            P(("ep", "tp"), None),
            P("ep", None),
            P("ep"),
            P("ep", None),
        ),
        out_specs=(
            P("ep", None),
            P("ep", None),
            P(),
            P(None, "tp"),
            P(None, "tp"),
            P("tp", None),
            P(),
            P(),
            P("ep", None, None, "tp"),
            P("ep", "tp", None),
            P(),
        ),
        check_vma=False,
    )
```

profile of v0, /device:TPU:0, one launch (start us, length us, event | category | flops | bytes accessed | tf_op | source)
XLA Modules:
  0.0 2068.4 jit_solution(9732954341228894659)
XLA Ops:
  19.9 41.9 %while.30 = (s32[]{:T(128)}, bf16[2,512,512]{2,1,0:T(8,128)(2,1)}, f32[2,4,2,512]{3,2,1,0:T(2,128)S(1)}, s32[2]{0:T(128)S(1)}, s32[1024]{0:T(1024)S(1)}, /*index...) while((s32[]{:T(128)}, bf16[2,512,512]{2,1,0:T(8,128)(2,1)}, ...), condition=%wide.region_7.8_spmd, body=%wide.region_4.7_spmd.sunk | while | flops 1129051648 | bytes 56775056 | solution.py:174
  73.8 24.5 %all-reduce.6.cloned.1.call-done = f32[1024,1024]{1,0:T(8,128)} async-done(((f32[1024,1024]{1,0:T(8,128)}), f32[1024,1024]{1,0:T(8,128)}) %all-reduce.6.cloned.1.call-update) | async-done | bytes 4194320 | tf_op jit(solution)/shard_map/psum | solution.py:176
  103.7 26.1 %scatter_custom_fusion = bf16[6144,1024]{1,0:T(8,128)(2,1)} fusion(s32[4096]{0:T(1024)S(1)} %bitcast.357, bf16[]{:T(256)} %constant.195.clone.1, bf16[512,1024]{1,0:T(8,128)(2,1)} %get-tuple-element.454), kind=kCustom, calls=%fused_computation.97 | custom fusion | bytes 13631490 | tf_op jit(solution)/shard_map/scatter | solution.py:199
  165.7 223.8 %all-to-all-done = bf16[384,16,1024]{2,0,1:T(8,128)(2,1)} async-done(((bf16[384,16,1024]{2,0,1:T(8,128)(2,1)}), bf16[384,16,1024]{2,0,1:T(8,128)(2,1)}, u32[]{:S(2)}, u32[]{:S(2)}) %all-to-all-start) | async-done | bytes 12582944 | tf_op jit(solution)/shard_map/all_to_all | solution.py:201
  389.5 21.4 %convolution_bitcast_fusion.1 = f32[6144,1,2,512]{3,0,2,1:T(8,128)} fusion(bf16[6144,1024,1]{1,0,2:T(8,128)(2,1)} %bitcast.46, bf16[1,2,1024,512]{3,2,1,0:T(8,128)(2,1)} %all-gather.8.cloned.1.call-done), kind=kOutput, calls=%fused_computation.78 | convolution fusion | flops 12884901888 | bytes 39845888 | tf_op jit(solution)/shard_map/rnd,ncdf->rncf/dot_general | solution.py:96
  468.9 55.4 %all-to-all-start.1 = ((bf16[16,2,196608]{2,1,0:T(2,128)(2,1)}), bf16[16,2,196608]{2,1,0:T(2,128)(2,1)}, u32[]{:S(2)}, u32[]{:S(2)}) async-start(bf16[16,2,196608]{2,1,0:T(2,128)(2,1)} %reshape.808), calls=%async_computation.1 | async-start | bytes 25165824 | tf_op jit(solution)/shard_map/all_to_all | solution.py:216
  526.2 233.1 %all-to-all-done.1 = bf16[16,2,196608]{2,1,0:T(2,128)(2,1)} async-done(((bf16[16,2,196608]{2,1,0:T(2,128)(2,1)}), bf16[16,2,196608]{2,1,0:T(2,128)(2,1)}, u32[]{:S(2)}, u32[]{:S(2)}) %all-to-all-start.1) | async-done | bytes 12582944 | tf_op jit(solution)/shard_map/all_to_all | solution.py:216
  759.3 20.6 reshape.809
  793.8 20.6 copy.97
  814.4 27.1 %gather_fusion = bf16[4096,1024]{1,0:T(8,128)(2,1)} fusion(bf16[6144,1024]{1,0:T(8,128)(2,1)} %bitcast.333, s32[4096]{0:T(1024)S(1)} %fusion.107), kind=kCustom, calls=%fused_computation.clone | custom fusion | bytes 16793600 | tf_op jit(solution)/shard_map/jit(_take)/gather | solution.py:217
  847.7 27.8 %scatter_custom_fusion.1 = bf16[6144,1024]{1,0:T(8,128)(2,1)} fusion(s32[4096]{0:T(1024)S(1)} %bitcast.358, f32[512,1024]{1,0:T(8,128)S(1)} %get-tuple-element.453, f32[4096]{0:T(1024)S(1)} %div.93, bf16[]{:T(256)} %constant.195.clone.1), kind=kCustom, calls=%fused_computation.96 | custom fusion | flops 8388608 | bytes 14696450 | tf_op jit(solution)/shard_map/scatter | solution.py:246
  887.4 327.1 %all_to_all.60 = bf16[384,16,1024]{2,0,1:T(8,128)(2,1)} all-to-all(bf16[384,16,1024]{2,0,1:T(8,128)(2,1)S(1)} %copy.99), channel_id=1, replica_groups=mesh['ep'=16,'tp'=2] {'ep'}, dimensions={1} | all-to-all | bytes 25165824 | tf_op jit(solution)/shard_map/all_to_all | solution.py:248
  1214.5 24.5 %fusion.53 = (bf16[6144,1,512]{2,0,1:T(8,128)(2,1)}, bf16[6144,1,512]{2,0,1:T(8,128)(2,1)}) fusion(f32[6144,1,2,512]{3,0,2,1:T(8,128)} %convolution_bitcast_fusion.1, bf16[6144,1024]{1,0:T(8,128)(2,1)} %bitcast.339, bf16[1,512,1024]{2,1,0:T(8,128)(2,1)} %all-gather.10.cloned.1.call-done), kind=kOutput, calls=%fused_computation.84 | convolution fusion | flops 6483345408 | bytes 51380224 | tf_op jit(solution)/shard_map/rnd,nfd->rnf/dot_general | solution.py:255
  1239.0 21.1 %fusion.60 = bf16[6144,1,1024]{2,0,1:T(8,128)(2,1)} fusion(bf16[6144,1,512]{2,0,1:T(8,128)(2,1)} %get-tuple-element.435, bf16[6144,1,512]{2,0,1:T(8,128)(2,1)} %get-tuple-element.434, bf16[1,2,1024,512]{3,2,1,0:T(8,128)(2,1)S(1)} %copy-done.55), kind=kOutput, calls=%fused_computation.95 | convolution fusion | flops 12897484800 | bytes 27262976 | tf_op jit(solution)/shard_map/rncf,ncdf->rnd/dot_general | solution.py:267
  1298.1 227.4 %all-to-all-done.3 = bf16[16,2,196608]{2,1,0:T(2,128)(2,1)} async-done(((bf16[16,2,196608]{2,1,0:T(2,128)(2,1)}), bf16[16,2,196608]{2,1,0:T(2,128)(2,1)}, u32[]{:S(2)}, u32[]{:S(2)}) %all-to-all-start.3) | async-done | bytes 12582944 | tf_op jit(solution)/shard_map/all_to_all | solution.py:270
  1525.5 20.8 %reshape.807 = bf16[6144,1,1024]{2,1,0:T(2,128)(2,1)} reshape(bf16[16,2,196608]{2,1,0:T(2,128)(2,1)} %all-to-all-done.3) | data formatting | bytes 25165824
  1560.3 20.5 copy.101
  1580.8 27.1 %gather_fusion.1 = bf16[4096,1024]{1,0:T(8,128)(2,1)} fusion(bf16[6144,1024]{1,0:T(8,128)(2,1)} %bitcast.332, s32[4096]{0:T(1024)S(1)} %fusion.107), kind=kCustom, calls=%fused_computation.1.clone | custom fusion | bytes 16793600 | tf_op jit(solution)/shard_map/jit(_take)/gather | solution.py:279
  1659.8 31.6 %all-gather.14.cloned.1.call-done = bf16[1024,1024]{1,0:T(8,128)(2,1)} async-done(((bf16[512,1024]{1,0:T(8,128)(2,1)}), bf16[1024,1024]{1,0:T(8,128)(2,1)}) %all-gather.14.cloned.1.call-update) | async-done | bytes 2097168 | tf_op jit(solution)/shard_map/all_gather | solution.py:297
  1695.3 145.7 %while.31 = (s32[]{:T(128)}, f32[2,512,4,2,64]{1,0,4,3,2:T(2,128)}, f32[2,1024,4,64]{1,3,2,0:T(8,128)}, f32[2,1024,4,64]{1,3,2,0:T(8,128)}, s32[2]{0:T(128)S(1)}...) while((s32[]{:T(128)}, f32[2,512,4,2,64]{1,0,4,3,2:T(2,128)}, ...), condition=%wide.region_27.29_spmd, body=%wide.region_25.28_spmd.sunk | while | flops 2727343616 | bytes 192516688 | solution.py:349
  1748.9 19.6 dynamic_update_slice.47
  1821.2 19.6 dynamic_update_slice.47
  1903.8 84.2 %all-reduce = (bf16[1024]{0:T(1024)(128)(2,1)S(1)}, bf16[1024]{0:T(1024)(128)(2,1)S(1)}, bf16[1024,16]{0,1:T(8,128)(2,1)S(1)}, bf16[4]{0:T(256)(128)(2,1)S(1)}) all-reduce(bf16[1024]{0:T(1024)(128)(2,1)S(1)} %get-tuple-element.365, bf16[1024]{0:T(1024)(128)(2,1)S(1)} %reduce_sum.319, ...), channel_id=1, replica_groups=mesh['ep'=16,'tp'=2] {'ep'}, use_global_device_ids=true, to_apply=%region_33.35 | all-reduce | flops 18436 | bytes 73744 | tf_op jit(solution)/shard_map/psum | solution.py:382
  1996.6 59.5 %all-reduce.10.cloned.1.call-done = (bf16[1024,1024]{1,0:T(8,128)(2,1)}, bf16[512,1024]{1,0:T(8,128)(2,1)}) async-done(((bf16[1024,1024]{1,0:T(8,128)(2,1)}, bf16[512,1024]{1,0:T(8,128)(2,1)}), (bf16[1024,1024]{1,0:T(8,128)(2,1)}, bf16[512,1024]{1,0:T(8,128)(2,1)})) %all-reduce.10.cloned.1.call-update) | async-done | bytes 3145744 | tf_op jit(solution)/shard_map/psum | solution.py:380
  (308 shorter events, 472.6 us)
Async XLA Ops:
  7.2 54.6 %copy-start = (bf16[512,1024]{1,0:T(8,128)(2,1)S(1)}, bf16[512,1024]{1,0:T(8,128)(2,1)}, u32[]{:S(2)}) copy-start(bf16[512,1024]{1,0:T(8,128)(2,1)} %param.23) | copy-start | bytes 3145732
  7.2 91.0 %all-reduce.6.cloned.1.call-start = ((), (), s32[]{:S(2)}) async-start(), calls=%async_computation.6 | async-start | bytes 8388608 | tf_op jit(solution)/shard_map/psum | solution.py:176
  66.9 31.3 %copy-start.8 = (bf16[1024,1024]{1,0:T(8,128)(2,1)S(1)}, bf16[1024,1024]{1,0:T(8,128)(2,1)}, u32[]{:S(2)}) copy-start(bf16[1024,1024]{1,0:T(8,128)(2,1)} %param.19) | copy-start | bytes 6291460
  67.6 33.9 %copy-start.40 = (f32[1024]{0:T(1024)}, f32[1024]{0:T(1024)S(1)}, u32[]{:S(2)}) copy-start(f32[1024]{0:T(1024)S(1)} %convert_element_type.259) | copy-start | bytes 12292
  101.7 28.1 %copy-start.48 = (f32[512]{0:T(512)}, f32[512]{0:T(512)S(1)}, u32[]{:S(2)}) copy-start(f32[512]{0:T(512)S(1)} %add_rsqrt_fusion.1) | copy-start | bytes 6148
  144.8 244.7 %all-to-all-start = ((bf16[384,16,1024]{2,0,1:T(8,128)(2,1)}), bf16[384,16,1024]{2,0,1:T(8,128)(2,1)}, u32[]{:S(2)}, u32[]{:S(2)}) async-start(bf16[384,16,1024]{2,0,1:T(8,128)(2,1)} %copy.95), calls=%async_computation | async-start | bytes 25165824 | tf_op jit(solution)/shard_map/all_to_all | solution.py:201
  151.6 14.1 all-gather.8.cloned.1.call-start
  152.4 271.3 %all-gather.10.cloned.1.call-start = ((), (), s32[]{:S(2)}) async-start(), calls=%async_computation.8 | async-start | bytes 1572864 | tf_op jit(solution)/shard_map/all_gather | solution.py:210
  468.9 55.6 %copy-start.38 = (bf16[1024,16]{0,1:T(8,128)(2,1)S(1)}, bf16[1024,16]{0,1:T(8,128)(2,1)}, u32[]{:S(2)}) copy-start(bf16[1024,16]{0,1:T(8,128)(2,1)} %param.25) | copy-start | bytes 98308
  468.9 290.4 %all-to-all-start.1 = ((bf16[16,2,196608]{2,1,0:T(2,128)(2,1)}), bf16[16,2,196608]{2,1,0:T(2,128)(2,1)}, u32[]{:S(2)}, u32[]{:S(2)}) async-start(bf16[16,2,196608]{2,1,0:T(2,128)(2,1)} %reshape.808), calls=%async_computation.1 | async-start | bytes 25165824 | tf_op jit(solution)/shard_map/all_to_all | solution.py:216
  524.4 317.0 %copy-start.46 = (pred[4096]{0:T(1024)(128)(4,1)}, pred[4096]{0:T(1024)(128)(4,1)S(1)}, u32[]{:S(2)}) copy-start(pred[4096]{0:T(1024)(128)(4,1)S(1)} %compare_and_fusion) | copy-start | bytes 12292
  847.5 28.0 %copy-start.18 = (f32[512,8]{1,0:T(8,128)}, f32[512,8]{1,0:T(8,128)S(1)}, u32[]{:S(2)}) copy-start(f32[512,8]{1,0:T(8,128)S(1)} %copy.90) | copy-start | bytes 49156
  1292.9 232.6 %all-to-all-start.3 = ((bf16[16,2,196608]{2,1,0:T(2,128)(2,1)}), bf16[16,2,196608]{2,1,0:T(2,128)(2,1)}, u32[]{:S(2)}, u32[]{:S(2)}) async-start(bf16[16,2,196608]{2,1,0:T(2,128)(2,1)} %reshape.806), calls=%async_computation.3 | async-start | bytes 25165824 | tf_op jit(solution)/shard_map/all_to_all | solution.py:270
  1298.0 393.5 %all-gather.14.cloned.1.call-start = ((), (), s32[]{:S(2)}) async-start(), calls=%async_computation.10 | async-start | bytes 3145728 | tf_op jit(solution)/shard_map/all_gather | solution.py:297
  1298.1 324.0 %copy-start.35 = (f32[512,16]{0,1:T(8,128)}, f32[512,16]{0,1:T(8,128)S(1)}, u32[]{:S(2)}) copy-start(f32[512,16]{0,1:T(8,128)S(1)} %fusion.103) | copy-start | bytes 98308
  1580.8 27.1 %copy-start.47 = (pred[4096]{0:T(1024)(128)(4,1)S(1)}, pred[4096]{0:T(1024)(128)(4,1)}, u32[]{:S(2)}) copy-start(pred[4096]{0:T(1024)(128)(4,1)} %copy-done.46) | copy-start | bytes 12292
  1627.5 244.9 %reduce-scatter.5.cloned.1.call-start = ((), (), s32[]{:S(2)}) async-start(), calls=%async_computation.13 | async-start | bytes 1572864 | tf_op jit(solution)/shard_map/reduce_scatter | solution.py:275
  1639.9 51.6 %copy-start.11 = (bf16[1024,1024]{1,0:T(8,128)(2,1)S(1)}, bf16[1024,1024]{1,0:T(8,128)(2,1)}, u32[]{:S(2)}) copy-start(bf16[1024,1024]{1,0:T(8,128)(2,1)} %param.31) | copy-start | bytes 6291460
  1639.9 237.9 %reduce-scatter.3.cloned.1.call-start = ((), (), s32[]{:S(2)}) async-start(), calls=%async_computation.12 | async-start | bytes 3145728 | tf_op jit(solution)/shard_map/reduce_scatter | solution.py:272
  1659.0 225.3 %all-gather.12.cloned.1.call-start = ((), (), s32[]{:S(2)}) async-start(), calls=%async_computation.9 | async-start | bytes 3145728 | tf_op jit(solution)/shard_map/all_gather | solution.py:222
  1659.8 35.6 %copy-start.23 = (s32[1,1024]{1,0:T(1,128)S(1)}, s32[1,1024]{1,0:T(1,128)}, u32[]{:S(2)}) copy-start(s32[1,1024]{1,0:T(1,128)} %copy-done.22) | copy-start | bytes 12292
  1659.8 35.6 %copy-start.32 = (s32[1024]{0:T(1024)S(1)}, s32[1024]{0:T(1024)}, u32[]{:S(2)}) copy-start(s32[1024]{0:T(1024)} %param.30) | copy-start | bytes 12292
  1659.8 241.0 %all-reduce.8.cloned.1.call-start = ((), (), s32[]{:S(2)}) async-start(), calls=%async_computation.11 | async-start | bytes 4194304 | tf_op jit(solution)/shard_map/psum | solution.py:368
  1857.5 198.6 %all-reduce.10.cloned.1.call-start = ((), (), s32[]{:S(2)}) async-start(), calls=%async_computation.14 | async-start | bytes 6291456 | tf_op jit(solution)/shard_map/psum | solution.py:380
  (48 other events, 291.5 us)
Sparse Core Ops, SparseCore 0:
  67.1 31.1 all-reduce.5
  154.1 11.5 all-gather.7
  167.3 10.2 all-gather.9
  1627.6 63.8 all-gather.13
  1693.6 9.7 reduce-scatter.4
  1706.1 15.9 reduce-scatter.2
  1723.6 11.7 all-gather.11
  1857.7 43.1 all-reduce.7
  1907.0 149.1 all-reduce.9
where the time goes:
time: 2080 us; the launch traced here: 2070 us
  waiting for transfers between devices  826 us (40%)
  blocking collectives  417 us (20%)
  local copies, waits for them, and re-layouts  325 us (16%)
  matrix products  223 us (11%)
  other arithmetic  178 us (9%)
  starting transfers between devices  67.7 us (3%)
    all_to_all x1, blocking collectives, on_device(): lax.all_to_all(grad_outgoing.reshape(capacity, experts, MODEL_WIDTH), 'ep...  327 us
    all_to_all x1, waiting for transfers between devices, on_device(): lax.all_to_all(expert_rows, 'ep', split_axis=0, concat_axis=1, tiled=True)  233 us
    all_to_all x1, waiting for transfers between devices, on_device(): lax.all_to_all(grad_rows_expert, 'ep', split_axis=0, concat_axis=1, tiled...  227 us
    all_to_all x1, waiting for transfers between devices, on_device(): lax.all_to_all(outgoing.reshape(capacity, experts, MODEL_WIDTH), 'ep', sp...  224 us
    unnamed x112, local copies, waits for them, and re-layouts  112 us
    psum x1, blocking collectives, on_device(): lax.psum(gain_a_grad.astype(jnp.bfloat16), 'ep').astype(jnp.float32)  84.2 us
    psum x1, waiting for transfers between devices, on_device(): lax.psum(grad_w_qkv.astype(jnp.bfloat16), 'ep').astype(jnp.float32)  59.5 us
    all_to_all x1, starting transfers between devices, on_device(): lax.all_to_all(expert_rows, 'ep', split_axis=0, concat_axis=1, tiled=True)  55.4 us
  transfers between devices with their start and end apart: 12, of which 8 were waited for; matrix products, arithmetic and copies ran while one was open for 13% of the time, Pallas kernels for 0%

commit v1 on v0

v1 whole, which is shorter than its diff:
```python
import functools
import math

import jax
import jax.numpy as jnp
from jax import lax
from jax.experimental import pallas as pl
from jax.experimental.pallas import tpu as pltpu
from jax.sharding import PartitionSpec as P

SEQUENCE_LENGTH = 1024
WINDOW = 1024
ATTN_SCALE = 0.015625
RESID_SCALE = 0.22
NORM_EPS = 1e-06
ROPE_BASE = 10000.0
F32 = jnp.float32
BF = jnp.bfloat16
VMEM_BYTES = 60 * 1024 * 1024


def dot(a, b):
    return jnp.dot(a, b, preferred_element_type=F32)


def dot_nt(a, b):
    return lax.dot_general(a, b, (((1,), (1,)), ((), ())), preferred_element_type=F32)


def dot_tn(a, b):
    return lax.dot_general(a, b, (((0,), (0,)), ((), ())), preferred_element_type=F32)


HD = 64
NEG = -1e30
BLK = 256


def swap_halves(v, lane):
    return jnp.where(lane % HD < HD // 2, pltpu.roll(v, 128 - HD // 2, 1), pltpu.roll(v, HD // 2, 1))


def mask_bias(start, valid, i, keys):
    row = lax.broadcasted_iota(jnp.int32, (BLK, keys), 0) + i * BLK
    key = lax.broadcasted_iota(jnp.int32, (BLK, keys), 1)
    first = jnp.maximum(start[i * BLK : (i + 1) * BLK, :], row[:, :1] - (WINDOW - 1))
    ok = (key >= first) & (key <= row) & ((valid[:, :keys] > 0) | (key == row))
    return jnp.where(ok, 0.0, NEG).astype(F32)


def attn_forward_body(x, gain, wq, wkv, wo, cos, sin, start, valid, h1, q, kd, vd, o, lse, part):
    nkv = wkv.shape[1] // 128
    lane = lax.broadcasted_iota(jnp.int32, (BLK, 128), 1)
    low = lane < HD
    ga = gain[...].astype(F32)
    for i in range(x.shape[0] // BLK):
        rs = pl.ds(i * BLK, BLK)
        keys = (i + 1) * BLK
        xb = x[rs, :].astype(F32)
        r = lax.rsqrt(jnp.mean(xb * xb, axis=1, keepdims=True) + NORM_EPS)
        hb = (xb * r * ga).astype(BF)
        h1[rs, :] = hb
        qp = dot(hb, wq[...])
        kvp = dot(hb, wkv[...])
        cb, sb = cos[rs, :], sin[rs, :]
        for n in range(nkv):
            ns = slice(n * 128, (n + 1) * 128)
            qn = qp[:, ns]
            q[rs, ns] = ((qn * cb + swap_halves(qn, lane) * sb) * ATTN_SCALE).astype(BF)
            kv = kvp[:, ns]
            rot = kv * cb + swap_halves(kv, lane) * sb
            kd[rs, ns] = jnp.where(low, rot, pltpu.roll(rot, HD, 1)).astype(BF)
            vd[rs, ns] = jnp.where(low, pltpu.roll(kv, HD, 1), kv).astype(BF)
        bias = mask_bias(start, valid, i, keys)
        bias2 = jnp.concatenate([bias, bias], axis=0)
        lse_all = jnp.zeros((BLK, 128), F32)
        for n in range(nkv):
            ns = slice(n * 128, (n + 1) * 128)
            qn = q[rs, ns]
            zero = jnp.zeros_like(qn)
            q2 = jnp.concatenate([jnp.where(low, qn, zero), jnp.where(low, zero, qn)], axis=0)
            s = dot_nt(q2, kd[:keys, ns]) + bias2
            m = jnp.max(s, axis=1, keepdims=True)
            p = jnp.exp(s - m)
            total = jnp.sum(p, axis=1, keepdims=True)
            o2 = dot(p.astype(BF), vd[:keys, ns]) * (1.0 / total)
            o[rs, ns] = jnp.where(low, o2[:BLK], o2[BLK:]).astype(BF)
            l2 = m + jnp.log(total)
            lse_all = jnp.where(lane == 2 * n, l2[:BLK], jnp.where(lane == 2 * n + 1, l2[BLK:], lse_all))
        lse[rs, :] = lse_all
        part[rs, :] = dot(o[rs, :], wo[...]).astype(BF)


def attn_forward(x, gain, wq, wkv, wo, cos, sin, start, valid):
    rows, width = x.shape
    wid = wq.shape[1]
    kvw = wkv.shape[1]
    shape = jax.ShapeDtypeStruct
    return pl.pallas_call(
        attn_forward_body,
        out_shape=[
            shape((rows, width), BF),
            shape((rows, wid), BF),
            shape((rows, kvw), BF),
            shape((rows, kvw), BF),
            shape((rows, wid), BF),
            shape((rows, 128), F32),
            shape((rows, width), BF),
        ],
        compiler_params=pltpu.CompilerParams(vmem_limit_bytes=VMEM_BYTES),
        cost_estimate=pl.CostEstimate(
            flops=2 * rows * width * 3 * wid + 4 * rows * rows * 4 * wid,
            bytes_accessed=12 * rows * width,
            transcendentals=rows * rows * wid // 128,
        ),
        name="attention_forward",
    )(x, gain, wq, wkv, wo, cos, sin, start, valid)


def attn_backward_body(first, q, kd, vd, do, lse, h1, cos, sin, start, valid, dq, dkv, gw, dk, dv):
    nkv = kd.shape[1] // 128
    wid = q.shape[1]
    lane = lax.broadcasted_iota(jnp.int32, (BLK, 128), 1)
    low = lane < HD
    dk[...] = jnp.zeros_like(dk)
    dv[...] = jnp.zeros_like(dv)
    nb = q.shape[0] // BLK
    for i in range(nb):
        rs = pl.ds(i * BLK, BLK)
        keys = (i + 1) * BLK
        cb, sb = cos[rs, :], sin[rs, :]
        bias = mask_bias(start, valid, i, keys)
        bias2 = jnp.concatenate([bias, bias], axis=0)
        lse_i = lse[rs, :]
        for n in range(nkv):
            ns = slice(n * 128, (n + 1) * 128)
            qn, dn = q[rs, ns], do[rs, ns]
            zero = jnp.zeros_like(qn)
            q2 = jnp.concatenate([jnp.where(low, qn, zero), jnp.where(low, zero, qn)], axis=0)
            d2 = jnp.concatenate([jnp.where(low, dn, zero), jnp.where(low, zero, dn)], axis=0)
            h = 2 * (first + n)
            l2 = jnp.concatenate([lse_i[:, h : h + 1], lse_i[:, h + 1 : h + 2]], axis=0)
            p = jnp.exp(dot_nt(q2, kd[:keys, ns]) + bias2 - l2)
            dp = dot_nt(d2, vd[:keys, ns])
            shift = jnp.sum(p * dp, axis=1, keepdims=True)
            ds = (p * (dp - shift)).astype(BF)
            dv[:keys, ns] += dot_tn(p.astype(BF), d2)
            dk[:keys, ns] += dot_tn(ds, q2)
            dq2 = dot(ds, kd[:keys, ns])
            dqn = jnp.where(low, dq2[:BLK], dq2[BLK:]) * ATTN_SCALE
            dq[rs, ns] = (dqn * cb - swap_halves(dqn, lane) * sb).astype(BF)
    for i in range(nb):
        rs = pl.ds(i * BLK, BLK)
        cb, sb = cos[rs, :], sin[rs, :]
        for n in range(nkv):
            ns = slice(n * 128, (n + 1) * 128)
            kk = dk[rs, ns]
            kk = kk + pltpu.roll(kk, HD, 1)
            vv = dv[rs, ns]
            vv = vv + pltpu.roll(vv, HD, 1)
            dkv[rs, ns] = jnp.where(low, kk * cb - swap_halves(kk, lane) * sb, vv).astype(BF)
    gw[:, :wid] = dot_tn(h1[...], dq[...]).astype(BF)
    gw[:, wid:] = dot_tn(h1[...], dkv[...]).astype(BF)


def attn_backward(first, count, q, kd, vd, do, lse, h1, cos, sin, start, valid):
    rows, width = h1.shape
    w = count * 128
    shape = jax.ShapeDtypeStruct
    part = pl.BlockSpec((rows, w), lambda _: (0, first // count))
    whole = lambda v: pl.BlockSpec(v.shape, lambda _: (0, 0))
    return pl.pallas_call(
        functools.partial(attn_backward_body, first),
        grid=(1,),
        in_specs=[part] * 4 + [whole(v) for v in (lse, h1, cos, sin, start, valid)],
        out_specs=[
            pl.BlockSpec((rows, w), lambda _: (0, 0)),
            pl.BlockSpec((rows, w), lambda _: (0, 0)),
            pl.BlockSpec((width, 2 * w), lambda _: (0, 0)),
        ],
        out_shape=[shape((rows, w), BF), shape((rows, w), BF), shape((width, 2 * w), BF)],
        scratch_shapes=[pltpu.VMEM((rows, w), F32), pltpu.VMEM((rows, w), F32)],
        compiler_params=pltpu.CompilerParams(vmem_limit_bytes=VMEM_BYTES),
        cost_estimate=pl.CostEstimate(
            flops=4 * rows * width * w + 10 * rows * rows * 2 * w * 2,
            bytes_accessed=10 * rows * width,
            transcendentals=rows * rows * w // 128,
        ),
        name="attention_backward",
    )(q, kd, vd, do, lse, h1, cos, sin, start, valid)


def tables(doc_lengths):
    lengths = doc_lengths.reshape(-1)
    places = jnp.arange(SEQUENCE_LENGTH, dtype=jnp.int32)
    ends = jnp.cumsum(lengths)
    passed = (places[:, None] >= ends[None, :]).astype(jnp.int32)
    start = jnp.sum(passed * lengths[None, :], axis=1)
    offsets = (places - start).astype(F32)
    step = jnp.arange(128, dtype=jnp.int32)
    frequencies = jnp.exp((step % 32).astype(F32) * (-2.0 * math.log(ROPE_BASE) / HD))
    angles = offsets[:, None] * frequencies[None, :]
    sine = jnp.sin(angles)
    return jnp.cos(angles), jnp.where(step[None, :] % HD < HD // 2, -sine, sine), start[:, None]


def whole_block(v):
    return pl.BlockSpec(v.shape, lambda *_: (0,) * len(v.shape))


def gate_table(h2, routes, wr, lane):
    mask = routes[:, 0:1] == lane
    for k in range(1, routes.shape[1]):
        mask = mask | (routes[:, k : k + 1] == lane)
    sel = jnp.where(mask, dot(h2[...], wr[...]), -jnp.inf)
    weight = jnp.exp(sel - jnp.max(sel, axis=1, keepdims=True))
    return weight / jnp.sum(weight, axis=1, keepdims=True)


def middle_body(x, own, other, gain, live, mid, h2, stats):
    attn = RESID_SCALE * (own[...].astype(F32) + other[...].astype(F32))
    m = x[...].astype(F32) + attn
    mid[...] = m
    r = lax.rsqrt(jnp.mean(m * m, axis=1, keepdims=True) + NORM_EPS)
    h2[...] = (m * r * gain[...].astype(F32)).astype(BF)
    v = live[...]
    total = jnp.sum(v * jnp.sum(attn * attn, axis=1, keepdims=True))
    lane = lax.broadcasted_iota(jnp.int32, stats.shape, 1)
    stats[...] = jnp.where(lane == 1, total, jnp.where(lane == 3, jnp.sum(v), 0.0))


def middle_norm(x, own, other, gain, live):
    rows, width = x.shape
    shape = jax.ShapeDtypeStruct
    return pl.pallas_call(
        middle_body,
        out_shape=[shape((rows, width), F32), shape((rows, width), BF), shape((8, 128), F32)],
        compiler_params=pltpu.CompilerParams(vmem_limit_bytes=VMEM_BYTES),
        cost_estimate=pl.CostEstimate(flops=10 * rows * width, bytes_accessed=12 * rows * width, transcendentals=rows),
        name="middle_norm",
    )(x, own, other, gain, live)


def experts_body(nchunk, halves, rt, *refs):
    ids, h2, g, routes, wr = refs[:5]
    gus = refs[5 : 5 + nchunk]
    downs = refs[5 + nchunk : 5 + 2 * nchunk]
    moe, dx, dgt, gat, dgu = refs[5 + 2 * nchunk : 10 + 2 * nchunk]
    gates, dgacc, macc, xacc, gbuf, dbuf, sem = refs[10 + 2 * nchunk :]
    c = pl.program_id(0)
    rows = h2.shape[0]
    f = gbuf.shape[3]
    lane = lax.broadcasted_iota(jnp.int32, (rows, 128), 1)

    def copies(k, slot):
        return (
            pltpu.make_async_copy(gus[k], gbuf.at[slot], sem.at[slot, 0]),
            pltpu.make_async_copy(downs[k], dbuf.at[slot], sem.at[slot, 1]),
        )

    @pl.when(c == 0)
    def _():
        for copy in copies(0, 0):
            copy.start()
        gates[...] = gate_table(h2, routes, wr, lane)
        dgacc[...] = jnp.zeros_like(dgacc)
        macc[...] = jnp.zeros_like(macc)
        xacc[...] = jnp.zeros_like(xacc)

    for k in range(1, nchunk):

        @pl.when(c + 1 == k)
        def _(k=k):
            for copy in copies(k, k % 2):
                copy.start()

    slot = lax.rem(c, 2)
    for copy in copies(0, slot):
        copy.wait()
    r = c // halves
    e = ids[r]
    ln = lane[:rt]
    for i in range(rows // rt):
        rs = pl.ds(i * rt, rt)
        hb = h2[rs, :]
        gp = dot(hb, gbuf[slot, 0])
        up = dot(hb, gbuf[slot, 1])
        u = dot_nt(g[rs, :], dbuf[slot])
        gate = jnp.sum(jnp.where(ln == e, gates[rs, :], 0.0), axis=1, keepdims=True)
        sg = jax.nn.sigmoid(gp)
        sl = gp * sg
        act = sl * up
        ga = (gate * act).astype(BF)
        dgacc[rs, :] += jnp.where(ln == r, jnp.sum(act * u, axis=1, keepdims=True) * RESID_SCALE, 0.0)
        da = (RESID_SCALE * gate) * u
        dgp = (da * up * (sg + sl * (1.0 - sg))).astype(BF)
        dup = (da * sl).astype(BF)
        gat[0, :, rs] = ga.T
        dgu[0, rs, :f] = dgp
        dgu[0, rs, f:] = dup
        macc[rs, :] += dot(ga, dbuf[slot])
        xacc[rs, :] += dot_nt(dgp, gbuf[slot, 0]) + dot_nt(dup, gbuf[slot, 1])

    @pl.when(c == nchunk - 1)
    def _():
        moe[...] = macc[...].astype(BF)
        dx[...] = xacc[...].astype(BF)
        dgt[...] = dgacc[...].T[: dgt.shape[0]]


def experts(ids, h2, g, routes, wr, gus, downs, halves):
    rows, width = h2.shape
    nchunk = len(gus)
    f = gus[0].shape[2]
    deep = 8 * -(-nchunk // halves // 8)
    shape = jax.ShapeDtypeStruct
    return pl.pallas_call(
        functools.partial(experts_body, nchunk, halves, min(rows, 512)),
        grid_spec=pltpu.PrefetchScalarGridSpec(
            num_scalar_prefetch=1,
            grid=(nchunk,),
            in_specs=[whole_block(v) for v in (h2, g, routes, wr)]
            + [pl.BlockSpec(memory_space=pl.ANY)] * (2 * nchunk),
            out_specs=[
                pl.BlockSpec((rows, width), lambda c, _: (0, 0)),
                pl.BlockSpec((rows, width), lambda c, _: (0, 0)),
                pl.BlockSpec((deep, rows), lambda c, _: (0, 0)),
                pl.BlockSpec((1, f, rows), lambda c, _: (c, 0, 0)),
                pl.BlockSpec((1, rows, 2 * f), lambda c, _: (c, 0, 0)),
            ],
            scratch_shapes=[
                pltpu.VMEM((rows, 128), F32),
                pltpu.VMEM((rows, 128), F32),
                pltpu.VMEM((rows, width), F32),
                pltpu.VMEM((rows, width), F32),
                pltpu.VMEM((2, 2, width, f), BF),
                pltpu.VMEM((2, f, width), BF),
                pltpu.SemaphoreType.DMA((2, 2)),
            ],
        ),
        out_shape=[
            shape((rows, width), BF),
            shape((rows, width), BF),
            shape((deep, rows), F32),
            shape((nchunk, f, rows), BF),
            shape((nchunk, rows, 2 * f), BF),
        ],
        compiler_params=pltpu.CompilerParams(vmem_limit_bytes=VMEM_BYTES),
        cost_estimate=pl.CostEstimate(
            flops=12 * rows * width * f * nchunk,
            bytes_accessed=6 * nchunk * width * f + 12 * rows * width,
            transcendentals=rows * f * nchunk,
        ),
        name="experts",
    )(ids, h2, g, routes, wr, *gus, *downs)


def weight_grads_body(nb, *refs):
    h2 = refs[:nb]
    g = refs[nb : 2 * nb]
    gat = refs[2 * nb : 3 * nb]
    dgu = refs[3 * nb : 4 * nb]
    wgu, wd = refs[4 * nb :]
    f = wd.shape[1]
    acc = sum(dot_tn(h2[b][...], dgu[b][0]) for b in range(nb))
    wgu[0, 0] = acc[:, :f].astype(BF)
    wgu[0, 1] = acc[:, f:].astype(BF)
    acc = sum(dot(gat[b][0], g[b][...]) for b in range(nb))
    wd[0] = (acc * RESID_SCALE).astype(BF)


def weight_grads(h2s, gs, gats, dgus, first, count):
    nb = len(h2s)
    rows, width = h2s[0].shape
    f = gats[0].shape[1]
    shape = jax.ShapeDtypeStruct
    return pl.pallas_call(
        functools.partial(weight_grads_body, nb),
        grid=(count,),
        in_specs=[whole_block(v) for v in (*h2s, *gs)]
        + [pl.BlockSpec((1, f, rows), lambda c: (first + c, 0, 0))] * nb
        + [pl.BlockSpec((1, rows, 2 * f), lambda c: (first + c, 0, 0))] * nb,
        out_specs=[
            pl.BlockSpec((1, 2, width, f), lambda c: (c, 0, 0, 0)),
            pl.BlockSpec((1, f, width), lambda c: (c, 0, 0)),
        ],
        out_shape=[shape((count, 2, width, f), BF), shape((count, f, width), BF)],
        compiler_params=pltpu.CompilerParams(vmem_limit_bytes=VMEM_BYTES),
        cost_estimate=pl.CostEstimate(
            flops=6 * rows * nb * width * f * count,
            bytes_accessed=6 * count * width * f + 4 * rows * nb * width,
            transcendentals=0,
        ),
        name="expert_weight_grads",
    )(*h2s, *gs, *gats, *dgus)


def middle_back_body(nb, nlocal, nexp, *refs):
    ids, h2, mid, gain, routes, wr = refs[:6]
    dxs = refs[6 : 6 + nb]
    dgts = refs[6 + nb : 6 + 2 * nb]
    gm, small = refs[6 + 2 * nb :]
    rows = h2.shape[0]
    lane = lax.broadcasted_iota(jnp.int32, (rows, 128), 1)
    gates = gate_table(h2, routes, wr, lane)
    dgate = jnp.zeros((rows, 128), F32)
    for b in range(nb):
        cols = dgts[b][...].T
        for r in range(nlocal):
            dgate = jnp.where(lane == ids[b * nlocal + r], cols[:, r : r + 1], dgate)
    dsel = gates * (dgate - jnp.sum(gates * dgate, axis=1, keepdims=True))
    high = dsel.astype(BF)
    rest = (dsel - high.astype(F32)).astype(BF)
    small[:nexp, :] = (dot_tn(high, h2[...]) + dot_tn(rest, h2[...]))[:nexp]
    dh = dot_nt(high, wr[...]) + dot_nt(rest, wr[...])
    for b in range(nb):
        dh = dh + dxs[b][...].astype(F32)
    m = mid[...]
    r2 = lax.rsqrt(jnp.mean(m * m, axis=1, keepdims=True) + NORM_EPS)
    xhat = m * r2
    small[nexp : nexp + 8, :] = jnp.broadcast_to(jnp.sum(dh * xhat, axis=0, keepdims=True), (8, dh.shape[1]))
    su = dh * gain[...].astype(F32)
    gm[...] = (r2 * (su - xhat * jnp.mean(su * xhat, axis=1, keepdims=True))).astype(BF)


def middle_back(ids, h2, mid, gain, routes, wr, dxs, dgts, nlocal, nexp):
    rows, width = h2.shape
    shape = jax.ShapeDtypeStruct
    args = (h2, mid, gain, routes, wr, *dxs, *dgts)
    return pl.pallas_call(
        functools.partial(middle_back_body, len(dxs), nlocal, nexp),
        in_specs=[pl.BlockSpec(memory_space=pltpu.SMEM)] + [pl.BlockSpec(memory_space=pltpu.VMEM)] * len(args),
        out_shape=[shape((rows, width), BF), shape((nexp + 8, width), F32)],
        compiler_params=pltpu.CompilerParams(vmem_limit_bytes=VMEM_BYTES),
        cost_estimate=pl.CostEstimate(flops=40 * rows * width, bytes_accessed=20 * rows * width, transcendentals=rows),
        name="middle_back",
    )(ids, *args)


def out_back_body(cot, gm, wo, o, do, gwo):
    rows = cot.shape[0]
    da = (RESID_SCALE * (cot[...].astype(F32) + gm[...].astype(F32))).astype(BF)
    do[...] = dot_nt(da, wo[...]).astype(BF)
    gwo[...] = dot_tn(o[...], da).astype(BF)


def out_back(cot, gm, wo, o):
    rows, width = cot.shape
    w = wo.shape[0]
    shape = jax.ShapeDtypeStruct
    return pl.pallas_call(
        out_back_body,
        out_shape=[shape((rows, w), BF), shape((w, width), BF)],
        compiler_params=pltpu.CompilerParams(vmem_limit_bytes=VMEM_BYTES),
        cost_estimate=pl.CostEstimate(flops=4 * rows * width * w, bytes_accessed=10 * rows * width, transcendentals=0),
        name="attention_out_back",
    )(cot, gm, wo, o)


def input_back_body(nq, x, wq, wkv, *refs):
    dq = refs[:nq]
    dkv = refs[nq : 2 * nq]
    dh, ga = refs[2 * nq :]
    xb = x[...].astype(F32)
    xhat = xb * lax.rsqrt(jnp.mean(xb * xb, axis=1, keepdims=True) + NORM_EPS)
    acc = None
    for w, parts in ((wq, dq), (wkv, dkv)):
        at = 0
        for part in parts:
            n = part.shape[1]
            term = dot_nt(part[...], w[:, at : at + n])
            acc = term if acc is None else acc + term
            at += n
    dh[...] = acc.astype(BF)
    ga[...] = jnp.broadcast_to(jnp.sum(acc * xhat, axis=0, keepdims=True), ga.shape)


def input_back(x, wq, wkv, dqs, dkvs):
    rows, width = x.shape
    shape = jax.ShapeDtypeStruct
    return pl.pallas_call(
        functools.partial(input_back_body, len(dqs)),
        out_shape=[shape((rows, width), BF), shape((8, width), F32)],
        compiler_params=pltpu.CompilerParams(vmem_limit_bytes=VMEM_BYTES),
        cost_estimate=pl.CostEstimate(
            flops=4 * rows * width * wq.shape[1], bytes_accessed=10 * rows * width, transcendentals=rows
        ),
        name="input_back",
    )(x, wq, wkv, *dqs, *dkvs)


def token_grads_body(x, cot, gm, own, other, gain, out):
    xb = x[...].astype(F32)
    r = lax.rsqrt(jnp.mean(xb * xb, axis=1, keepdims=True) + NORM_EPS)
    xhat = xb * r
    su = (own[...].astype(F32) + other[...].astype(F32)) * gain[...].astype(F32)
    norm = r * (su - xhat * jnp.mean(su * xhat, axis=1, keepdims=True))
    out[...] = cot[...].astype(F32) + gm[...].astype(F32) + norm


def token_grads(x, cot, gm, own, other, gain):
    rows, width = x.shape
    rt = min(rows, 128)
    block = pl.BlockSpec((rt, width), lambda i: (i, 0))
    return pl.pallas_call(
        token_grads_body,
        grid=(rows // rt,),
        in_specs=[block] * 5 + [whole_block(gain)],
        out_specs=block,
        out_shape=jax.ShapeDtypeStruct((rows, width), F32),
        cost_estimate=pl.CostEstimate(flops=12 * rows * width, bytes_accessed=14 * rows * width, transcendentals=rows),
        name="token_grads",
    )(x, cot, gm, own, other, gain)


def layer_out_body(nb, *refs):
    mid, live = refs[:2]
    moes = refs[2 : 2 + nb]
    out, stats = refs[2 + nb :]
    moe = sum(m[...].astype(F32) for m in moes) * RESID_SCALE
    outf = mid[...] + moe
    out[...] = outf.astype(BF)
    v = live[...]
    s0 = jnp.sum(v * jnp.sum(outf * outf, axis=1, keepdims=True))
    s2 = jnp.sum(v * jnp.sum(moe * moe, axis=1, keepdims=True))
    lane = lax.broadcasted_iota(jnp.int32, stats.shape, 1)
    stats[...] = jnp.where(lane == 0, s0, jnp.where(lane == 2, s2, 0.0))


def layer_out_share(mid, live, moes):
    rows, width = mid.shape
    shape = jax.ShapeDtypeStruct
    return pl.pallas_call(
        functools.partial(layer_out_body, len(moes)),
        out_shape=[shape((rows, width), BF), shape((8, 128), F32)],
        compiler_params=pltpu.CompilerParams(vmem_limit_bytes=VMEM_BYTES),
        cost_estimate=pl.CostEstimate(flops=12 * rows * width, bytes_accessed=14 * rows * width, transcendentals=0),
        name="layer_out",
    )(mid, live, *moes)


def on_device(
    tokens,
    gain_attn,
    query_weight_matrix,
    key_value_weight,
    w_out,
    gain_ffn,
    w_router,
    w_gate_up,
    w_down,
    routes,
    doc_lengths,
    valid_mask,
    cotangent,
):
    rows, width = tokens.shape
    share = routes.shape[0]
    n_ep, n_tp = lax.axis_size("ep"), lax.axis_size("tp")
    nexp = w_router.shape[1]
    inner = math.gcd(n_ep, 4)
    outer = n_ep // inner
    me, core = lax.axis_index("ep"), lax.axis_index("tp")
    me_in, me_out = me % inner, me // inner
    begin = core * share

    def across(v, k):
        return lax.ppermute(v, "ep", [(i, i ^ k) for i in range(n_ep)])

    def along(v, k):
        return lax.ppermute(v, "ep", [(i, (i + k * inner) % n_ep) for i in range(n_ep)])

    def swap(v):
        return lax.ppermute(v, "tp", [(0, 1), (1, 0)])

    def plane(v):
        return [v] + [across(v, k) for k in range(1, inner)]

    def cut(v, at, size):
        return lax.dynamic_slice_in_dim(v, at, size)

    def total(terms):
        acc = terms[0].astype(F32)
        for term in terms[1:]:
            acc = acc + term.astype(F32)
        return acc

    def core_rows(v):
        if n_tp != 2:
            return lax.all_gather(v, "tp", axis=0, tiled=True)
        other = swap(v)
        return jnp.where(core == 0, jnp.concatenate([v, other]), jnp.concatenate([other, v]))

    def sum_small(v):
        v = total(plane(v))
        v = total([v] + [along(v, k) for k in range(1, outer)])
        return v + swap(v) if n_tp == 2 else lax.psum(v, "tp")

    def sum_ep(v):
        size = v.shape[0] // inner
        part = total(
            [cut(v, me_in * size, size)]
            + [across(cut(v, (me_in ^ k) * size, size), k) for k in range(1, inner)]
        ).astype(BF)
        small = size // outer
        mine = total(
            [cut(part, me_out * small, small)]
            + [along(cut(part, (me_out + k) % outer * small, small), k) for k in range(1, outer)]
        ).astype(BF)
        part = lax.dynamic_update_slice_in_dim(jnp.zeros_like(part), mine, me_out * small, 0)
        for k in range(1, outer):
            part = lax.dynamic_update_slice_in_dim(part, along(mine, k), (me_out - k) % outer * small, 0)
        v = lax.dynamic_update_slice_in_dim(jnp.zeros_like(v), part, me_in * size, 0)
        for k in range(1, inner):
            v = lax.dynamic_update_slice_in_dim(v, across(part, k), (me_in ^ k) * size, 0)
        return v

    def column(v):
        held = [v]
        for _ in range(1, outer):
            held.append(along(held[-1], 1))
        return held

    gus, downs = [], []
    for gu, down in zip(column(w_gate_up[0]), column(w_down[0]), strict=True):
        if n_tp == 2:
            gus += [gu, swap(gu)]
            downs += [down, swap(down)]
        else:
            gus.append(lax.all_gather(gu, "tp", axis=2, tiled=True))
            downs.append(lax.all_gather(down, "tp", axis=0, tiled=True))
    halves = 2 if n_tp == 2 else 1
    gs = plane(cut(cotangent, begin, share))
    routes_all = plane(routes)
    local = jnp.arange(outer, dtype=jnp.int32) * inner
    ids = (me - local) % n_ep
    ids_all = jnp.concatenate([((me ^ k) - local) % n_ep for k in range(inner)])

    cos, sin, start = tables(doc_lengths)
    valid_row = valid_mask[None, :]
    live = cut(valid_mask, begin, share).astype(F32)[:, None]
    gain_a, gain_f = gain_attn[None, :], gain_ffn[None, :]
    wr = jnp.pad(w_router, ((0, 0), (0, 128 - nexp)))

    h1, q, kd, vd, o, lse, part = attn_forward(
        tokens, gain_a, query_weight_matrix, key_value_weight, w_out, cos, sin, start, valid_row
    )
    if n_tp == 2:
        own, other = cut(part, begin, share), swap(cut(part, (1 - core) * share, share))
    else:
        own = lax.psum_scatter(part.astype(F32), "tp", scatter_dimension=0, tiled=True)
        other = jnp.zeros_like(own)
    mid, h2, stats = middle_norm(cut(tokens, begin, share), own, other, gain_f, live)
    h2s = plane(h2)

    moes, dxs, dgts, gats, dgus = [], [], [], [], []
    for k in range(inner):
        moe, dx, dgt, gat, dgu = experts(ids, h2s[k], gs[k], routes_all[k], wr, gus, downs, halves)
        moes.append(moe if k == 0 else across(moe, k))
        dxs.append(dx if k == 0 else across(dx, k))
        dgts.append(dgt if k == 0 else across(dgt, k))
        gats.append(gat)
        dgus.append(dgu)

    def expert_grads(r):
        dgu_w, down_w = weight_grads(h2s, gs, gats, dgus, r * halves, halves)
        if n_tp == 2:
            return total([dgu_w[0], swap(dgu_w[1])]), total([down_w[0], swap(down_w[1])])
        return (
            lax.psum_scatter(dgu_w[0].astype(F32), "tp", scatter_dimension=2, tiled=True),
            lax.psum_scatter(down_w[0].astype(F32), "tp", scatter_dimension=0, tiled=True),
        )

    sums = expert_grads(1 % outer)
    for r in range(2, outer + 1):
        sent = [along(v.astype(BF), 1) for v in sums]
        sums = [a.astype(F32) + b for a, b in zip(sent, expert_grads(r % outer), strict=True)]
    grad_w_gate_up, grad_w_down = sums[0][None], sums[1][None]

    gm_share, small = middle_back(ids_all, h2, mid, gain_f, routes, wr, dxs, dgts, outer, nexp)
    gm = core_rows(gm_share)
    small_sum = sum_small(small)
    do, gwo = out_back(cotangent, gm, w_out, o)
    out_sum = sum_ep(gwo)
    out_share, stats_out = layer_out_share(mid, live, moes)
    layer_out = core_rows(out_share)

    nkv = kd.shape[1] // 128
    groups = 2 if nkv % 2 == 0 else 1
    each = nkv // groups
    dqs, dkvs, gws = [], [], []
    for n in range(groups):
        dq, dkv, gw = attn_backward(n * each, each, q, kd, vd, do, lse, h1, cos, sin, start, valid_row)
        dqs.append(dq)
        dkvs.append(dkv)
        gws.append(sum_ep(gw))
    dh1, ga_part = input_back(tokens, query_weight_matrix, key_value_weight, dqs, dkvs)
    if n_tp == 2:
        dh_other = swap(dh1)
    else:
        dh1, dh_other = lax.psum(dh1.astype(F32), "tp"), jnp.zeros_like(dh1)
    grad_tokens = token_grads(tokens, cotangent, gm, dh1, dh_other, gain_a)
    last = jnp.concatenate([ga_part[:1], jnp.pad((stats + stats_out)[:1], ((0, 0), (0, width - 128)))])
    last_sum = sum_small(last)
    s = last_sum[1]
    w = each * 128
    return (
        layer_out,
        grad_tokens,
        last_sum[0],
        jnp.concatenate([v[:, :w] for v in gws], axis=1).astype(F32),
        jnp.concatenate([v[:, w:] for v in gws], axis=1).astype(F32),
        out_sum.astype(F32),
        small_sum[nexp],
        small_sum[:nexp].T,
        grad_w_gate_up,
        grad_w_down,
        jnp.sqrt(s[:3] / (s[3] * width)),
    )


def solution(mesh):
    return jax.shard_map(
        on_device,
        mesh=mesh,
        in_specs=(
            P("ep", None),
            P(),
            P(None, "tp"),
            P(None, "tp"),
            P("tp", None),
            P(),
            P(),
            P("ep", None, None, "tp"),
            P("ep", "tp", None),
            P(("ep", "tp"), None),
            P("ep", None),
            P("ep"),
            P("ep", None),
        ),
        out_specs=(
            P("ep", None),
            P("ep", None),
            P(),
            P(None, "tp"),
            P(None, "tp"),
            P("tp", None),
            P(),
            P(),
            P("ep", None, None, "tp"),
            P("ep", "tp", None),
            P(),
        ),
        check_vma=False,
    )
```

time: 2080 us -> 639 us (0.31)
  waiting for transfers between devices: 826 us -> 236 us
  blocking collectives: 417 us -> 0 us
  local copies, waits for them, and re-layouts: 325 us -> 28.2 us
  Pallas kernels: 0 us -> 234 us
  matrix products: 223 us -> 0 us
  other arithmetic: 178 us -> 35.2 us
  starting transfers between devices: 67.7 us -> 93.2 us
    all_to_all x3 -> x0, waiting for transfers between devices: 684 us -> none  [the longest x1 233 us: on_device(): lax.all_to_all(expert_rows, 'ep', split_axis=0, concat_axis=1, tiled=True)]
    all_to_all x1 -> x0, blocking collectives: 327 us -> none  [on_device(): lax.all_to_all(grad_outgoing.reshape(capacity, experts, MODEL_WIDTH), 'ep...]
    ppermute x0 -> x100, waiting for transfers between devices: none -> 236 us  [the longest x42 117 us: across(): return lax.ppermute(v, 'ep', [(i, i ^ k) for i in range(n_ep)])]
    pallas_call x0 -> x17, Pallas kernels: none -> 234 us  [the longest x4 86.6 us: experts(): pl.pallas_call(functools.partial(experts_body, nchunk, halves, min(rows,...]
    dot_general x29 -> x0, matrix products: 223 us -> none  [the longest x4 26.7 us: block_scores(): jnp.einsum('qngd,knd->ngqk', query_block, key_block, preferred_element_ty...]
    unnamed x112 -> x92, local copies, waits for them, and re-layouts: 112 us -> 4.11 us
    psum x3 -> x0, waiting for transfers between devices: 94.9 us -> none  [the longest x1 59.5 us: on_device(): lax.psum(grad_w_qkv.astype(jnp.bfloat16), 'ep').astype(jnp.float32)]
    ppermute x0 -> x100, starting transfers between devices: none -> 93.2 us  [the longest x42 65.5 us: across(): return lax.ppermute(v, 'ep', [(i, i ^ k) for i in range(n_ep)])]
  transfers between devices with their start and end apart: 12 -> 100, of which waited for: 8 -> 39; matrix products, arithmetic and copies ran while one was open for 13% -> 9% of each run, Pallas kernels for 0% -> 37%
where the time goes in v1:
time: 639 us; the launch traced here: 629 us
  waiting for transfers between devices  236 us (37%)
  Pallas kernels  234 us (37%)
  starting transfers between devices  93.2 us (15%)
  other arithmetic  35.2 us (6%)
  local copies, waits for them, and re-layouts  28.2 us (4%)
    ppermute x42, waiting for transfers between devices, across(): return lax.ppermute(v, 'ep', [(i, i ^ k) for i in range(n_ep)])  117 us
    ppermute x36, waiting for transfers between devices, along(): lax.ppermute(v, 'ep', [(i, (i + k * inner) % n_ep) for i in range(n_ep)])  117 us
    pallas_call x4, Pallas kernels, experts(): pl.pallas_call(functools.partial(experts_body, nchunk, halves, min(rows,...  86.6 us
    ppermute x42, starting transfers between devices, across(): return lax.ppermute(v, 'ep', [(i, i ^ k) for i in range(n_ep)])  65.5 us
    pallas_call x4, Pallas kernels, weight_grads(): pl.pallas_call(functools.partial(weight_grads_body, nb), grid=(count,), i...  50.7 us
    pallas_call x2, Pallas kernels, attn_backward(): pl.pallas_call(functools.partial(attn_backward_body, first), grid=(1,), i...  31.8 us
    ppermute x36, starting transfers between devices, along(): lax.ppermute(v, 'ep', [(i, (i + k * inner) % n_ep) for i in range(n_ep)])  25.3 us
    pallas_call x1, Pallas kernels, attn_forward(): pl.pallas_call(attn_forward_body, out_shape=[shape((rows, width), BF), sh...  24.9 us
  transfers between devices with their start and end apart: 100, of which 39 were waited for; matrix products, arithmetic and copies ran while one was open for 9% of the time, Pallas kernels for 37%

profile of v1, /device:TPU:0, one launch (start us, length us, event | category | flops | bytes accessed | tf_op | source)
XLA Modules:
  0.0 628.9 jit_solution(9783093429320200594)
XLA Ops:
  10.7 18.5 %collective-permute-done.2.refs_7_ = bf16[2,1024,256]{2,1,0:T(8,128)(2,1)} collective-permute-done((bf16[2,1024,256]{2,1,0:T(8,128)(2,1)}, bf16[2,1024,256]{2,1,0:T(8,128)(2,1)}, u32[]{:S(2)}, u32[]{:S(2)}) %collective-permute-start.2) | collective-permute-done | bytes 1048608 | tf_op jit(solution)/shard_map/ppermute | solution.py:571
  29.2 24.9 %attention_forward.1 = (bf16[1024,1024]{1,0:T(8,128)(2,1)}, bf16[1024,512]{1,0:T(8,128)(2,1)}, bf16[1024,512]{1,0:T(8,128)(2,1)}, bf16[1024,512]{1,0:T(8,128)(2,...) custom-call(bf16[1024,1024]{1,0:T(8,128)(2,1)} %x.9, ...), custom_call_target="tpu_custom_call" | custom-call | flops 11811160064 | bytes 12582912 | tf_op jit(solution)/shard_map/attention_forward/pallas_call | solution.py:99
  60.7 6.9 %collective-permute-done.21.refs_3_ = s32[512,8]{1,0:T(8,128)S(1)} collective-permute-done((s32[512,8]{1,0:T(8,128)S(1)}, s32[512,8]{1,0:T(8,128)S(1)}, u32[]{:S(2)}, u32[]{:S(2)}) %collective-permute-start.21) | collective-permute-done | bytes 16416 | tf_op jit(solution)/shard_map/ppermute | solution.py:568
  74.9 16.0 %collective-permute-done.11.refs_17_ = bf16[256,1024]{1,0:T(8,128)(2,1)S(1)} collective-permute-done((bf16[256,1024]{1,0:T(8,128)(2,1)}, bf16[256,1024]{1,0:T(8,128)(2,1)S(1)}, u32[]{:S(2)}, u32[]{:S(2)}) %collective-permute-start.11) | collective-permute-done | bytes 524320 | tf_op jit(solution)/shard_map/ppermute | solution.py:571
  100.8 23.4 %collective-permute-done.13.refs_19_ = bf16[256,1024]{1,0:T(8,128)(2,1)} collective-permute-done((bf16[256,1024]{1,0:T(8,128)(2,1)S(1)}, bf16[256,1024]{1,0:T(8,128)(2,1)}, u32[]{:S(2)}, u32[]{:S(2)}) %collective-permute-start.13) | collective-permute-done | bytes 524320 | tf_op jit(solution)/shard_map/ppermute | solution.py:571
  134.7 21.9 %experts.6 = (bf16[512,1024]{1,0:T(8,128)(2,1)}, bf16[512,1024]{1,0:T(8,128)(2,1)}, f32[8,512]{1,0:T(8,128)}, bf16[8,256,512]{2,1,0:T(8,128)(2,1)}, bf16[8,512,512]{2,1,0:T(8,128)(2,1)}) custom-call(s32[4]{0:T(128)} %copy-done.36, bf16[512,1024]{1,0:T(8,128)(2,1)} %collective-permute-done.19.refs_1_.refs_2_, bf16[512,1024]{1,0:T(8,128)(2,1)} %copy-done.2, ...), custom_call_target="tpu_custom_call" | custom-call | flops 12884901888 | bytes 18874368 | tf_op jit(solution)/shard_map/experts/pallas_call | solution.py:317
  162.7 47.7 %collective-permute-done.23.refs_1_.refs_3_ = bf16[512,1024]{1,0:T(8,128)(2,1)} collective-permute-done((bf16[512,1024]{1,0:T(8,128)(2,1)}, bf16[512,1024]{1,0:T(8,128)(2,1)}, u32[]{:S(2)}, u32[]{:S(2)}) %collective-permute-start.23) | collective-permute-done | bytes 1048608 | tf_op jit(solution)/shard_map/ppermute | solution.py:568
  210.4 21.5 %experts.7 = (bf16[512,1024]{1,0:T(8,128)(2,1)}, bf16[512,1024]{1,0:T(8,128)(2,1)}, f32[8,512]{1,0:T(8,128)}, bf16[8,256,512]{2,1,0:T(8,128)(2,1)}, bf16[8,512,512]{2,1,0:T(8,128)(2,1)}) custom-call(s32[4]{0:T(128)} %copy-done.36, bf16[512,1024]{1,0:T(8,128)(2,1)} %collective-permute-done.23.refs_1_.refs_3_, ...), custom_call_target="tpu_custom_call" | custom-call | flops 12884901888 | bytes 18874368 | tf_op jit(solution)/shard_map/experts/pallas_call | solution.py:317
  236.1 21.5 %experts.5 = (bf16[512,1024]{1,0:T(8,128)(2,1)}, bf16[512,1024]{1,0:T(8,128)(2,1)}, f32[8,512]{1,0:T(8,128)}, bf16[8,256,512]{2,1,0:T(8,128)(2,1)}, bf16[8,512,512]{2,1,0:T(8,128)(2,1)}) custom-call(s32[4]{0:T(128)} %copy-done.36, bf16[512,1024]{1,0:T(8,128)(2,1)} %copy-done.3, bf16[512,1024]{1,0:T(8,128)(2,1)} %collective-permute-done.16.refs_2_.refs_5_, ...), custom_call_target="tpu_custom_call" | custom-call | flops 12884901888 | bytes 18874368 | tf_op jit(solution)/shard_map/experts/pallas_call | solution.py:317
  258.2 21.7 %experts.4 = (bf16[512,1024]{1,0:T(8,128)(2,1)}, bf16[512,1024]{1,0:T(8,128)(2,1)}, f32[8,512]{1,0:T(8,128)}, bf16[8,256,512]{2,1,0:T(8,128)(2,1)}, bf16[8,512,512]{2,1,0:T(8,128)(2,1)}) custom-call(s32[4]{0:T(128)} %copy-done.36, bf16[512,1024]{1,0:T(8,128)(2,1)} %get-tuple-element.65.refs_1_.refs_0_, bf16[512,1024]{1,0:T(8,128)(2,1)} %copy-done.1, ...), custom_call_target="tpu_custom_call" | custom-call | flops 12884901888 | bytes 18874368 | tf_op jit(solution)/shard_map/experts/pallas_call | solution.py:317
  279.9 12.6 %expert_weight_grads.4 = (bf16[2,2,1024,256]{3,2,1,0:T(8,128)(2,1)}, bf16[2,256,1024]{2,1,0:T(8,128)(2,1)}) custom-call(bf16[512,1024]{1,0:T(8,128)(2,1)} %get-tuple-element.65.refs_1_.refs_0_, bf16[512,1024]{1,0:T(8,128)(2,1)} %copy-done.3, bf16[512,1024]{1,0:T(8,128)(2,1)} %collective-permute-done.19.refs_1_.refs_2_, ...), custom_call_target="tpu_custom_call" | custom-call | flops 6442450944 | bytes 11534336 | tf_op jit(solution)/shard_map/expert_weight_grads/pallas_call | solution.py:377
  294.4 12.6 %expert_weight_grads.5 = (bf16[2,2,1024,256]{3,2,1,0:T(8,128)(2,1)}, bf16[2,256,1024]{2,1,0:T(8,128)(2,1)}) custom-call(bf16[512,1024]{1,0:T(8,128)(2,1)} %get-tuple-element.65.refs_1_.refs_0_, bf16[512,1024]{1,0:T(8,128)(2,1)} %copy-done.3, bf16[512,1024]{1,0:T(8,128)(2,1)} %collective-permute-done.19.refs_1_.refs_2_, ...), custom_call_target="tpu_custom_call" | custom-call | flops 6442450944 | bytes 11534336 | tf_op jit(solution)/shard_map/expert_weight_grads/pallas_call | solution.py:377
  307.1 12.6 %expert_weight_grads.6 = (bf16[2,2,1024,256]{3,2,1,0:T(8,128)(2,1)}, bf16[2,256,1024]{2,1,0:T(8,128)(2,1)}) custom-call(bf16[512,1024]{1,0:T(8,128)(2,1)} %get-tuple-element.65.refs_1_.refs_0_, bf16[512,1024]{1,0:T(8,128)(2,1)} %copy-done.3, bf16[512,1024]{1,0:T(8,128)(2,1)} %collective-permute-done.19.refs_1_.refs_2_, ...), custom_call_target="tpu_custom_call" | custom-call | flops 6442450944 | bytes 11534336 | tf_op jit(solution)/shard_map/expert_weight_grads/pallas_call | solution.py:377
  319.7 12.7 %expert_weight_grads.7 = (bf16[2,2,1024,256]{3,2,1,0:T(8,128)(2,1)}, bf16[2,256,1024]{2,1,0:T(8,128)(2,1)}) custom-call(bf16[512,1024]{1,0:T(8,128)(2,1)} %get-tuple-element.65.refs_1_.refs_0_, bf16[512,1024]{1,0:T(8,128)(2,1)} %copy-done.3, bf16[512,1024]{1,0:T(8,128)(2,1)} %collective-permute-done.19.refs_1_.refs_2_, ...), custom_call_target="tpu_custom_call" | custom-call | flops 6442450944 | bytes 11534336 | tf_op jit(solution)/shard_map/expert_weight_grads/pallas_call | solution.py:377
  344.5 9.1 %middle_back.1 = (bf16[512,1024]{1,0:T(8,128)(2,1)}, f32[24,1024]{1,0:T(8,128)}) custom-call(s32[16]{0:T(128)} %pad_add_fusion.refs_0_, bf16[512,1024]{1,0:T(8,128)(2,1)} %get-tuple-element.65.refs_1_.refs_0_, f32[512,1024]{1,0:T(8,128)} %get-tuple-element.64.refs_0_.refs_2_, bf16[1,1024]{1,0:T(2,128)(2,1)} %broadcast_in_dim.41.gain.refs_3_, ...), custom_call_target="tpu_custom_call" | custom-call | flops 20971520 | bytes 10485760 | tf_op jit(solution)/shard_map/middle_back/pallas_call | solution.py:430
  373.1 13.3 %collective-permute-done.83 = f32[24,1024]{1,0:T(8,128)S(1)} collective-permute-done((f32[24,1024]{1,0:T(8,128)S(1)}, f32[24,1024]{1,0:T(8,128)S(1)}, u32[]{:S(2)}, u32[]{:S(2)}) %collective-permute-start.83) | collective-permute-done | bytes 98336 | tf_op jit(solution)/shard_map/ppermute | solution.py:571
  395.7 14.0 %collective-permute-done.22.refs_4_ = bf16[512,1024]{1,0:T(8,128)(2,1)} collective-permute-done((bf16[512,1024]{1,0:T(8,128)(2,1)}, bf16[512,1024]{1,0:T(8,128)(2,1)}, u32[]{:S(2)}, u32[]{:S(2)}) %collective-permute-start.22) | collective-permute-done | bytes 1048608 | tf_op jit(solution)/shard_map/ppermute | solution.py:568
  438.8 16.0 %attention_backward.3 = (bf16[1024,256]{1,0:T(8,128)(2,1)}, bf16[1024,256]{1,0:T(8,128)(2,1)}, bf16[1024,512]{1,0:T(8,128)(2,1)}) custom-call(bf16[1024,512]{1,0:T(8,128)(2,1)} %get-tuple-element.80.q, bf16[1024,512]{1,0:T(8,128)(2,1)} %get-tuple-element.81.kd, bf16[1024,512]{1,0:T(8,128)(2,1)} %get-tuple-element.82.vd, ...), custom_call_target="tpu_custom_call" | custom-call | flops 11811160064 | bytes 10485760 | tf_op jit(solution)/shard_map/attention_backward/pallas_call | solution.py:172
  454.8 15.8 %attention_backward.2 = (bf16[1024,256]{1,0:T(8,128)(2,1)}, bf16[1024,256]{1,0:T(8,128)(2,1)}, bf16[1024,512]{1,0:T(8,128)(2,1)}) custom-call(bf16[1024,512]{1,0:T(8,128)(2,1)} %get-tuple-element.80.q, bf16[1024,512]{1,0:T(8,128)(2,1)} %get-tuple-element.81.kd, bf16[1024,512]{1,0:T(8,128)(2,1)} %get-tuple-element.82.vd, ...), custom_call_target="tpu_custom_call" | custom-call | flops 11811160064 | bytes 10485760 | tf_op jit(solution)/shard_map/attention_backward/pallas_call | solution.py:172
  470.6 7.1 %input_back.1 = (bf16[1024,1024]{1,0:T(8,128)(2,1)}, f32[8,1024]{1,0:T(8,128)}) custom-call(bf16[1024,1024]{1,0:T(8,128)(2,1)} %x.9, bf16[1024,512]{1,0:T(8,128)(2,1)} %wq.3, bf16[1024,512]{1,0:T(8,128)(2,1)} %wkv.3, bf16[1024,256]{1,0:T(8,128)(2,1)} %get-tuple-element.87.refs_0_, bf16[1024,256]{1,0:T(8,128)(2,1)} %get-tuple-element.88.refs_1_, ...), custom_call_target="tpu_custom_call" | custom-call | flops 2147483648 | bytes 10485760 | tf_op jit(solution)/shard_map/input_back/pallas_call | solution.py:481
  518.3 10.4 %collective-permute-done.56 = bf16[256,512]{1,0:T(8,128)(2,1)S(1)} collective-permute-done((bf16[256,512]{1,0:T(8,128)(2,1)S(1)}, bf16[256,512]{1,0:T(8,128)(2,1)S(1)}, u32[]{:S(2)}, u32[]{:S(2)}) %collective-permute-start.56) | collective-permute-done | bytes 262176 | tf_op jit(solution)/shard_map/ppermute | solution.py:568
  584.1 8.3 %collective-permute-start.64 = (bf16[256,512]{1,0:T(8,128)(2,1)S(1)}, bf16[256,512]{1,0:T(8,128)(2,1)S(1)}, u32[]{:S(2)}, u32[]{:S(2)}) collective-permute-start(bf16[256,512]{1,0:T(8,128)(2,1)S(1)} %constant_dynamic-update-slice_fusion.12), channel_id=1, source_target_pairs={{0,2},{2,0},{4,6},{6,4},{8,10},{10,8},{12,14},{14,12},{16,18},{18,... | collective-permute-start | bytes 786440 | tf_op jit(solution)/shard_map/ppermute | solution.py:568
  602.2 6.9 %collective-permute-done.65 = bf16[256,512]{1,0:T(8,128)(2,1)S(1)} collective-permute-done((bf16[256,512]{1,0:T(8,128)(2,1)S(1)}, bf16[256,512]{1,0:T(8,128)(2,1)S(1)}, u32[]{:S(2)}, u32[]{:S(2)}) %collective-permute-start.65) | collective-permute-done | bytes 262176 | tf_op jit(solution)/shard_map/ppermute | solution.py:568
  612.6 8.9 %token_grads.1 = f32[1024,1024]{1,0:T(8,128)} custom-call(bf16[1024,1024]{1,0:T(8,128)(2,1)} %x.9, bf16[1024,1024]{1,0:T(8,128)(2,1)} %cot.3, bf16[1024,1024]{1,0:T(8,128)(2,1)} %maximum_select_fusion.1.gm, bf16[1024,1024]{1,0:T(8,128)(2,1)} %get-tuple-element.91.own, bf16[1024,1024]{1,0:T(8,128)(2,1)} %collective-permute-done.35.other, ...), custom_call_target="tpu_custom_call" | custom-call | flops 12582912 | bytes 14680064 | tf_op jit(solution)/shard_map/token_grads/pallas_call | solution.py:505
  (381 shorter events, 241.8 us)
Async XLA Ops:
  29.2 44.9 %collective-permute-start.4 = (bf16[2,1024,256]{2,1,0:T(8,128)(2,1)}, bf16[2,1024,256]{2,1,0:T(8,128)(2,1)}, u32[]{:S(2)}, u32[]{:S(2)}) collective-permute-start(bf16[2,1024,256]{2,1,0:T(8,128)(2,1)} %collective-permute-done.2.refs_7_), channel_id=1, source_target_pairs={{0,8},{2,10},{4,12},{6,14},{8,16},{10,18},{12,20},{14,22},{16,24},... | collective-permute-start | bytes 3145736 | tf_op jit(solution)/shard_map/ppermute | solution.py:571
  74.1 50.1 %collective-permute-start.6 = (bf16[2,1024,256]{2,1,0:T(8,128)(2,1)}, bf16[2,1024,256]{2,1,0:T(8,128)(2,1)}, u32[]{:S(2)}, u32[]{:S(2)}) collective-permute-start(bf16[2,1024,256]{2,1,0:T(8,128)(2,1)} %collective-permute-done.4.refs_9_), channel_id=1, source_target_pairs={{0,8},{2,10},{4,12},{6,14},{8,16},{10,18},{12,20},{14,22},{16,24},... | collective-permute-start | bytes 3145736 | tf_op jit(solution)/shard_map/ppermute | solution.py:571
  90.9 33.4 %collective-permute-start.13 = (bf16[256,1024]{1,0:T(8,128)(2,1)S(1)}, bf16[256,1024]{1,0:T(8,128)(2,1)}, u32[]{:S(2)}, u32[]{:S(2)}) collective-permute-start(bf16[256,1024]{1,0:T(8,128)(2,1)S(1)} %collective-permute-done.11.refs_17_), channel_id=1, source_target_pairs={{0,8},{2,10},{4,12},{6,14},{8,16},{10,18},{12,20},{14,22},{16,24},... | collective-permute-start | bytes 1572872 | tf_op jit(solution)/shard_map/ppermute | solution.py:571
  100.3 31.6 %collective-permute-start.3 = (bf16[2,1024,256]{2,1,0:T(8,128)(2,1)}, bf16[2,1024,256]{2,1,0:T(8,128)(2,1)}, u32[]{:S(2)}, u32[]{:S(2)}) collective-permute-start(bf16[2,1024,256]{2,1,0:T(8,128)(2,1)} %collective-permute-done.2.refs_7_), channel_id=1, source_target_pairs={{0,1},{1,0},{2,3},{3,2},{4,5},{5,4},{6,7},{7,6},{8,9},{9,8},{10,11... | collective-permute-start | bytes 3145736 | tf_op jit(solution)/shard_map/ppermute | solution.py:574
  127.3 34.0 %collective-permute-start.24 = (bf16[512,1024]{1,0:T(8,128)(2,1)S(1)}, bf16[512,1024]{1,0:T(8,128)(2,1)}, u32[]{:S(2)}, u32[]{:S(2)}) collective-permute-start(bf16[512,1024]{1,0:T(8,128)(2,1)S(1)} %constant_dynamic-slice_fusion.18.refs_2_.refs_4_), channel_id=1, source_target_pairs={{0,6},{2,4},{4,2},{6,0},{8,14},{10,12},{12,10},{14,8},{16,22},{18,... | collective-permute-start | bytes 3145736 | tf_op jit(solution)/shard_map/ppermute | solution.py:568
  132.0 103.0 %collective-permute-start.16 = (bf16[512,1024]{1,0:T(8,128)(2,1)S(1)}, bf16[512,1024]{1,0:T(8,128)(2,1)}, u32[]{:S(2)}, u32[]{:S(2)}) collective-permute-start(bf16[512,1024]{1,0:T(8,128)(2,1)S(1)} %constant_dynamic-slice_fusion.18.refs_2_.refs_4_), channel_id=1, source_target_pairs={{0,2},{2,0},{4,6},{6,4},{8,10},{10,8},{12,14},{14,12},{16,18},{18,... | collective-permute-start | bytes 3145736 | tf_op jit(solution)/shard_map/ppermute | solution.py:568
  132.5 101.9 %collective-permute-start.17 = (s32[512,8]{1,0:T(8,128)S(1)}, s32[512,8]{1,0:T(8,128)S(1)}, u32[]{:S(2)}, u32[]{:S(2)}) collective-permute-start(s32[512,8]{1,0:T(8,128)S(1)} %copy.44.refs_3_.refs_4_), channel_id=1, source_target_pairs={{0,2},{2,0},{4,6},{6,4},{8,10},{10,8},{12,14},{14,12},{16,18},{18,... | collective-permute-start | bytes 49160 | tf_op jit(solution)/shard_map/ppermute | solution.py:568
  134.0 76.4 %collective-permute-start.23 = (bf16[512,1024]{1,0:T(8,128)(2,1)}, bf16[512,1024]{1,0:T(8,128)(2,1)}, u32[]{:S(2)}, u32[]{:S(2)}) collective-permute-start(bf16[512,1024]{1,0:T(8,128)(2,1)} %get-tuple-element.65.refs_1_.refs_0_), channel_id=1, source_target_pairs={{0,6},{2,4},{4,2},{6,0},{8,14},{10,12},{12,10},{14,8},{16,22},{18,... | collective-permute-start | bytes 3145736 | tf_op jit(solution)/shard_map/ppermute | solution.py:568
  159.7 75.2 %collective-permute-start.15 = (bf16[512,1024]{1,0:T(8,128)(2,1)S(1)}, bf16[512,1024]{1,0:T(8,128)(2,1)S(1)}, u32[]{:S(2)}, u32[]{:S(2)}) collective-permute-start(bf16[512,1024]{1,0:T(8,128)(2,1)S(1)} %copy-done), channel_id=1, source_target_pairs={{0,2},{2,0},{4,6},{6,4},{8,10},{10,8},{12,14},{14,12},{16,18},{18,... | collective-permute-start | bytes 3145736 | tf_op jit(solution)/shard_map/ppermute | solution.py:568
  161.2 182.2 %collective-permute-start.29 = (bf16[512,1024]{1,0:T(8,128)(2,1)}, bf16[512,1024]{1,0:T(8,128)(2,1)}, u32[]{:S(2)}, u32[]{:S(2)}) collective-permute-start(bf16[512,1024]{1,0:T(8,128)(2,1)} %get-tuple-element.73), channel_id=1, source_target_pairs={{0,4},{2,6},{4,0},{6,2},{8,12},{10,14},{12,8},{14,10},{16,20},{18,... | collective-permute-start | bytes 3145736 | tf_op jit(solution)/shard_map/ppermute | solution.py:568
  231.9 111.6 %collective-permute-start.30 = (bf16[512,1024]{1,0:T(8,128)(2,1)}, bf16[512,1024]{1,0:T(8,128)(2,1)}, u32[]{:S(2)}, u32[]{:S(2)}) collective-permute-start(bf16[512,1024]{1,0:T(8,128)(2,1)} %get-tuple-element.74), channel_id=1, source_target_pairs={{0,6},{2,4},{4,2},{6,0},{8,14},{10,12},{12,10},{14,8},{16,22},{18,... | collective-permute-start | bytes 3145736 | tf_op jit(solution)/shard_map/ppermute | solution.py:568
  234.4 102.1 %collective-permute-start.32 = (f32[8,512]{1,0:T(8,128)S(1)}, f32[8,512]{1,0:T(8,128)S(1)}, u32[]{:S(2)}, u32[]{:S(2)}) collective-permute-start(f32[8,512]{1,0:T(8,128)S(1)} %copy-done.42), channel_id=1, source_target_pairs={{0,4},{2,6},{4,0},{6,2},{8,12},{10,14},{12,8},{14,10},{16,20},{18,... | collective-permute-start | bytes 49160 | tf_op jit(solution)/shard_map/ppermute | solution.py:568
  257.6 85.9 %collective-permute-start.28 = (bf16[512,1024]{1,0:T(8,128)(2,1)}, bf16[512,1024]{1,0:T(8,128)(2,1)S(1)}, u32[]{:S(2)}, u32[]{:S(2)}) collective-permute-start(bf16[512,1024]{1,0:T(8,128)(2,1)} %get-tuple-element.72), channel_id=1, source_target_pairs={{0,2},{2,0},{4,6},{6,4},{8,10},{10,8},{12,14},{14,12},{16,18},{18,... | collective-permute-start | bytes 3145736 | tf_op jit(solution)/shard_map/ppermute | solution.py:568
  294.4 44.4 %collective-permute-start.93 = (bf16[256,1024]{1,0:T(8,128)(2,1)}, bf16[256,1024]{1,0:T(8,128)(2,1)S(1)}, u32[]{:S(2)}, u32[]{:S(2)}) collective-permute-start(bf16[256,1024]{1,0:T(8,128)(2,1)} %slice_bitcast_fusion.7), channel_id=1, source_target_pairs={{0,1},{1,0},{2,3},{3,2},{4,5},{5,4},{6,7},{7,6},{8,9},{9,8},{10,11... | collective-permute-start | bytes 1572872 | tf_op jit(solution)/shard_map/ppermute | solution.py:574
  360.7 49.0 %collective-permute-start.22 = (bf16[512,1024]{1,0:T(8,128)(2,1)}, bf16[512,1024]{1,0:T(8,128)(2,1)}, u32[]{:S(2)}, u32[]{:S(2)}) collective-permute-start(bf16[512,1024]{1,0:T(8,128)(2,1)} %get-tuple-element.68), channel_id=1, source_target_pairs={{0,4},{2,6},{4,0},{6,2},{8,12},{10,14},{12,8},{14,10},{16,20},{18,... | collective-permute-start | bytes 3145736 | tf_op jit(solution)/shard_map/ppermute | solution.py:568
  364.8 44.8 %collective-permute-start.26 = (bf16[512,1024]{1,0:T(8,128)(2,1)}, bf16[512,1024]{1,0:T(8,128)(2,1)}, u32[]{:S(2)}, u32[]{:S(2)}) collective-permute-start(bf16[512,1024]{1,0:T(8,128)(2,1)} %get-tuple-element.69), channel_id=1, source_target_pairs={{0,6},{2,4},{4,2},{6,0},{8,14},{10,12},{12,10},{14,8},{16,22},{18,... | collective-permute-start | bytes 3145736 | tf_op jit(solution)/shard_map/ppermute | solution.py:568
  365.4 44.7 %collective-permute-start.86 = (bf16[2,1024,256]{2,1,0:T(8,128)(2,1)S(1)}, bf16[2,1024,256]{2,1,0:T(8,128)(2,1)S(1)}, u32[]{:S(2)}, u32[]{:S(2)}) collective-permute-start(bf16[2,1024,256]{2,1,0:T(8,128)(2,1)S(1)} %copy-done.22), channel_id=1, source_target_pairs={{0,1},{1,0},{2,3},{3,2},{4,5},{5,4},{6,7},{7,6},{8,9},{9,8},{10,11... | collective-permute-start | bytes 3145736 | tf_op jit(solution)/shard_map/ppermute | solution.py:574
  393.5 35.1 %collective-permute-start.34 = (bf16[512,1024]{1,0:T(8,128)(2,1)S(1)}, bf16[512,1024]{1,0:T(8,128)(2,1)}, u32[]{:S(2)}, u32[]{:S(2)}) collective-permute-start(bf16[512,1024]{1,0:T(8,128)(2,1)S(1)} %copy-done.12), channel_id=1, source_target_pairs={{0,1},{1,0},{2,3},{3,2},{4,5},{5,4},{6,7},{7,6},{8,9},{9,8},{10,11... | collective-permute-start | bytes 3145736 | tf_op jit(solution)/shard_map/ppermute | solution.py:574
  415.6 64.3 %collective-permute-start.88 = (bf16[2,1024,256]{2,1,0:T(8,128)(2,1)}, bf16[2,1024,256]{2,1,0:T(8,128)(2,1)}, u32[]{:S(2)}, u32[]{:S(2)}) collective-permute-start(bf16[2,1024,256]{2,1,0:T(8,128)(2,1)} %slice_bitcast_fusion.2), channel_id=1, source_target_pairs={{0,1},{1,0},{2,3},{3,2},{4,5},{5,4},{6,7},{7,6},{8,9},{9,8},{10,11... | collective-permute-start | bytes 3145736 | tf_op jit(solution)/shard_map/ppermute | solution.py:574
  421.1 61.1 %collective-permute-start.87 = (bf16[2,1024,256]{2,1,0:T(8,128)(2,1)}, bf16[2,1024,256]{2,1,0:T(8,128)(2,1)}, u32[]{:S(2)}, u32[]{:S(2)}) collective-permute-start(bf16[2,1024,256]{2,1,0:T(8,128)(2,1)} %fusion.6), channel_id=1, source_target_pairs={{0,8},{2,10},{4,12},{6,14},{8,16},{10,18},{12,20},{14,22},{16,24},... | collective-permute-start | bytes 3145736 | tf_op jit(solution)/shard_map/ppermute | solution.py:571
  423.4 61.7 %collective-permute-start.27 = (bf16[512,1024]{1,0:T(8,128)(2,1)}, bf16[512,1024]{1,0:T(8,128)(2,1)}, u32[]{:S(2)}, u32[]{:S(2)}) collective-permute-start(bf16[512,1024]{1,0:T(8,128)(2,1)} %get-tuple-element.70), channel_id=1, source_target_pairs={{0,1},{1,0},{2,3},{3,2},{4,5},{5,4},{6,7},{7,6},{8,9},{9,8},{10,11... | collective-permute-start | bytes 3145736 | tf_op jit(solution)/shard_map/ppermute | solution.py:574
  504.6 94.5 %collective-permute-start.90 = (bf16[2,1024,256]{2,1,0:T(8,128)(2,1)S(1)}, bf16[2,1024,256]{2,1,0:T(8,128)(2,1)S(1)}, u32[]{:S(2)}, u32[]{:S(2)}) collective-permute-start(bf16[2,1024,256]{2,1,0:T(8,128)(2,1)S(1)} %copy-done.21), channel_id=1, source_target_pairs={{0,1},{1,0},{2,3},{3,2},{4,5},{5,4},{6,7},{7,6},{8,9},{9,8},{10,11... | collective-permute-start | bytes 3145736 | tf_op jit(solution)/shard_map/ppermute | solution.py:574
  504.6 96.2 %collective-permute-start.89 = (bf16[2,1024,256]{2,1,0:T(8,128)(2,1)S(1)}, bf16[2,1024,256]{2,1,0:T(8,128)(2,1)S(1)}, u32[]{:S(2)}, u32[]{:S(2)}) collective-permute-start(bf16[2,1024,256]{2,1,0:T(8,128)(2,1)S(1)} %fusion.5), channel_id=1, source_target_pairs={{0,8},{2,10},{4,12},{6,14},{8,16},{10,18},{12,20},{14,22},{16,24},... | collective-permute-start | bytes 3145736 | tf_op jit(solution)/shard_map/ppermute | solution.py:571
  578.5 34.1 %collective-permute-start.35 = (bf16[1024,1024]{1,0:T(8,128)(2,1)S(1)}, bf16[1024,1024]{1,0:T(8,128)(2,1)}, u32[]{:S(2)}, u32[]{:S(2)}) collective-permute-start(bf16[1024,1024]{1,0:T(8,128)(2,1)S(1)} %copy-done.11), channel_id=1, source_target_pairs={{0,1},{1,0},{2,3},{3,2},{4,5},{5,4},{6,7},{7,6},{8,9},{9,8},{10,11... | collective-permute-start | bytes 6291464 | tf_op jit(solution)/shard_map/ppermute | solution.py:574
  (121 other events, 1740.4 us)

commit v2 on v1

v2 whole, which is shorter than its diff:
```python
import functools
import math

import jax
import jax.numpy as jnp
from jax import lax
from jax.experimental import pallas as pl
from jax.experimental.pallas import tpu as pltpu
from jax.sharding import PartitionSpec as P

SEQUENCE_LENGTH = 1024
WINDOW = 1024
ATTN_SCALE = 0.015625
RESID_SCALE = 0.22
TOPK = 8
NORM_EPS = 1e-06
ROPE_BASE = 10000.0
F32 = jnp.float32
BF = jnp.bfloat16
VMEM_BYTES = 60 * 1024 * 1024
COST = 0.02
GAIN_F, GAIN_A, STATS = 64, 65, 66


def cost(flops, bytes_accessed, transcendentals=0):
    return pl.CostEstimate(
        flops=int(COST * flops), bytes_accessed=int(COST * bytes_accessed), transcendentals=int(COST * transcendentals)
    )


def dot(a, b):
    return jnp.dot(a, b, preferred_element_type=F32)


def dot_nt(a, b):
    return lax.dot_general(a, b, (((1,), (1,)), ((), ())), preferred_element_type=F32)


def dot_tn(a, b):
    return lax.dot_general(a, b, (((0,), (0,)), ((), ())), preferred_element_type=F32)


def whole_block(v):
    return pl.BlockSpec(v.shape, lambda *_: (0,) * len(v.shape))


def gate_table(h2, pay, wr):
    rows = h2.shape[0]
    lane = lax.broadcasted_iota(jnp.int32, (rows, 128), 1).astype(F32)
    routes = pay[rows : rows + 16, :rows].astype(F32).T
    mask = routes[:, 0:1] == lane
    for k in range(1, TOPK):
        mask = mask | (routes[:, k : k + 1] == lane)
    sel = jnp.where(mask, dot(h2[...], wr[...]), -jnp.inf)
    weight = jnp.exp(sel - jnp.max(sel, axis=1, keepdims=True))
    return weight / jnp.sum(weight, axis=1, keepdims=True)


def middle_body(core, x, own, other, gain, live, mid, h2, stats):
    attn = RESID_SCALE * (own[...].astype(F32) + other[...].astype(F32))
    m = x[...].astype(F32) + attn
    mid[...] = m
    r = lax.rsqrt(jnp.mean(m * m, axis=1, keepdims=True) + NORM_EPS)
    h2[...] = (m * r * gain[...].astype(F32)).astype(BF)
    v = live[...]
    total = jnp.sum(v * jnp.sum(attn * attn, axis=1, keepdims=True))
    lane = lax.broadcasted_iota(jnp.int32, stats.shape, 1)
    stats[...] = jnp.where(lane == 1, total, jnp.where(lane == 3, jnp.sum(v), 0.0))


def middle_norm(core, x, own, other, gain, live):
    share, width = own.shape
    shape = jax.ShapeDtypeStruct
    part = lambda n: pl.BlockSpec((share, n), lambda _, c: (c[0], 0))
    full = lambda *s: pl.BlockSpec(s, lambda *_: (0, 0))
    return pl.pallas_call(
        middle_body,
        grid_spec=pltpu.PrefetchScalarGridSpec(
            num_scalar_prefetch=1,
            grid=(1,),
            in_specs=[part(width), whole_block(own), whole_block(other), whole_block(gain), part(1)],
            out_specs=[full(share, width), full(share, width), full(8, 128)],
        ),
        out_shape=[shape((share, width), F32), shape((share, width), BF), shape((8, 128), F32)],
        compiler_params=pltpu.CompilerParams(vmem_limit_bytes=VMEM_BYTES),
        cost_estimate=cost(10 * share * width, 12 * share * width),
        name="middle_norm",
    )(core, x, own, other, gain, live)


def experts_body(nb, nchunk, halves, first, carried, *refs):
    ids = refs[0]
    at = 1
    h2s, pays = refs[at : at + nb], refs[at + nb : at + 2 * nb]
    at += 2 * nb
    prevs = [None] * nb
    if carried:
        prevs = [refs[at + 2 * b : at + 2 * b + 2] for b in range(nb)]
        at += 2 * nb
    wr = refs[at]
    packs = refs[at + 1 : at + 1 + nchunk]
    at += 1 + nchunk
    outs = [refs[at + 4 * b : at + 4 * b + 4] for b in range(nb)]
    at += 4 * nb
    gates, dgacc, macc, xacc, buf, sem = refs[at:]
    c = pl.program_id(0)
    rows, width = h2s[0].shape
    f = buf.shape[3]
    lane = lax.broadcasted_iota(jnp.int32, (rows, 128), 1)

    @pl.when(c == 0)
    def _():
        pltpu.make_async_copy(packs[0], buf.at[0], sem.at[0]).start()
        for b in range(nb):
            gates[b] = gate_table(h2s[b], pays[b], wr)
            if carried:
                macc[b] = prevs[b][1][...].astype(F32)
                xacc[b] = prevs[b][0][:rows, :].astype(F32)
            else:
                macc[b] = jnp.zeros((rows, width), F32)
                xacc[b] = jnp.zeros((rows, width), F32)
        dgacc[...] = jnp.zeros_like(dgacc)

    for k in range(1, nchunk):

        @pl.when(c + 1 == k)
        def _(k=k):
            pltpu.make_async_copy(packs[k], buf.at[k % 2], sem.at[k % 2]).start()

    slot = lax.rem(c, 2)
    pltpu.make_async_copy(packs[0], buf.at[slot], sem.at[slot]).wait()
    r = first + c // halves
    e = ids[r]
    nd = width // f
    for b in range(nb):
        g, gat, dgu = pays[b], outs[b][2], outs[b][3]
        hb = h2s[b][...]
        gp = dot(hb, buf[slot, 0])
        up = dot(hb, buf[slot, 1])
        u = sum(dot_nt(g[:rows, k * f : (k + 1) * f], buf[slot, 2, k * f : (k + 1) * f, :]) for k in range(nd))
        gate = jnp.sum(jnp.where(lane == e, gates[b], 0.0), axis=1, keepdims=True)
        sg = jax.nn.sigmoid(gp)
        sl = gp * sg
        act = sl * up
        ga = (gate * act).astype(BF)
        dgacc[b] += jnp.where(lane == r, jnp.sum(act * u, axis=1, keepdims=True) * RESID_SCALE, 0.0)
        da = (RESID_SCALE * gate) * u
        dgp = (da * up * (sg + sl * (1.0 - sg))).astype(BF)
        dup = (da * sl).astype(BF)
        gat[0] = ga.T
        dgu[0, :, :f] = dgp
        dgu[0, :, f:] = dup
        for k in range(nd):
            macc[b, :, k * f : (k + 1) * f] += dot(ga, buf[slot, 2, k * f : (k + 1) * f, :])
        xacc[b] += dot_nt(dgp, buf[slot, 0]) + dot_nt(dup, buf[slot, 1])

    @pl.when(c == nchunk - 1)
    def _():
        for b in range(nb):
            dx, moe = outs[b][:2]
            moe[...] = macc[b].astype(BF)
            dx[:rows, :] = xacc[b].astype(BF)
            dg = dgacc[b].T[:8]
            high = dg.astype(BF).astype(F32)
            tail = jnp.concatenate([high, dg - high], axis=0)
            if carried:
                row = lax.broadcasted_iota(jnp.int32, (16, rows), 0) % 8
                mine = (row >= first) & (row < first + nchunk // halves)
                tail = jnp.where(mine, tail, prevs[b][0][rows:, :rows].astype(F32))
            dx[rows:, :] = jnp.zeros((16, width), BF)
            dx[rows:, :rows] = tail.astype(BF)


def experts(ids, h2s, pays, prevs, wr, packs, halves, first):
    rows, width = h2s[0].shape
    nb, nchunk = len(h2s), len(packs)
    f = packs[0].shape[2]
    carried = prevs is not None
    flat = [v for prev in prevs for v in prev] if carried else []
    shape = jax.ShapeDtypeStruct
    once = lambda v: pl.BlockSpec(v.shape, lambda *_: (0,) * len(v.shape), pipeline_mode=pl.Buffered(1))
    out = pl.pallas_call(
        functools.partial(experts_body, nb, nchunk, halves, first, carried),
        grid_spec=pltpu.PrefetchScalarGridSpec(
            num_scalar_prefetch=1,
            grid=(nchunk,),
            in_specs=[once(v) for v in (*h2s, *pays, *flat, wr)] + [pl.BlockSpec(memory_space=pl.ANY)] * nchunk,
            out_specs=[
                pl.BlockSpec((rows + 16, width), lambda c, _: (0, 0)),
                pl.BlockSpec((rows, width), lambda c, _: (0, 0)),
                pl.BlockSpec((1, f, rows), lambda c, _: (c, 0, 0)),
                pl.BlockSpec((1, rows, 2 * f), lambda c, _: (c, 0, 0)),
            ]
            * nb,
            scratch_shapes=[
                pltpu.VMEM((nb, rows, 128), F32),
                pltpu.VMEM((nb, rows, 128), F32),
                pltpu.VMEM((nb, rows, width), F32),
                pltpu.VMEM((nb, rows, width), F32),
                pltpu.VMEM((2, 3, width, f), BF),
                pltpu.SemaphoreType.DMA((2,)),
            ],
        ),
        out_shape=[
            shape((rows + 16, width), BF),
            shape((rows, width), BF),
            shape((nchunk, f, rows), BF),
            shape((nchunk, rows, 2 * f), BF),
        ]
        * nb,
        compiler_params=pltpu.CompilerParams(vmem_limit_bytes=VMEM_BYTES),
        cost_estimate=cost(12 * rows * width * f * nchunk * nb, 6 * nchunk * width * f + 12 * rows * width * nb),
        name="experts",
    )(ids, *h2s, *pays, *flat, wr, *packs)
    return [out[4 * b : 4 * b + 4] for b in range(nb)]


def weight_grads_body(nb, halves, _, *refs):
    h2 = refs[:nb]
    g = refs[nb : 2 * nb]
    hidden, outs = refs[2 * nb : -halves], refs[-halves:]
    e, c = pl.program_id(0), pl.program_id(1)
    rows = h2[0].shape[0]
    width, f = outs[0].shape[2:]
    for n in range(len(hidden) // (2 * nb)):

        @pl.when(e == n)
        def _(n=n):
            gat, dgu = hidden[2 * nb * n : 2 * nb * n + nb], hidden[2 * nb * n + nb : 2 * nb * (n + 1)]
            acc = sum(dot_tn(h2[b][...], dgu[b][0]) for b in range(nb))
            down = sum(dot(gat[b][0], g[b][:rows, :]) for b in range(nb)) * RESID_SCALE
            for half in range(halves):

                @pl.when(c == half)
                def _(out=outs[half]):
                    out[0, 0] = acc[:, :f].astype(BF)
                    out[0, 1] = acc[:, f:].astype(BF)
                    for k in range(width // f):
                        out[0, 2, k * f : (k + 1) * f, :] = down[:, k * f : (k + 1) * f].astype(BF)


def weight_grads(tok, h2s, pays, saved, halves):
    nb, ne = len(h2s), len(saved[0])
    rows, width = h2s[0].shape
    f = saved[0][0][0].shape[1]
    shape = jax.ShapeDtypeStruct
    once = lambda v: pl.BlockSpec(v.shape, lambda *_: (0,) * len(v.shape), pipeline_mode=pl.Buffered(1))
    specs, args = [], []
    for n in range(ne):
        half = lambda e, c, n=n: jnp.where(e < n, 0, jnp.where(e == n, c, halves - 1))
        for j, block in ((0, (1, f, rows)), (1, (1, rows, 2 * f))):
            for b in range(nb):
                args.append(saved[b][n][j])
                specs.append(pl.BlockSpec(block, lambda e, c, o=saved[b][n][2], half=half: (o + half(e, c), 0, 0)))
    return pl.pallas_call(
        functools.partial(weight_grads_body, nb, halves),
        grid=(ne, halves),
        in_specs=[pl.BlockSpec(memory_space=pltpu.SMEM)] + [once(v) for v in (*h2s, *pays)] + specs,
        out_specs=[pl.BlockSpec((1, 3, width, f), lambda e, c: (e, 0, 0, 0))] * halves,
        out_shape=[shape((ne, 3, width, f), BF)] * halves,
        compiler_params=pltpu.CompilerParams(vmem_limit_bytes=VMEM_BYTES),
        cost_estimate=cost(6 * rows * nb * width * f * halves, 6 * halves * width * f + 4 * rows * nb * width),
        name="expert_weight_grads",
    )(tok, *h2s, *pays, *args)


def middle_back_body(nb, nlocal, _, *refs):
    ids, h2, mid, gain, pay, wr = refs[:6]
    dxs = refs[6 : 6 + nb]
    gm, small = refs[6 + nb :]
    rows, width = h2.shape
    lane = lax.broadcasted_iota(jnp.int32, (rows, 128), 1)
    gates = gate_table(h2, pay, wr)
    dgate = jnp.zeros((rows, 128), F32)
    for b in range(nb):
        tail = dxs[b][rows:, :rows].astype(F32)
        cols = (tail[:8] + tail[8:]).T
        for r in range(nlocal):
            dgate = jnp.where(lane == ids[b * nlocal + r], cols[:, r : r + 1], dgate)
    dsel = gates * (dgate - jnp.sum(gates * dgate, axis=1, keepdims=True))
    high = dsel.astype(BF)
    rest = (dsel - high.astype(F32)).astype(BF)
    router = dot_tn(h2[...], high) + dot_tn(h2[...], rest)
    dh = dot_nt(high, wr[...]) + dot_nt(rest, wr[...])
    for b in range(nb):
        dh = dh + dxs[b][:rows, :].astype(F32)
    m = mid[...]
    r2 = lax.rsqrt(jnp.mean(m * m, axis=1, keepdims=True) + NORM_EPS)
    xhat = m * r2
    col = jnp.broadcast_to(jnp.sum(dh * xhat, axis=0, keepdims=True), (8, width)).T[:, :1]
    small[...] = jnp.where(lax.broadcasted_iota(jnp.int32, (width, 128), 1) == GAIN_F, col, router)
    su = dh * gain[...].astype(F32)
    gm[...] = (r2 * (su - xhat * jnp.mean(su * xhat, axis=1, keepdims=True))).astype(BF)


def middle_back(tok, ids, h2, mid, gain, pay, wr, dxs, nlocal):
    rows, width = h2.shape
    shape = jax.ShapeDtypeStruct
    args = (h2, mid, gain, pay, wr, *dxs)
    return pl.pallas_call(
        functools.partial(middle_back_body, len(dxs), nlocal),
        in_specs=[pl.BlockSpec(memory_space=pltpu.SMEM)] * 2 + [pl.BlockSpec(memory_space=pltpu.VMEM)] * len(args),
        out_shape=[shape((rows, width), BF), shape((width, 128), F32)],
        compiler_params=pltpu.CompilerParams(vmem_limit_bytes=VMEM_BYTES),
        cost_estimate=cost(40 * rows * width, 20 * rows * width),
        name="middle_back",
    )(tok, ids, *args)


def placed(core, parts, i, rt):
    if len(parts) == 1:
        return parts[0][i * rt : (i + 1) * rt, :].astype(F32)
    share = parts[0].shape[0]
    at = i * rt % share
    mine, other = (p[at : at + rt, :].astype(F32) for p in parts)
    return jnp.where(core[0] == i * rt // share, mine, other)


def out_back_body(core, cot, wo, o, *refs):
    parts, (do, gwo, da) = refs[:-3], refs[-3:]
    rows = cot.shape[0]
    rt = 256
    for i in range(rows // rt):
        rs = pl.ds(i * rt, rt)
        d = (RESID_SCALE * (cot[rs, :].astype(F32) + placed(core, parts, i, rt))).astype(BF)
        da[rs, :] = d
        do[rs, :] = dot_nt(d, wo[...]).astype(BF)
    gwo[...] = dot_tn(o[...], da[...]).astype(BF)


def out_back(core, cot, wo, o, parts):
    rows, width = cot.shape
    w = wo.shape[0]
    shape = jax.ShapeDtypeStruct
    return pl.pallas_call(
        out_back_body,
        in_specs=[pl.BlockSpec(memory_space=pltpu.SMEM)]
        + [pl.BlockSpec(memory_space=pltpu.VMEM)] * (3 + len(parts)),
        out_shape=[shape((rows, w), BF), shape((w, width), BF)],
        scratch_shapes=[pltpu.VMEM((rows, width), BF)],
        compiler_params=pltpu.CompilerParams(vmem_limit_bytes=VMEM_BYTES),
        cost_estimate=cost(4 * rows * width * w, 10 * rows * width),
        name="attention_out_back",
    )(core, cot, wo, o, *parts)


def input_back_body(nq, _, wq, wkv, *refs):
    dq = refs[:nq]
    dkv = refs[nq : 2 * nq]
    dh = refs[2 * nq]
    acc = None
    for w, parts in ((wq, dq), (wkv, dkv)):
        at = 0
        for part in parts:
            n = part.shape[1]
            term = dot_nt(part[...], w[:, at : at + n])
            acc = term if acc is None else acc + term
            at += n
    dh[...] = acc.astype(BF)


def input_back(tok, wq, wkv, dqs, dkvs):
    rows = dqs[0].shape[0]
    width = wq.shape[0]
    rt = 256
    nq = len(dqs)
    block = lambda n: pl.BlockSpec((rt, n), lambda i: (i, 0))
    return pl.pallas_call(
        functools.partial(input_back_body, nq),
        grid=(rows // rt,),
        in_specs=[pl.BlockSpec(memory_space=pltpu.SMEM), whole_block(wq), whole_block(wkv)] + [block(v.shape[1]) for v in (*dqs, *dkvs)],
        out_specs=block(width),
        out_shape=jax.ShapeDtypeStruct((rows, width), BF),
        compiler_params=pltpu.CompilerParams(vmem_limit_bytes=VMEM_BYTES),
        cost_estimate=cost(4 * rows * width * wq.shape[1], 10 * rows * width),
        name="input_back",
    )(tok, wq, wkv, *dqs, *dkvs)


def token_grads_body(npart, core, x, cot, own, other, gain, *refs):
    parts, out = refs[:npart], refs[npart]
    xb = x[...].astype(F32)
    r = lax.rsqrt(jnp.mean(xb * xb, axis=1, keepdims=True) + NORM_EPS)
    xhat = xb * r
    su = (own[...].astype(F32) + other[...].astype(F32)) * gain[...].astype(F32)
    norm = r * (su - xhat * jnp.mean(su * xhat, axis=1, keepdims=True))
    gm = parts[0][...].astype(F32)
    if npart == 2:
        half = pl.num_programs(0) // 2
        gm = jnp.where(core[0] == pl.program_id(0) // half, gm, parts[1][...].astype(F32))
    out[...] = cot[...].astype(F32) + gm + norm


def token_grads(core, x, cot, own, other, gain, parts):
    rows, width = x.shape
    rt = 128
    block = pl.BlockSpec((rt, width), lambda i, _: (i, 0))
    n = parts[0].shape[0] // rt
    part = pl.BlockSpec((rt, width), lambda i, _: (i % n, 0))
    return pl.pallas_call(
        functools.partial(token_grads_body, len(parts)),
        grid_spec=pltpu.PrefetchScalarGridSpec(
            num_scalar_prefetch=1,
            grid=(rows // rt,),
            in_specs=[block] * 4 + [whole_block(gain)] + [part] * len(parts),
            out_specs=block,
        ),
        out_shape=jax.ShapeDtypeStruct((rows, width), F32),
        compiler_params=pltpu.CompilerParams(vmem_limit_bytes=VMEM_BYTES),
        cost_estimate=cost(12 * rows * width, 14 * rows * width),
        name="token_grads",
    )(core, x, cot, own, other, gain, *parts)


def layer_out_body(nb, _, *refs):
    mid, live = refs[:2]
    moes = refs[2 : 2 + nb]
    out, stats = refs[2 + nb :]
    moe = sum(m[...].astype(F32) for m in moes) * RESID_SCALE
    outf = mid[...] + moe
    out[...] = outf.astype(BF)
    v = live[...]
    s0 = jnp.sum(v * jnp.sum(outf * outf, axis=1, keepdims=True))
    s2 = jnp.sum(v * jnp.sum(moe * moe, axis=1, keepdims=True))
    lane = lax.broadcasted_iota(jnp.int32, stats.shape, 1)

    @pl.when(pl.program_id(0) == 0)
    def _():
        stats[...] = jnp.zeros_like(stats)

    stats[...] += jnp.where(lane == 0, s0, jnp.where(lane == 2, s2, 0.0))


def layer_out_share(tok, mid, live, moes):
    rows, width = mid.shape
    shape = jax.ShapeDtypeStruct
    rt = 128
    block = lambda n: pl.BlockSpec((rt, n), lambda i: (i, 0))
    return pl.pallas_call(
        functools.partial(layer_out_body, len(moes)),
        grid=(rows // rt,),
        in_specs=[pl.BlockSpec(memory_space=pltpu.SMEM), block(width), block(1)] + [block(width)] * len(moes),
        out_specs=[block(width), pl.BlockSpec((8, 128), lambda i: (0, 0))],
        out_shape=[shape((rows, width), BF), shape((8, 128), F32)],
        compiler_params=pltpu.CompilerParams(vmem_limit_bytes=VMEM_BYTES),
        cost_estimate=cost(12 * rows * width, 14 * rows * width),
        name="layer_out",
    )(tok, mid, live, *moes)


def gather_rows_body(npart, cols, me, *refs):
    parts, outs = refs[: npart * len(cols)], refs[npart * len(cols) :]
    size = parts[0].shape[0]
    at = [0] * len(outs)
    for g, widths in enumerate(cols):
        begin = 0
        for j, w in enumerate(widths):
            if not w:
                continue
            for k in range(npart):
                rows = pl.ds(pl.multiple_of((me[0] ^ k) * size, size), size)
                outs[j][rows, at[j] : at[j] + w] = parts[g * npart + k][:, begin : begin + w].astype(F32)
            begin += w
            at[j] += w


def gather_rows(me, groups, cols):
    npart = len(groups[0])
    size = groups[0][0].shape[0]
    flat = [v for group in groups for v in group]
    widths = [sum(c[j] for c in cols) for j in range(len(cols[0]))]
    return pl.pallas_call(
        functools.partial(gather_rows_body, npart, cols),
        in_specs=[pl.BlockSpec(memory_space=pltpu.SMEM)] + [pl.BlockSpec(memory_space=pltpu.VMEM)] * len(flat),
        out_shape=[jax.ShapeDtypeStruct((npart * size, w), F32) for w in widths],
        compiler_params=pltpu.CompilerParams(vmem_limit_bytes=VMEM_BYTES),
        cost_estimate=cost(0, 6 * npart * size * sum(widths)),
        name="gather_rows",
    )(me, *flat)
HD = 64
NEG = -1e30
BLK = 256


def swap_halves(v, lane):
    return jnp.where(lane % HD < HD // 2, pltpu.roll(v, 128 - HD // 2, 1), pltpu.roll(v, HD // 2, 1))


def mask_bias(start, valid, i, keys):
    row = lax.broadcasted_iota(jnp.int32, (BLK, keys), 0) + i * BLK
    key = lax.broadcasted_iota(jnp.int32, (BLK, keys), 1)
    first = jnp.maximum(start, row[:, :1] - (WINDOW - 1))
    ok = (key >= first) & (key <= row) & ((valid[:, :keys] > 0) | (key == row))
    return jnp.where(ok, 0.0, NEG).astype(F32)


def doc_starts(lengths, place):
    start = jnp.zeros_like(place)
    end = 0
    for j in range(lengths.shape[1]):
        end = end + lengths[0, j]
        start = jnp.where(place >= end, end, start)
    return start


def prepare_body(core, gu, down, cot, routes, pack, pay):
    width, f = gu.shape[2:]
    share = cot.shape[0]
    pack[:2] = gu[0]
    for k in range(width // f):
        pack[2, k * f : (k + 1) * f, :] = down[0, :, k * f : (k + 1) * f]
    pay[:share, :] = cot[...]
    pay[share:, :] = jnp.zeros((pay.shape[0] - share, width), BF)
    pay[share : share + routes.shape[0], :share] = routes[...].astype(F32).astype(BF)


def prepare(core, gu, down, cot, routes):
    width, f = gu.shape[2:]
    share = routes.shape[1]
    shape = jax.ShapeDtypeStruct
    return pl.pallas_call(
        prepare_body,
        grid_spec=pltpu.PrefetchScalarGridSpec(
            num_scalar_prefetch=1,
            grid=(1,),
            in_specs=[
                whole_block(gu),
                whole_block(down),
                pl.BlockSpec((share, width), lambda _, c: (c[0], 0)),
                whole_block(routes),
            ],
            out_specs=[
                pl.BlockSpec((3, width, f), lambda *_: (0, 0, 0)),
                pl.BlockSpec((share + 16, width), lambda *_: (0, 0)),
            ],
        ),
        out_shape=[shape((3, width, f), BF), shape((share + 16, width), BF)],
        compiler_params=pltpu.CompilerParams(vmem_limit_bytes=VMEM_BYTES),
        cost_estimate=cost(0, 12 * width * f),
        name="prepare",
    )(core, gu, down, cot, routes)


def attn_forward_body(core, lengths, x, gain, wq, wkv, wo, valid, h1, q, kd, vd, o, lse, cos, sin, own, *rest):
    nkv = wkv.shape[1] // 128
    lane = lax.broadcasted_iota(jnp.int32, (BLK, 128), 1)
    low = lane < HD
    ga = gain[...].astype(F32)
    frequencies = jnp.exp((lane[:1] % (HD // 2)).astype(F32) * (-2.0 * math.log(ROPE_BASE) / HD))
    half = own.shape[0]
    for i in range(x.shape[0] // BLK):
        rs = pl.ds(i * BLK, BLK)
        keys = (i + 1) * BLK
        place = lax.broadcasted_iota(jnp.int32, (BLK, 1), 0) + i * BLK
        start = doc_starts(lengths, place)
        angles = (place - start).astype(F32) * frequencies
        cb = jnp.cos(angles)
        sb = jnp.sin(angles)
        sb = jnp.where(lane % HD < HD // 2, -sb, sb)
        cos[rs, :] = cb
        sin[rs, :] = sb
        xb = x[rs, :].astype(F32)
        r = lax.rsqrt(jnp.mean(xb * xb, axis=1, keepdims=True) + NORM_EPS)
        hb = (xb * r * ga).astype(BF)
        h1[rs, :] = hb
        qp = dot(hb, wq[...])
        kvp = dot(hb, wkv[...])
        for n in range(nkv):
            ns = slice(n * 128, (n + 1) * 128)
            qn = qp[:, ns]
            q[rs, ns] = ((qn * cb + swap_halves(qn, lane) * sb) * ATTN_SCALE).astype(BF)
            kv = kvp[:, ns]
            rot = kv * cb + swap_halves(kv, lane) * sb
            kd[rs, ns] = jnp.where(low, rot, pltpu.roll(rot, HD, 1)).astype(BF)
            vd[rs, ns] = jnp.where(low, pltpu.roll(kv, HD, 1), kv).astype(BF)
        bias = mask_bias(start, valid, i, keys)
        bias2 = jnp.concatenate([bias, bias], axis=0)
        lse_all = jnp.zeros((BLK, 128), F32)
        for n in range(nkv):
            ns = slice(n * 128, (n + 1) * 128)
            qn = q[rs, ns]
            zero = jnp.zeros_like(qn)
            q2 = jnp.concatenate([jnp.where(low, qn, zero), jnp.where(low, zero, qn)], axis=0)
            s = dot_nt(q2, kd[:keys, ns]) + bias2
            m = jnp.max(s, axis=1, keepdims=True)
            p = jnp.exp(s - m)
            total = jnp.sum(p, axis=1, keepdims=True)
            o2 = dot(p.astype(BF), vd[:keys, ns]) * (1.0 / total)
            o[rs, ns] = jnp.where(low, o2[:BLK], o2[BLK:]).astype(BF)
            l2 = m + jnp.log(total)
            lse_all = jnp.where(lane == 2 * n, l2[:BLK], jnp.where(lane == 2 * n + 1, l2[BLK:], lse_all))
        lse[rs, :] = lse_all
        term = dot(o[rs, :], wo[...]).astype(BF)
        if not rest:
            own[rs, :] = term
        else:
            at = pl.ds(i * BLK % half, BLK)

            @pl.when(core[0] == i * BLK // half)
            def _():
                own[at, :] = term

            @pl.when(core[0] != i * BLK // half)
            def _():
                rest[0][at, :] = term


def attn_forward(core, lengths, x, gain, wq, wkv, wo, valid, split):
    rows, width = x.shape
    wid = wq.shape[1]
    kvw = wkv.shape[1]
    shape = jax.ShapeDtypeStruct
    part = [shape((rows // 2, width), BF)] * 2 if split else [shape((rows, width), BF)]
    return pl.pallas_call(
        attn_forward_body,
        in_specs=[pl.BlockSpec(memory_space=pltpu.SMEM)] * 2 + [pl.BlockSpec(memory_space=pltpu.VMEM)] * 6,
        out_shape=[
            shape((rows, width), BF),
            shape((rows, wid), BF),
            shape((rows, kvw), BF),
            shape((rows, kvw), BF),
            shape((rows, wid), BF),
            shape((rows, 128), F32),
            shape((rows, 128), F32),
            shape((rows, 128), F32),
            *part,
        ],
        compiler_params=pltpu.CompilerParams(vmem_limit_bytes=VMEM_BYTES),
        cost_estimate=cost(2 * rows * width * 3 * wid + 4 * rows * rows * 4 * wid, 12 * rows * width),
        name="attention_forward",
    )(core, lengths, x, gain, wq, wkv, wo, valid)


def attn_backward_body(first, folded, _, lengths, q, kd, vd, do, lse, h1, cos, sin, valid, wq, wkv, gain, *rest):
    extras, (dq, dkv, gw, dk, dv) = rest[:-5], rest[-5:]
    if folded:
        extras, gwo = extras[:-1], extras[-1]
        depth = gwo.shape[0]
        for n in range(gwo.shape[1] // depth):
            rs = slice(n * depth, (n + 1) * depth)
            gw[rs, 2 * q.shape[1] + 128 :] = gwo[:, rs]
    nkv = kd.shape[1] // 128
    wid = q.shape[1]
    width = h1.shape[1]
    lane = lax.broadcasted_iota(jnp.int32, (BLK, 128), 1)
    low = lane < HD
    dk[...] = jnp.zeros_like(dk)
    dv[...] = jnp.zeros_like(dv)
    nb = q.shape[0] // BLK
    for i in range(nb):
        rs = pl.ds(i * BLK, BLK)
        keys = (i + 1) * BLK
        cb, sb = cos[rs, :], sin[rs, :]
        place = lax.broadcasted_iota(jnp.int32, (BLK, 1), 0) + i * BLK
        bias = mask_bias(doc_starts(lengths, place), valid, i, keys)
        bias2 = jnp.concatenate([bias, bias], axis=0)
        lse_i = lse[rs, :]
        for n in range(nkv):
            ns = slice(n * 128, (n + 1) * 128)
            qn, dn = q[rs, ns], do[rs, ns]
            zero = jnp.zeros_like(qn)
            q2 = jnp.concatenate([jnp.where(low, qn, zero), jnp.where(low, zero, qn)], axis=0)
            d2 = jnp.concatenate([jnp.where(low, dn, zero), jnp.where(low, zero, dn)], axis=0)
            h = 2 * (first + n)
            l2 = jnp.concatenate([lse_i[:, h : h + 1], lse_i[:, h + 1 : h + 2]], axis=0)
            p = jnp.exp(dot_nt(q2, kd[:keys, ns]) + bias2 - l2)
            dp = dot_nt(d2, vd[:keys, ns])
            shift = jnp.sum(p * dp, axis=1, keepdims=True)
            ds = (p * (dp - shift)).astype(BF)
            dv[:keys, ns] += dot_tn(p.astype(BF), d2)
            dk[:keys, ns] += dot_tn(ds, q2)
            dq2 = dot(ds, kd[:keys, ns])
            dqn = jnp.where(low, dq2[:BLK], dq2[BLK:]) * ATTN_SCALE
            dq[rs, ns] = (dqn * cb - swap_halves(dqn, lane) * sb).astype(BF)
    for i in range(nb):
        rs = pl.ds(i * BLK, BLK)
        cb, sb = cos[rs, :], sin[rs, :]
        for n in range(nkv):
            ns = slice(n * 128, (n + 1) * 128)
            kk = dk[rs, ns]
            kk = kk + pltpu.roll(kk, HD, 1)
            vv = dv[rs, ns]
            vv = vv + pltpu.roll(vv, HD, 1)
            dkv[rs, ns] = jnp.where(low, kk * cb - swap_halves(kk, lane) * sb, vv).astype(BF)
    gq = dot_tn(h1[...], dq[...])
    gk = dot_tn(h1[...], dkv[...])
    gw[:, :wid] = gq.astype(BF)
    gw[:, wid : 2 * wid] = gk.astype(BF)
    ga = jnp.sum(gq * wq[...].astype(F32) + gk * wkv[...].astype(F32), axis=1, keepdims=True) / gain[...].astype(F32)
    lanes = lax.broadcasted_iota(jnp.int32, (width, 128), 1)
    if extras:
        small, s1, s2 = extras
        stats = (s1[...] + s2[...]).T[:, :1]
        stats = jnp.concatenate([stats, jnp.zeros((width - 128, 1), F32)], axis=0)
        rest_cols = jnp.where(lanes == STATS, stats, small[...])
    else:
        rest_cols = jnp.zeros((width, 128), F32)
    gw[:, 2 * wid : 2 * wid + 128] = jnp.where(lanes == GAIN_A, ga, rest_cols).astype(BF)


def attn_backward(first, count, tok, lengths, q, kd, vd, do, lse, h1, cos, sin, valid, wq, wkv, gain, extras=(), gwo=None):
    rows, width = h1.shape
    w = count * 128
    cols = 2 * w + 128 + (0 if gwo is None else gwo.shape[0])
    folded = gwo is not None
    if folded:
        extras = (*extras, gwo)
    shape = jax.ShapeDtypeStruct
    part = pl.BlockSpec((rows, w), lambda _: (0, first // count))
    wpart = pl.BlockSpec((width, w), lambda _: (0, first // count))
    return pl.pallas_call(
        functools.partial(attn_backward_body, first, folded),
        grid=(1,),
        in_specs=[pl.BlockSpec(memory_space=pltpu.SMEM)] * 2
        + [part] * 4
        + [whole_block(v) for v in (lse, h1, cos, sin, valid)]
        + [wpart] * 2
        + [whole_block(v) for v in (gain, *extras)],
        out_specs=[
            pl.BlockSpec((rows, w), lambda _: (0, 0)),
            pl.BlockSpec((rows, w), lambda _: (0, 0)),
            pl.BlockSpec((width, cols), lambda _: (0, 0)),
        ],
        out_shape=[shape((rows, w), BF), shape((rows, w), BF), shape((width, cols), BF)],
        scratch_shapes=[pltpu.VMEM((rows, w), F32), pltpu.VMEM((rows, w), F32)],
        compiler_params=pltpu.CompilerParams(vmem_limit_bytes=VMEM_BYTES),
        cost_estimate=cost(4 * rows * width * w + 20 * rows * rows * w, 10 * rows * width),
        name="attention_backward",
    )(tok, lengths, q, kd, vd, do, lse, h1, cos, sin, valid, wq, wkv, gain, *extras)


def on_device(
    tokens,
    gain_attn,
    query_weight_matrix,
    key_value_weight,
    w_out,
    gain_ffn,
    w_router,
    w_gate_up,
    w_down,
    routes,
    doc_lengths,
    valid_mask,
    cotangent,
):
    rows, width = tokens.shape
    share = routes.shape[0]
    n_ep, n_tp = lax.axis_size("ep"), lax.axis_size("tp")
    nexp = w_router.shape[1]
    inner = math.gcd(n_ep, 4)
    outer = n_ep // inner
    me = lax.axis_index("ep")
    me_in = me % inner
    core = lax.axis_index("tp")[None]
    pair = n_tp == 2

    def across(v, k):
        return lax.ppermute(v, "ep", [(i, i ^ k) for i in range(n_ep)])

    def along(v, k):
        return lax.ppermute(v, "ep", [(i, (i + k * inner) % n_ep) for i in range(n_ep)])

    def swap(v):
        return lax.ppermute(v, "tp", [(0, 1), (1, 0)])

    def after(v, *earlier):
        return lax.optimization_barrier((v, *earlier))[0]

    def total(terms):
        acc = terms[0].astype(F32)
        for term in terms[1:]:
            acc = acc + term.astype(F32)
        return acc

    def scatter_plane(v):
        size = v.shape[0] // inner
        cut = lambda k: lax.dynamic_slice_in_dim(v, (me_in ^ k) * size, size)
        return [cut(0)] + [across(cut(k), k) for k in range(1, inner)]

    def summed(terms):
        return total(terms).astype(BF)

    def column_steps(v):
        bit = 1
        while bit < outer:
            other = lax.ppermute(v, "ep", [(i, i ^ (bit * inner)) for i in range(n_ep)])
            yield other
            v = summed([v, release(other)])
            bit *= 2
        yield v

    def unpacked(v):
        f = v.shape[2]
        return v[:2], v[2].reshape(width // f, f, f).transpose(1, 0, 2).reshape(f, width)

    def packed(gu, down):
        f = gu.shape[2]
        return jnp.concatenate([gu, down.reshape(f, width // f, f).transpose(1, 0, 2).reshape(1, width, f)])

    def full_hidden(v):
        if pair:
            return [v, swap(v)]
        gu, down = unpacked(v)
        return [
            packed(
                lax.all_gather(gu, "tp", axis=2, tiled=True),
                lax.all_gather(down, "tp", axis=0, tiled=True),
            )
        ]

    def own_hidden(v):
        if pair:
            return v[0].astype(F32) + swap(v[1]).astype(F32)
        gu, down = unpacked(v[0].astype(F32))
        return packed(
            lax.psum_scatter(gu, "tp", scatter_dimension=2, tiled=True),
            lax.psum_scatter(down, "tp", scatter_dimension=0, tiled=True),
        )

    halves = 2 if pair else 1
    local = jnp.arange(outer, dtype=jnp.int32) * inner
    ids = (me - local) % n_ep
    ids_all = jnp.concatenate([((me ^ k) - local) % n_ep for k in range(inner)])
    valid_row = valid_mask[None, :]
    live_all = valid_mask.astype(F32)[:, None]
    live = lax.dynamic_slice_in_dim(live_all, core[0] * share, share)
    gain_a, gain_f = gain_attn[None, :], gain_ffn[None, :]
    wr = jnp.pad(w_router, ((0, 0), (0, 128 - nexp)))

    tok = core

    def finish(*values):
        nonlocal tok
        tok = after(tok, *values)

    def release(v):
        return after(v, tok)

    pack, pay = prepare(tok, w_gate_up, w_down, cotangent, routes.T)
    held = [pack]
    if outer > 1:
        held.append(along(pack, 1))
    pays = [pay] + [across(pay, k) for k in range(1, min(inner, 3))]
    chunks = [full_hidden(pack)]
    finish(pack)

    h1, q, kd, vd, o, lse, cos, sin, *part = attn_forward(
        tok, doc_lengths, tokens, gain_a, query_weight_matrix, key_value_weight, w_out, valid_row, pair
    )
    if pair:
        own, other = part[0], swap(part[1])
    else:
        own = lax.psum_scatter(part[0].astype(F32), "tp", scatter_dimension=0, tiled=True)
        other = jnp.zeros_like(own)
    finish(own, other, *pays, *chunks[0])
    mid, h2, stats = middle_norm(tok, tokens, own, other, gain_f, live_all)
    h2s = [h2] + [across(h2, k) for k in range(1, min(inner, 3))]
    finish(h2, *held[1:])

    near = min(2, outer)
    last = outer - 1
    far = list(range(3, inner))
    close = list(range(min(inner, 3)))
    state = [None] * inner
    saved = [dict() for _ in range(inner)]

    def work(blocks, first, count):
        prevs = None if state[blocks[0]] is None else [state[b] for b in blocks]
        out = experts(
            release(ids),
            [h2s[b] for b in blocks],
            [pays[b] for b in blocks],
            prevs,
            wr,
            [c for r in range(first, first + count) for c in chunks[r]],
            halves,
            first,
        )
        for b, (dx, moe, gat, dgu) in zip(blocks, out, strict=True):
            state[b] = (dx, moe)
            for r in range(count):
                saved[b][first + r] = (gat, dgu, r * halves)
        finish(out[0][1])

    def expert_grads(experts_of):
        out = weight_grads(tok, h2s, pays, [[s[r] for r in experts_of] for s in saved], halves)
        finish(out[0])
        return out

    def next_held():
        v = release(held[-1])
        if len(held) < outer:
            held.append(along(v, 1))
        chunks.append(full_hidden(v))

    if outer > 1:
        next_held()
    work([0], 0, near)
    finish(*h2s)
    for b in close[1:]:
        work([b], 0, near)
        if b == 1:
            if outer > 2:
                finish(held[-1])
                next_held()
            for k in far:
                pays.append(across(release(pay), k))
                h2s.append(across(release(h2), k))
    for r in range(near, last):
        work(close, r, 1)
        if r + 1 < last:
            finish(held[-1])
            next_held()
    finish(*h2s, *pays)
    for b in far:
        work([b], 0, max(last, near))
    if last >= near:
        finish(held[-1])
        next_held()

    first = 1 % outer
    later = [[r] for r in range(2, min(outer, 3))] + [[*range(3, outer), 0]]
    later = later if outer > 1 else []
    raw = expert_grads([first])
    parts = {first: own_hidden([v[0] for v in raw])}
    if last >= near and inner > 1:
        work(list(range(1, inner)), last, 1)
    ring = parts[first].astype(BF)
    finish(ring)
    if outer > 1:
        ring = along(ring, 1)
    dxs = [None] + [across(state[k][0], k) for k in range(1, inner)]
    if last >= near:
        work([0], last, 1)
    dxs[0] = state[0][0]
    raws = [expert_grads(rs) for rs in later]
    finish(*dxs, *([ring] if outer > 1 else []))
    moes = [state[0][1]] + [across(release(state[k][1]), k) for k in range(1, inner)]

    def ring_step(r):
        nonlocal ring
        term = release(ring).astype(F32) + parts[r]
        if r == 0:
            return term
        ring = term.astype(BF)
        finish(ring)
        ring = along(ring, 1)

    gm_share, small = middle_back(tok, ids_all, h2, mid, gain_f, pay, wr, dxs, outer)
    gm = [gm_share, swap(gm_share)] if pair else [lax.all_gather(gm_share, "tp", axis=0, tiled=True)]
    finish(gm_share)
    for rs, raw in zip(later, raws, strict=True):
        if pair:
            other = swap(release(raw[1]))
            parts.update({r: raw[0][n].astype(F32) + other[n].astype(F32) for n, r in enumerate(rs)})
            if rs == [2]:
                finish(other)
        else:
            parts.update({r: own_hidden([raw[0][n]]) for n, r in enumerate(rs)})
    if outer > 2:
        ring_step(2)
    do, gwo = out_back(tok, cotangent, w_out, o, gm)
    finish(do)

    nkv = kd.shape[1] // 128
    groups = 2 if nkv % 2 == 0 else 1
    each = nkv // groups
    dqs, dkvs, terms = [], [], []
    for n in range(groups):
        if n == groups - 1:
            finish(*moes)
            out_share, stats_out = layer_out_share(tok, mid, live, moes)
            finish(out_share)
            if outer > 3:
                finish(ring)
                ring_step(3)
        dq, dkv, gw = attn_backward(
            n * each,
            each,
            tok,
            doc_lengths,
            q,
            kd,
            vd,
            do,
            lse,
            h1,
            cos,
            sin,
            valid_row,
            query_weight_matrix,
            key_value_weight,
            gain_attn[:, None],
            (small, stats, stats_out) if n == groups - 1 else (),
            gwo if n == 0 else None,
        )
        finish(gw)
        dqs.append(dq)
        dkvs.append(dkv)
        if n == 0:
            terms.append(scatter_plane(gw))
    finish(*terms[0])
    ahead = column_steps(summed([release(t) for t in terms[0]]))
    moving = next(ahead)
    if groups > 1:
        terms.append(scatter_plane(release(gw)))
    dh1 = input_back(tok, query_weight_matrix, key_value_weight, dqs, dkvs)
    finish(dh1, moving, *([ring] if outer > 1 else []))
    if pair:
        dh_other = swap(release(dh1))
        out_other = swap(release(out_share))
    else:
        dh1, dh_other = lax.psum(dh1.astype(F32), "tp"), jnp.zeros_like(dh1)
    if groups > 1:
        moving = next(ahead)
    finish(dh_other)
    grad_tokens = token_grads(tok, tokens, cotangent, dh1, dh_other, gain_a, gm)
    finish(grad_tokens)
    gws = []
    if groups > 1:
        finish(*terms[1])
        behind = column_steps(summed([release(t) for t in terms[1]]))
        late = next(behind)
    if pair:
        layer_out = jnp.where(
            core[0] == 0,
            jnp.concatenate([release(out_share), out_other]),
            jnp.concatenate([out_other, release(out_share)]),
        )
        finish(layer_out)
    else:
        layer_out = lax.all_gather(out_share, "tp", axis=0, tiled=True)
    finish(moving)
    for v in ahead:
        whole = v
    gws.append([whole] + [across(release(whole), k) for k in range(1, inner)])
    if groups > 1:
        finish(late)
        for v in behind:
            late = v
        gws.append([late] + [across(release(late), k) for k in range(1, inner)])
    for r in range(4, outer):
        ring_step(r)
    sums = ring_step(0) if outer > 1 else parts[0]
    gu_grad, down_grad = unpacked(sums)
    w = each * 128
    depth = w_out.shape[0]
    grad_w_query, grad_w_kv, extras, folded = gather_rows(
        release(me_in[None]), gws, [(w, w, 128, depth if n == 0 else 0) for n in range(groups)]
    )
    grad_w_out = jnp.concatenate([folded[n * depth : (n + 1) * depth] for n in range(width // depth)], axis=1)
    extras = sum(extras[:, n * 128 : (n + 1) * 128] for n in range(groups))
    extras = extras + swap(extras) if pair else lax.psum(extras, "tp")
    s = extras[:4, STATS]
    return (
        layer_out,
        grad_tokens,
        extras[:, GAIN_A],
        grad_w_query,
        grad_w_kv,
        grad_w_out,
        extras[:, GAIN_F],
        extras[:, :nexp],
        gu_grad[None],
        down_grad[None],
        jnp.sqrt(s[:3] / (s[3] * width)),
    )


def solution(mesh):
    return jax.shard_map(
        on_device,
        mesh=mesh,
        in_specs=(
            P("ep", None),
            P(),
            P(None, "tp"),
            P(None, "tp"),
            P("tp", None),
            P(),
            P(),
            P("ep", None, None, "tp"),
            P("ep", "tp", None),
            P(("ep", "tp"), None),
            P("ep", None),
            P("ep"),
            P("ep", None),
        ),
        out_specs=(
            P("ep", None),
            P("ep", None),
            P(),
            P(None, "tp"),
            P(None, "tp"),
            P("tp", None),
            P(),
            P(),
            P("ep", None, None, "tp"),
            P("ep", "tp", None),
            P(),
        ),
        check_vma=False,
    )
```

time: 639 us -> 496 us (0.78)
  waiting for transfers between devices: 236 us -> 113 us
  starting transfers between devices: 93.2 us -> 42.7 us
  Pallas kernels: 234 us -> 278 us
  other arithmetic: 35.2 us -> 28.6 us
    ppermute x36 -> x6, waiting for transfers between devices: 117 us -> 0.04 us  [along(): lax.ppermute(v, 'ep', [(i, (i + k * inner) % n_ep) for i in range(n_ep)])]
    ppermute x42 -> x24, waiting for transfers between devices: 117 us -> 59.7 us  [across(): return lax.ppermute(v, 'ep', [(i, i ^ k) for i in range(n_ep)])]
    ppermute x0 -> x4, waiting for transfers between devices: none -> 45.2 us  [column_steps(): other = lax.ppermute(v, 'ep', [(i, i ^ bit * inner) for i in range(n_ep)])]
    pallas_call x17 -> x21, Pallas kernels: 234 us -> 278 us  [the longest x7 117 us: experts(): pl.pallas_call(functools.partial(experts_body, nb, nchunk, halves, first,...]
    ppermute x42 -> x24, starting transfers between devices: 65.5 us -> 28.8 us  [across(): return lax.ppermute(v, 'ep', [(i, i ^ k) for i in range(n_ep)])]
    ppermute x36 -> x6, starting transfers between devices: 25.3 us -> 9.96 us  [along(): lax.ppermute(v, 'ep', [(i, (i + k * inner) % n_ep) for i in range(n_ep)])]
    squeeze x8 -> x0, local copies, waits for them, and re-layouts: 9.8 us -> none  [the longest x4 5.63 us: expert_grads(): down_w[1]]
    ppermute x22 -> x12, waiting for transfers between devices: 1.13 us -> 7.97 us  [swap(): return lax.ppermute(v, 'tp', [(0, 1), (1, 0)])]
  transfers between devices with their start and end apart: 100 -> 46, of which waited for: 39 -> 17; matrix products, arithmetic and copies ran while one was open for 9% -> 8% of each run, Pallas kernels for 37% -> 50%
where the time goes in v2:
time: 496 us; the launch traced here: 489 us
  Pallas kernels  278 us (56%)
  waiting for transfers between devices  113 us (23%)
  starting transfers between devices  42.7 us (9%)
  other arithmetic  28.6 us (6%)
  local copies, waits for them, and re-layouts  24.3 us (5%)
    pallas_call x7, Pallas kernels, experts(): pl.pallas_call(functools.partial(experts_body, nb, nchunk, halves, first,...  117 us
    ppermute x24, waiting for transfers between devices, across(): return lax.ppermute(v, 'ep', [(i, i ^ k) for i in range(n_ep)])  59.7 us
    pallas_call x3, Pallas kernels, weight_grads(): pl.pallas_call(functools.partial(weight_grads_body, nb, halves), grid=(ne...  49.6 us
    ppermute x4, waiting for transfers between devices, column_steps(): other = lax.ppermute(v, 'ep', [(i, i ^ bit * inner) for i in range(n_ep)])  45.2 us
    pallas_call x2, Pallas kernels, attn_backward(): pl.pallas_call(functools.partial(attn_backward_body, first, folded), grid...  36.4 us
    ppermute x24, starting transfers between devices, across(): return lax.ppermute(v, 'ep', [(i, i ^ k) for i in range(n_ep)])  28.8 us
    pallas_call x1, Pallas kernels, attn_forward(): pl.pallas_call(attn_forward_body, in_specs=[pl.BlockSpec(memory_space=plt...  25.7 us
    unnamed x68, local copies, waits for them, and re-layouts  10.4 us
  transfers between devices with their start and end apart: 46, of which 17 were waited for; matrix products, arithmetic and copies ran while one was open for 8% of the time, Pallas kernels for 50%

profile of v2, /device:TPU:0, one launch (start us, length us, event | category | flops | bytes accessed | tf_op | source)
XLA Modules:
  0.0 488.8 jit_solution(716530422267604272)
XLA Ops:
  10.6 25.7 %attention_forward.1 = (bf16[1024,1024]{1,0:T(8,128)(2,1)}, bf16[1024,512]{1,0:T(8,128)(2,1)}, bf16[1024,512]{1,0:T(8,128)(2,1)}, bf16[1024,512]{1,0:T(8,128)(2,...) custom-call(s32[1]{0:T(128)} %bitcast.core._, ...), custom_call_target="tpu_custom_call" | custom-call | flops 236223200 | bytes 251658 | tf_op jit(solution)/shard_map/attention_forward/pallas_call | solution.py:614
  50.7 13.5 %experts.7 = (bf16[528,1024]{1,0:T(8,128)(2,1)}, bf16[512,1024]{1,0:T(8,128)(2,1)}, bf16[4,256,512]{2,1,0:T(8,128)(2,1)}, bf16[4,512,512]{2,1,0:T(8,128)(2,1)}) custom-call(s32[4]{0:T(128)} %and_select_fusion.3.refs_0_, bf16[512,1024]{1,0:T(8,128)(2,1)} %get-tuple-element.195.refs_1_.refs_0_, bf16[528,1024]{1,0:T(8,128)(2,1)} %get-tuple-element.196.refs_2_.refs_4_, ...), custom_call_target="tpu_custom_call" | custom-call | flops 128849016 | bytes 251658 | tf_op jit(solution)/shard_map/experts/pallas_call | solution.py:182
  64.1 7.9 %collective-permute-done.6.refs_1_.refs_2_ = bf16[512,1024]{1,0:T(8,128)(2,1)S(1)} collective-permute-done((bf16[512,1024]{1,0:T(8,128)(2,1)}, bf16[512,1024]{1,0:T(8,128)(2,1)S(1)}, u32[]{:S(2)}, u32[]{:S(2)}) %collective-permute-start.6) | collective-permute-done | bytes 1048608 | tf_op jit(solution)/shard_map/ppermute | solution.py:759
  73.0 13.5 %experts.8 = (bf16[528,1024]{1,0:T(8,128)(2,1)}, bf16[512,1024]{1,0:T(8,128)(2,1)}, bf16[4,256,512]{2,1,0:T(8,128)(2,1)}, bf16[4,512,512]{2,1,0:T(8,128)(2,1)}) custom-call(s32[4]{0:T(128)} %and_select_fusion.3.refs_0_, bf16[512,1024]{1,0:T(8,128)(2,1)} %copy-done.4, bf16[528,1024]{1,0:T(8,128)(2,1)} %copy-done.2, ...), custom_call_target="tpu_custom_call" | custom-call | flops 128849016 | bytes 251658 | tf_op jit(solution)/shard_map/experts/pallas_call | solution.py:182
  91.2 13.6 %experts.9 = (bf16[528,1024]{1,0:T(8,128)(2,1)}, bf16[512,1024]{1,0:T(8,128)(2,1)}, bf16[4,256,512]{2,1,0:T(8,128)(2,1)}, bf16[4,512,512]{2,1,0:T(8,128)(2,1)}) custom-call(s32[4]{0:T(128)} %and_select_fusion.3.refs_0_, bf16[512,1024]{1,0:T(8,128)(2,1)} %collective-permute-done.7.refs_1_.refs_3_.refs_2_, bf16[528,1024]{1,0:T(8,128)(2,1)} %copy-done.3, ...), custom_call_target="tpu_custom_call" | custom-call | flops 128849016 | bytes 251658 | tf_op jit(solution)/shard_map/experts/pallas_call | solution.py:182
  104.8 23.7 %experts.10 = (bf16[528,1024]{1,0:T(8,128)(2,1)}, bf16[512,1024]{1,0:T(8,128)(2,1)}, bf16[2,256,512]{2,1,0:T(8,128)(2,1)}, bf16[2,512,512]{2,1,0:T(8,128)(2,1)},...) custom-call(s32[4]{0:T(128)} %and_select_fusion.3.refs_0_, ...), custom_call_target="tpu_custom_call" | custom-call | flops 193273536 | bytes 440401 | tf_op jit(solution)/shard_map/experts/pallas_call | solution.py:182
  128.5 9.1 %collective-permute-done.10.refs_1_.refs_3_ = bf16[512,1024]{1,0:T(8,128)(2,1)} collective-permute-done((bf16[512,1024]{1,0:T(8,128)(2,1)S(1)}, bf16[512,1024]{1,0:T(8,128)(2,1)}, u32[]{:S(2)}, u32[]{:S(2)}) %collective-permute-start.10) | collective-permute-done | bytes 1048608 | tf_op jit(solution)/shard_map/ppermute | solution.py:759
  138.7 17.7 %experts.11 = (bf16[528,1024]{1,0:T(8,128)(2,1)}, bf16[512,1024]{1,0:T(8,128)(2,1)}, bf16[6,256,512]{2,1,0:T(8,128)(2,1)}, bf16[6,512,512]{2,1,0:T(8,128)(2,1)}) custom-call(s32[4]{0:T(128)} %and_select_fusion.3.refs_0_, bf16[512,1024]{1,0:T(8,128)(2,1)} %collective-permute-done.10.refs_1_.refs_3_, bf16[528,1024]{1,0:T(8,128)(2,1)} %copy-done.5, ...), custom_call_target="tpu_custom_call" | custom-call | flops 193273536 | bytes 314572 | tf_op jit(solution)/shard_map/experts/pallas_call | solution.py:182
  156.4 13.8 %expert_weight_grads.3 = (bf16[1,3,1024,256]{3,2,1,0:T(8,128)(2,1)}, bf16[1,3,1024,256]{3,2,1,0:T(8,128)(2,1)}) custom-call(s32[1]{0:T(128)} %bitcast.core._, bf16[512,1024]{1,0:T(8,128)(2,1)} %get-tuple-element.195.refs_1_.refs_0_, bf16[512,1024]{1,0:T(8,128)(2,1)} %copy-done.4, bf16[512,1024]{1,0:T(8,128)(2,1)} %collective-permute-done.7.refs_1_.refs_3_.refs_2_, ...), custom_call_target="tpu_custom_call" | custom-call | flops 128849016 | bytes 230686 | tf_op jit(solution)/shard_map/expert_weight_grads/pallas_call | solution.py:255
  178.4 24.4 %experts.12 = (bf16[528,1024]{1,0:T(8,128)(2,1)}, bf16[512,1024]{1,0:T(8,128)(2,1)}, bf16[2,256,512]{2,1,0:T(8,128)(2,1)}, bf16[2,512,512]{2,1,0:T(8,128)(2,1)},...) custom-call(s32[4]{0:T(128)} %and_select_fusion.3.refs_0_, ...), custom_call_target="tpu_custom_call" | custom-call | flops 193273536 | bytes 440401 | tf_op jit(solution)/shard_map/experts/pallas_call | solution.py:182
  206.9 10.3 %experts.13 = (bf16[528,1024]{1,0:T(8,128)(2,1)}, bf16[512,1024]{1,0:T(8,128)(2,1)}, bf16[2,256,512]{2,1,0:T(8,128)(2,1)}, bf16[2,512,512]{2,1,0:T(8,128)(2,1)}) custom-call(s32[4]{0:T(128)} %and_select_fusion.3.refs_0_, bf16[512,1024]{1,0:T(8,128)(2,1)} %get-tuple-element.195.refs_1_.refs_0_, bf16[528,1024]{1,0:T(8,128)(2,1)} %get-tuple-element.196.refs_2_.refs_4_, ...), custom_call_target="tpu_custom_call" | custom-call | flops 64424508 | bytes 188743 | tf_op jit(solution)/shard_map/experts/pallas_call | solution.py:182
  217.2 13.8 %expert_weight_grads.4 = (bf16[1,3,1024,256]{3,2,1,0:T(8,128)(2,1)}, bf16[1,3,1024,256]{3,2,1,0:T(8,128)(2,1)}) custom-call(s32[1]{0:T(128)} %bitcast.core._, bf16[512,1024]{1,0:T(8,128)(2,1)} %get-tuple-element.195.refs_1_.refs_0_, bf16[512,1024]{1,0:T(8,128)(2,1)} %copy-done.4, bf16[512,1024]{1,0:T(8,128)(2,1)} %collective-permute-done.7.refs_1_.refs_3_.refs_2_, ...), custom_call_target="tpu_custom_call" | custom-call | flops 128849016 | bytes 230686 | tf_op jit(solution)/shard_map/expert_weight_grads/pallas_call | solution.py:255
  231.1 22.0 %expert_weight_grads.5 = (bf16[2,3,1024,256]{3,2,1,0:T(8,128)(2,1)}, bf16[2,3,1024,256]{3,2,1,0:T(8,128)(2,1)}) custom-call(s32[1]{0:T(128)} %bitcast.core._, bf16[512,1024]{1,0:T(8,128)(2,1)} %get-tuple-element.195.refs_1_.refs_0_, bf16[512,1024]{1,0:T(8,128)(2,1)} %copy-done.4, bf16[512,1024]{1,0:T(8,128)(2,1)} %collective-permute-done.7.refs_1_.refs_3_.refs_2_, ...), custom_call_target="tpu_custom_call" | custom-call | flops 128849016 | bytes 230686 | tf_op jit(solution)/shard_map/expert_weight_grads/pallas_call | solution.py:255
  254.1 9.9 %middle_back.1 = (bf16[512,1024]{1,0:T(8,128)(2,1)}, f32[1024,128]{1,0:T(8,128)}) custom-call(s32[1]{0:T(128)} %bitcast.core._, s32[16]{0:T(128)} %pad_add_fusion.refs_0_, bf16[512,1024]{1,0:T(8,128)(2,1)} %get-tuple-element.195.refs_1_.refs_0_, f32[512,1024]{1,0:T(8,128)} %get-tuple-element.250.refs_2_.refs_0_, ...), custom_call_target="tpu_custom_call" | custom-call | flops 419430 | bytes 209715 | tf_op jit(solution)/shard_map/middle_back/pallas_call | solution.py:300
  278.8 6.1 %attention_out_back.1 = (bf16[1024,512]{1,0:T(8,128)(2,1)}, bf16[512,1024]{1,0:T(8,128)(2,1)}) custom-call(s32[1]{0:T(128)} %bitcast.core._, bf16[1024,1024]{1,0:T(8,128)(2,1)} %cot.5, bf16[512,1024]{1,0:T(8,128)(2,1)} %wo.3, bf16[1024,512]{1,0:T(8,128)(2,1)} %get-tuple-element.258.o, bf16[512,1024]{1,0:T(8,128)(2,1)} %get-tuple-element.251.refs_0_, ...), custom_call_target="tpu_custom_call" | custom-call | flops 42949672 | bytes 209715 | tf_op jit(solution)/shard_map/attention_out_back/pallas_call | solution.py:335
  284.9 17.9 %attention_backward.2 = (bf16[1024,256]{1,0:T(8,128)(2,1)}, bf16[1024,256]{1,0:T(8,128)(2,1)}, bf16[1024,1152]{1,0:T(8,128)(2,1)}) custom-call(s32[1]{0:T(128)} %bitcast.core._, s32[1,4]{1,0:T(1,128)} %lengths.5, bf16[1024,512]{1,0:T(8,128)(2,1)} %get-tuple-element.261.q, bf16[1024,512]{1,0:T(8,128)(2,1)} %get-tuple-element.262.kd, ...), custom_call_target="tpu_custom_call" | custom-call | flops 128849016 | bytes 209715 | tf_op jit(solution)/shard_map/attention_backward/pallas_call | solution.py:711
  302.8 19.2 %collective-permute-done.22.refs_4_ = bf16[512,1024]{1,0:T(8,128)(2,1)} collective-permute-done((bf16[512,1024]{1,0:T(8,128)(2,1)}, bf16[512,1024]{1,0:T(8,128)(2,1)}, u32[]{:S(2)}, u32[]{:S(2)}) %collective-permute-start.22) | collective-permute-done | bytes 1048608 | tf_op jit(solution)/shard_map/ppermute | solution.py:759
  336.8 18.5 %attention_backward.3 = (bf16[1024,256]{1,0:T(8,128)(2,1)}, bf16[1024,256]{1,0:T(8,128)(2,1)}, bf16[1024,640]{1,0:T(8,128)(2,1)}) custom-call(s32[1]{0:T(128)} %bitcast.core._, s32[1,4]{1,0:T(1,128)} %lengths.5, bf16[1024,512]{1,0:T(8,128)(2,1)} %get-tuple-element.261.q, bf16[1024,512]{1,0:T(8,128)(2,1)} %get-tuple-element.262.kd, ...), custom_call_target="tpu_custom_call" | custom-call | flops 128849016 | bytes 209715 | tf_op jit(solution)/shard_map/attention_backward/pallas_call | solution.py:711
  360.4 6.2 %input_back.1.own = bf16[1024,1024]{1,0:T(8,128)(2,1)} custom-call(s32[1]{0:T(128)} %bitcast.core._, bf16[1024,512]{1,0:T(8,128)(2,1)} %wq.7, bf16[1024,512]{1,0:T(8,128)(2,1)} %wkv.7, bf16[1024,256]{1,0:T(8,128)(2,1)} %get-tuple-element.290.refs_0_, bf16[1024,256]{1,0:T(8,128)(2,1)} %get-tuple-element.291.refs_1_, ...), custom_call_target="tpu_custom_call" | custom-call | flops 42949672 | bytes 209715 | tf_op jit(solution)/shard_map/input_back/pallas_call | solution.py:368
  366.6 19.1 %collective-permute-done.29 = bf16[256,1152]{1,0:T(8,128)(2,1)S(1)} collective-permute-done((bf16[256,1152]{1,0:T(8,128)(2,1)S(1)}, bf16[256,1152]{1,0:T(8,128)(2,1)S(1)}, u32[]{:S(2)}, u32[]{:S(2)}) %collective-permute-start.29) | collective-permute-done | bytes 589856 | tf_op jit(solution)/shard_map/ppermute | solution.py:787
  394.5 9.4 %token_grads.1 = f32[1024,1024]{1,0:T(8,128)} custom-call(s32[1]{0:T(128)} %bitcast.core._, bf16[1024,1024]{1,0:T(8,128)(2,1)} %x.7, bf16[1024,1024]{1,0:T(8,128)(2,1)} %cot.5, bf16[1024,1024]{1,0:T(8,128)(2,1)} %input_back.1.own, bf16[1024,1024]{1,0:T(8,128)(2,1)} %copy-done.14, bf16[1,1024]{1,0:T(2,128)(2,1)} %broadcast_in_dim.26.gain, ...), custom_call_target="tpu_custom_call" | custom-call | flops 251658 | bytes 293601 | tf_op jit(solution)/shard_map/token_grads/pallas_call | solution.py:400
  412.5 8.0 %collective-permute-done.36 = bf16[256,1152]{1,0:T(8,128)(2,1)} collective-permute-done((bf16[256,1152]{1,0:T(8,128)(2,1)S(1)}, bf16[256,1152]{1,0:T(8,128)(2,1)}, u32[]{:S(2)}, u32[]{:S(2)}) %collective-permute-start.36) | collective-permute-done | bytes 589856 | tf_op jit(solution)/shard_map/ppermute | solution.py:787
  430.2 13.8 %collective-permute-done.41 = bf16[256,640]{1,0:T(8,128)(2,1)S(1)} collective-permute-done((bf16[256,640]{1,0:T(8,128)(2,1)S(1)}, bf16[256,640]{1,0:T(8,128)(2,1)S(1)}, u32[]{:S(2)}, u32[]{:S(2)}) %collective-permute-start.41) | collective-permute-done | bytes 327712 | tf_op jit(solution)/shard_map/ppermute | solution.py:787
  457.7 11.8 %collective-permute-done.43.refs_6_ = bf16[256,640]{1,0:T(8,128)(2,1)S(1)} collective-permute-done((bf16[256,640]{1,0:T(8,128)(2,1)S(1)}, bf16[256,640]{1,0:T(8,128)(2,1)S(1)}, u32[]{:S(2)}, u32[]{:S(2)}) %collective-permute-start.43) | collective-permute-done | bytes 327712 | tf_op jit(solution)/shard_map/ppermute | solution.py:759
  (193 shorter events, 137.9 us)
Async XLA Ops:
  4.0 35.2 %collective-permute-start.3 = (bf16[3,1024,256]{2,1,0:T(8,128)(2,1)}, bf16[3,1024,256]{2,1,0:T(8,128)(2,1)}, u32[]{:S(2)}, u32[]{:S(2)}) collective-permute-start(bf16[3,1024,256]{2,1,0:T(8,128)(2,1)} %get-tuple-element.168.refs_4_), channel_id=1, source_target_pairs={{0,1},{1,0},{2,3},{3,2},{4,5},{5,4},{6,7},{7,6},{8,9},{9,8},{10,11... | collective-permute-start | bytes 4718600 | tf_op jit(solution)/shard_map/ppermute | solution.py:765
  4.4 40.0 %collective-permute-start.4 = (bf16[3,1024,256]{2,1,0:T(8,128)(2,1)}, bf16[3,1024,256]{2,1,0:T(8,128)(2,1)}, u32[]{:S(2)}, u32[]{:S(2)}) collective-permute-start(bf16[3,1024,256]{2,1,0:T(8,128)(2,1)} %get-tuple-element.168.refs_4_), channel_id=1, source_target_pairs={{0,8},{2,10},{4,12},{6,14},{8,16},{10,18},{12,20},{14,22},{16,24},... | collective-permute-start | bytes 4718600 | tf_op jit(solution)/shard_map/ppermute | solution.py:762
  7.0 32.1 %collective-permute-start.1 = (bf16[528,1024]{1,0:T(8,128)(2,1)}, bf16[528,1024]{1,0:T(8,128)(2,1)S(1)}, u32[]{:S(2)}, u32[]{:S(2)}) collective-permute-start(bf16[528,1024]{1,0:T(8,128)(2,1)} %get-tuple-element.196.refs_2_.refs_4_), channel_id=1, source_target_pairs={{0,2},{2,0},{4,6},{6,4},{8,10},{10,8},{12,14},{14,12},{16,18},{18,... | collective-permute-start | bytes 3244040 | tf_op jit(solution)/shard_map/ppermute | solution.py:759
  8.5 30.7 %collective-permute-start.2 = (bf16[528,1024]{1,0:T(8,128)(2,1)}, bf16[528,1024]{1,0:T(8,128)(2,1)S(1)}, u32[]{:S(2)}, u32[]{:S(2)}) collective-permute-start(bf16[528,1024]{1,0:T(8,128)(2,1)} %get-tuple-element.196.refs_2_.refs_4_), channel_id=1, source_target_pairs={{0,4},{2,6},{4,0},{6,2},{8,12},{10,14},{12,8},{14,10},{16,20},{18,... | collective-permute-start | bytes 3244040 | tf_op jit(solution)/shard_map/ppermute | solution.py:759
  44.6 41.9 %collective-permute-start.8 = (bf16[3,1024,256]{2,1,0:T(8,128)(2,1)}, bf16[3,1024,256]{2,1,0:T(8,128)(2,1)}, u32[]{:S(2)}, u32[]{:S(2)}) collective-permute-start(bf16[3,1024,256]{2,1,0:T(8,128)(2,1)} %collective-permute-done.4.refs_6_), channel_id=1, source_target_pairs={{0,8},{2,10},{4,12},{6,14},{8,16},{10,18},{12,20},{14,22},{16,24},... | collective-permute-start | bytes 4718600 | tf_op jit(solution)/shard_map/ppermute | solution.py:762
  86.6 69.8 %collective-permute-start.12 = (bf16[3,1024,256]{2,1,0:T(8,128)(2,1)}, bf16[3,1024,256]{2,1,0:T(8,128)(2,1)}, u32[]{:S(2)}, u32[]{:S(2)}) collective-permute-start(bf16[3,1024,256]{2,1,0:T(8,128)(2,1)} %collective-permute-done.8.refs_14_.refs_8_), channel_id=1, source_target_pairs={{0,8},{2,10},{4,12},{6,14},{8,16},{10,18},{12,20},{14,22},{16,24},... | collective-permute-start | bytes 4718600 | tf_op jit(solution)/shard_map/ppermute | solution.py:762
  88.2 49.4 %collective-permute-start.11 = (bf16[528,1024]{1,0:T(8,128)(2,1)S(1)}, bf16[528,1024]{1,0:T(8,128)(2,1)S(1)}, u32[]{:S(2)}, u32[]{:S(2)}) collective-permute-start(bf16[528,1024]{1,0:T(8,128)(2,1)S(1)} %copy-done), channel_id=1, source_target_pairs={{0,6},{2,4},{4,2},{6,0},{8,14},{10,12},{12,10},{14,8},{16,22},{18,... | collective-permute-start | bytes 3244040 | tf_op jit(solution)/shard_map/ppermute | solution.py:759
  89.0 48.6 %collective-permute-start.10 = (bf16[512,1024]{1,0:T(8,128)(2,1)S(1)}, bf16[512,1024]{1,0:T(8,128)(2,1)}, u32[]{:S(2)}, u32[]{:S(2)}) collective-permute-start(bf16[512,1024]{1,0:T(8,128)(2,1)S(1)} %copy-done.1), channel_id=1, source_target_pairs={{0,6},{2,4},{4,2},{6,0},{8,14},{10,12},{12,10},{14,8},{16,22},{18,... | collective-permute-start | bytes 3145736 | tf_op jit(solution)/shard_map/ppermute | solution.py:759
  176.9 76.3 %collective-permute-start.18 = (bf16[3,1024,256]{2,1,0:T(8,128)(2,1)}, bf16[3,1024,256]{2,1,0:T(8,128)(2,1)S(1)}, u32[]{:S(2)}, u32[]{:S(2)}) collective-permute-start(bf16[3,1024,256]{2,1,0:T(8,128)(2,1)} %fusion), channel_id=1, source_target_pairs={{0,8},{2,10},{4,12},{6,14},{8,16},{10,18},{12,20},{14,22},{16,24},... | collective-permute-start | bytes 4718600 | tf_op jit(solution)/shard_map/ppermute | solution.py:762
  202.8 50.3 %collective-permute-start.15 = (bf16[528,1024]{1,0:T(8,128)(2,1)}, bf16[528,1024]{1,0:T(8,128)(2,1)S(1)}, u32[]{:S(2)}, u32[]{:S(2)}) collective-permute-start(bf16[528,1024]{1,0:T(8,128)(2,1)} %get-tuple-element.246), channel_id=1, source_target_pairs={{0,2},{2,0},{4,6},{6,4},{8,10},{10,8},{12,14},{14,12},{16,18},{18,... | collective-permute-start | bytes 3244040 | tf_op jit(solution)/shard_map/ppermute | solution.py:759
  203.7 49.4 %collective-permute-start.16 = (bf16[528,1024]{1,0:T(8,128)(2,1)}, bf16[528,1024]{1,0:T(8,128)(2,1)}, u32[]{:S(2)}, u32[]{:S(2)}) collective-permute-start(bf16[528,1024]{1,0:T(8,128)(2,1)} %get-tuple-element.247), channel_id=1, source_target_pairs={{0,4},{2,6},{4,0},{6,2},{8,12},{10,14},{12,8},{14,10},{16,20},{18,... | collective-permute-start | bytes 3244040 | tf_op jit(solution)/shard_map/ppermute | solution.py:759
  205.2 48.0 %collective-permute-start.17 = (bf16[528,1024]{1,0:T(8,128)(2,1)}, bf16[528,1024]{1,0:T(8,128)(2,1)}, u32[]{:S(2)}, u32[]{:S(2)}) collective-permute-start(bf16[528,1024]{1,0:T(8,128)(2,1)} %get-tuple-element.248), channel_id=1, source_target_pairs={{0,6},{2,4},{4,2},{6,0},{8,14},{10,12},{12,10},{14,8},{16,22},{18,... | collective-permute-start | bytes 3244040 | tf_op jit(solution)/shard_map/ppermute | solution.py:759
  267.6 64.3 %collective-permute-start.25 = (bf16[2,3,1024,256]{3,2,1,0:T(8,128)(2,1)}, bf16[2,3,1024,256]{3,2,1,0:T(8,128)(2,1)}, u32[]{:S(2)}, u32[]{:S(2)}) collective-permute-start(bf16[2,3,1024,256]{3,2,1,0:T(8,128)(2,1)} %get-tuple-element.282), channel_id=1, source_target_pairs={{0,1},{1,0},{2,3},{3,2},{4,5},{5,4},{6,7},{7,6},{8,9},{9,8},{10,11... | collective-permute-start | bytes 9437192 | tf_op jit(solution)/shard_map/ppermute | solution.py:765
  271.3 60.6 %collective-permute-start.24 = (bf16[3,1024,256]{2,1,0:T(8,128)(2,1)}, bf16[3,1024,256]{2,1,0:T(8,128)(2,1)}, u32[]{:S(2)}, u32[]{:S(2)}) collective-permute-start(bf16[3,1024,256]{2,1,0:T(8,128)(2,1)} %fusion.2), channel_id=1, source_target_pairs={{0,8},{2,10},{4,12},{6,14},{8,16},{10,18},{12,20},{14,22},{16,24},... | collective-permute-start | bytes 4718600 | tf_op jit(solution)/shard_map/ppermute | solution.py:762
  273.4 29.4 %collective-permute-start.23 = (bf16[512,1024]{1,0:T(8,128)(2,1)}, bf16[512,1024]{1,0:T(8,128)(2,1)S(1)}, u32[]{:S(2)}, u32[]{:S(2)}) collective-permute-start(bf16[512,1024]{1,0:T(8,128)(2,1)} %get-tuple-element.275), channel_id=1, source_target_pairs={{0,6},{2,4},{4,2},{6,0},{8,14},{10,12},{12,10},{14,8},{16,22},{18,... | collective-permute-start | bytes 3145736 | tf_op jit(solution)/shard_map/ppermute | solution.py:759
  275.5 46.5 %collective-permute-start.22 = (bf16[512,1024]{1,0:T(8,128)(2,1)}, bf16[512,1024]{1,0:T(8,128)(2,1)}, u32[]{:S(2)}, u32[]{:S(2)}) collective-permute-start(bf16[512,1024]{1,0:T(8,128)(2,1)} %get-tuple-element.273), channel_id=1, source_target_pairs={{0,4},{2,6},{4,0},{6,2},{8,12},{10,14},{12,8},{14,10},{16,20},{18,... | collective-permute-start | bytes 3145736 | tf_op jit(solution)/shard_map/ppermute | solution.py:759
  276.0 46.1 %collective-permute-start.21 = (bf16[512,1024]{1,0:T(8,128)(2,1)}, bf16[512,1024]{1,0:T(8,128)(2,1)}, u32[]{:S(2)}, u32[]{:S(2)}) collective-permute-start(bf16[512,1024]{1,0:T(8,128)(2,1)} %get-tuple-element.271), channel_id=1, source_target_pairs={{0,2},{2,0},{4,6},{6,4},{8,10},{10,8},{12,14},{14,12},{16,18},{18,... | collective-permute-start | bytes 3145736 | tf_op jit(solution)/shard_map/ppermute | solution.py:759
  328.4 26.9 %collective-permute-start.26 = (bf16[256,1152]{1,0:T(8,128)(2,1)}, bf16[256,1152]{1,0:T(8,128)(2,1)S(1)}, u32[]{:S(2)}, u32[]{:S(2)}) collective-permute-start(bf16[256,1152]{1,0:T(8,128)(2,1)} %get-tuple-element.351), channel_id=1, source_target_pairs={{0,2},{2,0},{4,6},{6,4},{8,10},{10,8},{12,14},{14,12},{16,18},{18,... | collective-permute-start | bytes 1769480 | tf_op jit(solution)/shard_map/ppermute | solution.py:759
  330.6 26.6 %collective-permute-start.28 = (bf16[256,1152]{1,0:T(8,128)(2,1)S(1)}, bf16[256,1152]{1,0:T(8,128)(2,1)S(1)}, u32[]{:S(2)}, u32[]{:S(2)}) collective-permute-start(bf16[256,1152]{1,0:T(8,128)(2,1)S(1)} %get-tuple-element.349), channel_id=1, source_target_pairs={{0,6},{2,4},{4,2},{6,0},{8,14},{10,12},{12,10},{14,8},{16,22},{18,... | collective-permute-start | bytes 1769480 | tf_op jit(solution)/shard_map/ppermute | solution.py:759
  335.6 50.0 %collective-permute-start.30 = (bf16[3,1024,256]{2,1,0:T(8,128)(2,1)}, bf16[3,1024,256]{2,1,0:T(8,128)(2,1)}, u32[]{:S(2)}, u32[]{:S(2)}) collective-permute-start(bf16[3,1024,256]{2,1,0:T(8,128)(2,1)} %fusion.1), channel_id=1, source_target_pairs={{0,8},{2,10},{4,12},{6,14},{8,16},{10,18},{12,20},{14,22},{16,24},... | collective-permute-start | bytes 4718600 | tf_op jit(solution)/shard_map/ppermute | solution.py:762
  359.4 26.2 %collective-permute-start.29 = (bf16[256,1152]{1,0:T(8,128)(2,1)S(1)}, bf16[256,1152]{1,0:T(8,128)(2,1)S(1)}, u32[]{:S(2)}, u32[]{:S(2)}) collective-permute-start(bf16[256,1152]{1,0:T(8,128)(2,1)S(1)} %add_convert_fusion.2), channel_id=1, source_target_pairs={{0,8},{2,10},{4,12},{6,14},{8,0},{10,2},{12,4},{14,6},{16,24},{18,... | collective-permute-start | bytes 1769480 | tf_op jit(solution)/shard_map/ppermute | solution.py:787
  393.2 27.2 %collective-permute-start.36 = (bf16[256,1152]{1,0:T(8,128)(2,1)S(1)}, bf16[256,1152]{1,0:T(8,128)(2,1)}, u32[]{:S(2)}, u32[]{:S(2)}) collective-permute-start(bf16[256,1152]{1,0:T(8,128)(2,1)S(1)} %add_convert_fusion.1), channel_id=1, source_target_pairs={{0,16},{2,18},{4,20},{6,22},{8,24},{10,26},{12,28},{14,30},{16,0},... | collective-permute-start | bytes 1769480 | tf_op jit(solution)/shard_map/ppermute | solution.py:787
  427.5 28.9 %collective-permute-start.39 = (bf16[256,1152]{1,0:T(8,128)(2,1)S(1)}, bf16[256,1152]{1,0:T(8,128)(2,1)S(1)}, u32[]{:S(2)}, u32[]{:S(2)}) collective-permute-start(bf16[256,1152]{1,0:T(8,128)(2,1)S(1)} %add_convert_fusion.refs_0_), channel_id=1, source_target_pairs={{0,4},{2,6},{4,0},{6,2},{8,12},{10,14},{12,8},{14,10},{16,20},{18,... | collective-permute-start | bytes 1769480 | tf_op jit(solution)/shard_map/ppermute | solution.py:759
  428.9 27.4 %collective-permute-start.40 = (bf16[256,1152]{1,0:T(8,128)(2,1)S(1)}, bf16[256,1152]{1,0:T(8,128)(2,1)S(1)}, u32[]{:S(2)}, u32[]{:S(2)}) collective-permute-start(bf16[256,1152]{1,0:T(8,128)(2,1)S(1)} %add_convert_fusion.refs_0_), channel_id=1, source_target_pairs={{0,6},{2,4},{4,2},{6,0},{8,14},{10,12},{12,10},{14,8},{16,22},{18,... | collective-permute-start | bytes 1769480 | tf_op jit(solution)/shard_map/ppermute | solution.py:759
  (55 other events, 656.8 us)

commit v3 on v2

--- a/solution.py
+++ b/solution.py
@@ -19,7 +19,7 @@
 BF = jnp.bfloat16
 VMEM_BYTES = 60 * 1024 * 1024
 COST = 0.02
-GAIN_F, GAIN_A, STATS = 64, 65, 66
+GAIN_F, GAIN_A, STATS = 32, 33, 34
 
 
 def cost(flops, bytes_accessed, transcendentals=0):
@@ -44,16 +44,21 @@
     return pl.BlockSpec(v.shape, lambda *_: (0,) * len(v.shape))
 
 
+def gate_rows(h2, routes, wr):
+    rows = h2.shape[0]
+    lane = lax.broadcasted_iota(jnp.int32, (rows, 128), 1).astype(F32)
+    picks = routes.astype(F32).T
+    mask = picks[:, 0:1] == lane
+    for k in range(1, TOPK):
+        mask = mask | (picks[:, k : k + 1] == lane)
+    sel = jnp.where(mask, dot(h2, wr[...]), -jnp.inf)
+    weight = jnp.exp(sel - jnp.max(sel, axis=1, keepdims=True))
+    return weight / jnp.sum(weight, axis=1, keepdims=True)
+
+
 def gate_table(h2, pay, wr):
     rows = h2.shape[0]
-    lane = lax.broadcasted_iota(jnp.int32, (rows, 128), 1).astype(F32)
-    routes = pay[rows : rows + 16, :rows].astype(F32).T
-    mask = routes[:, 0:1] == lane
-    for k in range(1, TOPK):
-        mask = mask | (routes[:, k : k + 1] == lane)
-    sel = jnp.where(mask, dot(h2[...], wr[...]), -jnp.inf)
-    weight = jnp.exp(sel - jnp.max(sel, axis=1, keepdims=True))
-    return weight / jnp.sum(weight, axis=1, keepdims=True)
+    return gate_rows(h2[...], pay[rows : rows + 16, :rows], wr)
 
 
 def middle_body(core, x, own, other, gain, live, mid, h2, stats):
@@ -264,84 +269,74 @@
     )(tok, *h2s, *pays, *args)
 
 
-def middle_back_body(nb, nlocal, _, *refs):
-    ids, h2, mid, gain, pay, wr = refs[:6]
-    dxs = refs[6 : 6 + nb]
-    gm, small = refs[6 + nb :]
+def middle_back_body(nb, nlocal, _, ids, h2, mid, gain, tail, wr, *refs):
+    dxs, tails = refs[:nb], refs[nb : 2 * nb]
+    *gms, small, acc = refs[2 * nb :]
     rows, width = h2.shape
+    at = pl.program_id(0)
+    cols = pl.ds(pl.multiple_of(at * rows, rows), rows)
     lane = lax.broadcasted_iota(jnp.int32, (rows, 128), 1)
-    gates = gate_table(h2, pay, wr)
+    gates = gate_rows(h2[...], tail[:, cols], wr)
     dgate = jnp.zeros((rows, 128), F32)
     for b in range(nb):
-        tail = dxs[b][rows:, :rows].astype(F32)
-        cols = (tail[:8] + tail[8:]).T
+        part = tails[b][:, cols].astype(F32)
+        part = (part[:8] + part[8:]).T
         for r in range(nlocal):
-            dgate = jnp.where(lane == ids[b * nlocal + r], cols[:, r : r + 1], dgate)
+            dgate = jnp.where(lane == ids[b * nlocal + r], part[:, r : r + 1], dgate)
     dsel = gates * (dgate - jnp.sum(gates * dgate, axis=1, keepdims=True))
     high = dsel.astype(BF)
     rest = (dsel - high.astype(F32)).astype(BF)
     router = dot_tn(h2[...], high) + dot_tn(h2[...], rest)
     dh = dot_nt(high, wr[...]) + dot_nt(rest, wr[...])
     for b in range(nb):
-        dh = dh + dxs[b][:rows, :].astype(F32)
+        dh = dh + dxs[b][...].astype(F32)
     m = mid[...]
     r2 = lax.rsqrt(jnp.mean(m * m, axis=1, keepdims=True) + NORM_EPS)
     xhat = m * r2
     col = jnp.broadcast_to(jnp.sum(dh * xhat, axis=0, keepdims=True), (8, width)).T[:, :1]
-    small[...] = jnp.where(lax.broadcasted_iota(jnp.int32, (width, 128), 1) == GAIN_F, col, router)
     su = dh * gain[...].astype(F32)
-    gm[...] = (r2 * (su - xhat * jnp.mean(su * xhat, axis=1, keepdims=True))).astype(BF)
+    grad = (r2 * (su - xhat * jnp.mean(su * xhat, axis=1, keepdims=True))).astype(BF)
+    for n, gm in enumerate(gms):
+
+        @pl.when(at == n)
+        def _(gm=gm):
+            gm[...] = grad
+
+    small_here = jnp.where(lax.broadcasted_iota(jnp.int32, (width, 128), 1) == GAIN_F, col, router)
+
+    @pl.when(at == 0)
+    def _():
+        acc[...] = small_here
+
+    @pl.when(at > 0)
+    def _():
+        acc[...] += small_here
+
+    small[...] = acc[...]
 
 
 def middle_back(tok, ids, h2, mid, gain, pay, wr, dxs, nlocal):
     rows, width = h2.shape
+    rt = rows // 2 if rows % 512 == 0 else rows
     shape = jax.ShapeDtypeStruct
-    args = (h2, mid, gain, pay, wr, *dxs)
+    block = pl.BlockSpec((rt, width), lambda i: (i, 0))
+    tail = pl.BlockSpec((16, width), lambda i: (rows // 16, 0))
+    whole = lambda v: pl.BlockSpec(v.shape, lambda i: (0, 0))
+    small = pl.BlockSpec((width, 128), lambda i: (0, 0))
     return pl.pallas_call(
         functools.partial(middle_back_body, len(dxs), nlocal),
-        in_specs=[pl.BlockSpec(memory_space=pltpu.SMEM)] * 2 + [pl.BlockSpec(memory_space=pltpu.VMEM)] * len(args),
-        out_shape=[shape((rows, width), BF), shape((width, 128), F32)],
+        grid=(rows // rt,),
+        in_specs=[pl.BlockSpec(memory_space=pltpu.SMEM)] * 2
+        + [block, block, whole(gain), tail, whole(wr)]
+        + [block] * len(dxs)
+        + [tail] * len(dxs),
+        out_specs=[pl.BlockSpec((rt, width), lambda i: (0, 0))] * (rows // rt) + [small],
+        out_shape=[shape((rt, width), BF)] * (rows // rt) + [shape((width, 128), F32)],
+        scratch_shapes=[pltpu.VMEM((width, 128), F32)],
         compiler_params=pltpu.CompilerParams(vmem_limit_bytes=VMEM_BYTES),
         cost_estimate=cost(40 * rows * width, 20 * rows * width),
         name="middle_back",
-    )(tok, ids, *args)
-
-
-def placed(core, parts, i, rt):
-    if len(parts) == 1:
-        return parts[0][i * rt : (i + 1) * rt, :].astype(F32)
-    share = parts[0].shape[0]
-    at = i * rt % share
-    mine, other = (p[at : at + rt, :].astype(F32) for p in parts)
-    return jnp.where(core[0] == i * rt // share, mine, other)
-
-
-def out_back_body(core, cot, wo, o, *refs):
-    parts, (do, gwo, da) = refs[:-3], refs[-3:]
-    rows = cot.shape[0]
-    rt = 256
-    for i in range(rows // rt):
-        rs = pl.ds(i * rt, rt)
-        d = (RESID_SCALE * (cot[rs, :].astype(F32) + placed(core, parts, i, rt))).astype(BF)
-        da[rs, :] = d
-        do[rs, :] = dot_nt(d, wo[...]).astype(BF)
-    gwo[...] = dot_tn(o[...], da[...]).astype(BF)
-
-
-def out_back(core, cot, wo, o, parts):
-    rows, width = cot.shape
-    w = wo.shape[0]
-    shape = jax.ShapeDtypeStruct
-    return pl.pallas_call(
-        out_back_body,
-        in_specs=[pl.BlockSpec(memory_space=pltpu.SMEM)]
-        + [pl.BlockSpec(memory_space=pltpu.VMEM)] * (3 + len(parts)),
-        out_shape=[shape((rows, w), BF), shape((w, width), BF)],
-        scratch_shapes=[pltpu.VMEM((rows, width), BF)],
-        compiler_params=pltpu.CompilerParams(vmem_limit_bytes=VMEM_BYTES),
-        cost_estimate=cost(4 * rows * width * w, 10 * rows * width),
-        name="attention_out_back",
-    )(core, cot, wo, o, *parts)
+    )(tok, ids, h2, mid, gain, pay, wr, *dxs, *dxs)
 
 
 def input_back_body(nq, _, wq, wkv, *refs):
@@ -377,39 +372,29 @@
     )(tok, wq, wkv, *dqs, *dkvs)
 
 
-def token_grads_body(npart, core, x, cot, own, other, gain, *refs):
-    parts, out = refs[:npart], refs[npart]
+def token_grads_body(_, x, cot, own, other, gm, gain, out):
     xb = x[...].astype(F32)
     r = lax.rsqrt(jnp.mean(xb * xb, axis=1, keepdims=True) + NORM_EPS)
     xhat = xb * r
     su = (own[...].astype(F32) + other[...].astype(F32)) * gain[...].astype(F32)
     norm = r * (su - xhat * jnp.mean(su * xhat, axis=1, keepdims=True))
-    gm = parts[0][...].astype(F32)
-    if npart == 2:
-        half = pl.num_programs(0) // 2
-        gm = jnp.where(core[0] == pl.program_id(0) // half, gm, parts[1][...].astype(F32))
-    out[...] = cot[...].astype(F32) + gm + norm
-
-
-def token_grads(core, x, cot, own, other, gain, parts):
+    out[...] = cot[...].astype(F32) + gm[...].astype(F32) + norm
+
+
+def token_grads(tok, x, cot, own, other, gm, gain):
     rows, width = x.shape
-    rt = 128
-    block = pl.BlockSpec((rt, width), lambda i, _: (i, 0))
-    n = parts[0].shape[0] // rt
-    part = pl.BlockSpec((rt, width), lambda i, _: (i % n, 0))
+    rt = 256
+    block = pl.BlockSpec((rt, width), lambda i: (i, 0))
     return pl.pallas_call(
-        functools.partial(token_grads_body, len(parts)),
-        grid_spec=pltpu.PrefetchScalarGridSpec(
-            num_scalar_prefetch=1,
-            grid=(rows // rt,),
-            in_specs=[block] * 4 + [whole_block(gain)] + [part] * len(parts),
-            out_specs=block,
-        ),
+        token_grads_body,
+        grid=(rows // rt,),
+        in_specs=[pl.BlockSpec(memory_space=pltpu.SMEM)] + [block] * 5 + [whole_block(gain)],
+        out_specs=block,
         out_shape=jax.ShapeDtypeStruct((rows, width), F32),
         compiler_params=pltpu.CompilerParams(vmem_limit_bytes=VMEM_BYTES),
         cost_estimate=cost(12 * rows * width, 14 * rows * width),
         name="token_grads",
-    )(core, x, cot, own, other, gain, *parts)
+    )(tok, x, cot, own, other, gm, gain)
 
 
 def layer_out_body(nb, _, *refs):
@@ -448,35 +433,46 @@
     )(tok, mid, live, *moes)
 
 
-def gather_rows_body(npart, cols, me, *refs):
-    parts, outs = refs[: npart * len(cols)], refs[npart * len(cols) :]
+def gather_rows_body(widths, count, turned, me, *refs):
+    parts, outs = refs[:count], refs[-len(widths) :]
     size = parts[0].shape[0]
-    at = [0] * len(outs)
-    for g, widths in enumerate(cols):
+    for k, part in enumerate(parts):
+        rows = pl.ds(pl.multiple_of((me[0] ^ k) * size, size), size)
         begin = 0
-        for j, w in enumerate(widths):
-            if not w:
-                continue
-            for k in range(npart):
-                rows = pl.ds(pl.multiple_of((me[0] ^ k) * size, size), size)
-                outs[j][rows, at[j] : at[j] + w] = parts[g * npart + k][:, begin : begin + w].astype(F32)
+        for j, (out, w) in enumerate(zip(outs, widths, strict=True)):
+            piece = part[:, begin : begin + w].astype(F32)
+            if turned and j == len(widths) - 1:
+                out[:, rows] = piece.T
+            else:
+                out[rows, :] = piece
             begin += w
-            at[j] += w
-
-
-def gather_rows(me, groups, cols):
-    npart = len(groups[0])
-    size = groups[0][0].shape[0]
-    flat = [v for group in groups for v in group]
-    widths = [sum(c[j] for c in cols) for j in range(len(cols[0]))]
+
+
+def gather_rows(me, parts, widths, groups, turned, earlier=()):
+    npart = len(parts)
+    rows = npart * parts[0].shape[0]
+    group = 1 if earlier else 0
+    last = len(widths) - 1
+    block = lambda j, w: (w, rows) if turned and j == last else (rows, w)
+    shape = lambda j, w: (rows, w * groups) if j < 2 else block(j, w)
     return pl.pallas_call(
-        functools.partial(gather_rows_body, npart, cols),
-        in_specs=[pl.BlockSpec(memory_space=pltpu.SMEM)] + [pl.BlockSpec(memory_space=pltpu.VMEM)] * len(flat),
-        out_shape=[jax.ShapeDtypeStruct((npart * size, w), F32) for w in widths],
+        functools.partial(gather_rows_body, widths, npart, turned),
+        grid=(1,),
+        in_specs=[pl.BlockSpec(memory_space=pltpu.SMEM)]
+        + [whole_block(v) for v in parts]
+        + [pl.BlockSpec(memory_space=pl.ANY)] * len(earlier),
+        out_specs=[
+            pl.BlockSpec(block(j, w), (lambda _: (0, group)) if j < 2 else (lambda _: (0, 0)))
+            for j, w in enumerate(widths)
+        ],
+        out_shape=[jax.ShapeDtypeStruct(shape(j, w), F32) for j, w in enumerate(widths)],
+        input_output_aliases={1 + npart + j: j for j in range(len(earlier))},
         compiler_params=pltpu.CompilerParams(vmem_limit_bytes=VMEM_BYTES),
-        cost_estimate=cost(0, 6 * npart * size * sum(widths)),
+        cost_estimate=cost(0, 6 * rows * sum(widths)),
         name="gather_rows",
-    )(me, *flat)
+    )(me, *parts, *earlier)
+
+
 HD = 64
 NEG = -1e30
 BLK = 256
@@ -631,17 +627,44 @@
     )(core, lengths, x, gain, wq, wkv, wo, valid)
 
 
-def attn_backward_body(first, folded, _, lengths, q, kd, vd, do, lse, h1, cos, sin, valid, wq, wkv, gain, *rest):
-    extras, (dq, dkv, gw, dk, dv) = rest[:-5], rest[-5:]
-    if folded:
-        extras, gwo = extras[:-1], extras[-1]
-        depth = gwo.shape[0]
-        for n in range(gwo.shape[1] // depth):
-            rs = slice(n * depth, (n + 1) * depth)
-            gw[rs, 2 * q.shape[1] + 128 :] = gwo[:, rs]
+def attn_backward_body(first, npart, nmore, npiece, places, core, at, lengths, q, kd, vd, lse, cos, sin, valid, gain, *refs):
+    it = iter(refs)
+    take = lambda n: [next(it) for _ in range(n)]
+    h1_hbm, wq_hbm, wkv_hbm = take(3)
+    more = take(nmore)
+    if places:
+        cot, wo, o_hbm, *parts = take(3 + npart)
+    else:
+        (do,) = take(1)
+    dq, dkv, sums = take(3)
+    pieces = take(npiece)
+    if places:
+        do, gm = take(2)
+    dk, dv, gw, h1, wq, wkv, sem = take(7)
+    if places:
+        da, o = take(2)
+    wid = q.shape[1]
+    width = h1.shape[1]
+    cols = pl.ds(first * 128, wid)
+    copies = [
+        pltpu.make_async_copy(h1_hbm, h1, sem.at[0]),
+        pltpu.make_async_copy(wq_hbm.at[:, cols], wq, sem.at[1]),
+        pltpu.make_async_copy(wkv_hbm.at[:, cols], wkv, sem.at[2]),
+    ]
+    if places:
+        copies.append(pltpu.make_async_copy(o_hbm, o, sem.at[3]))
+    for copy in copies:
+        copy.start()
+    if places:
+        for i in range(q.shape[0] // BLK):
+            rs = pl.ds(i * BLK, BLK)
+            g = placed(core, parts, i)
+            gm[rs, :] = g.astype(BF)
+            d = (RESID_SCALE * (cot[rs, :].astype(F32) + g)).astype(BF)
+            da[rs, :] = d
+            do[rs, :] = dot_nt(d, wo[...]).astype(BF)
     nkv = kd.shape[1] // 128
     wid = q.shape[1]
-    width = h1.shape[1]
     lane = lax.broadcasted_iota(jnp.int32, (BLK, 128), 1)
     low = lane < HD
     dk[...] = jnp.zeros_like(dk)
@@ -682,51 +705,85 @@
             vv = dv[rs, ns]
             vv = vv + pltpu.roll(vv, HD, 1)
             dkv[rs, ns] = jnp.where(low, kk * cb - swap_halves(kk, lane) * sb, vv).astype(BF)
+    for copy in copies:
+        copy.wait()
     gq = dot_tn(h1[...], dq[...])
     gk = dot_tn(h1[...], dkv[...])
     gw[:, :wid] = gq.astype(BF)
     gw[:, wid : 2 * wid] = gk.astype(BF)
     ga = jnp.sum(gq * wq[...].astype(F32) + gk * wkv[...].astype(F32), axis=1, keepdims=True) / gain[...].astype(F32)
     lanes = lax.broadcasted_iota(jnp.int32, (width, 128), 1)
-    if extras:
-        small, s1, s2 = extras
-        stats = (s1[...] + s2[...]).T[:, :1]
-        stats = jnp.concatenate([stats, jnp.zeros((width - 128, 1), F32)], axis=0)
-        rest_cols = jnp.where(lanes == STATS, stats, small[...])
+    ga = jnp.where(lanes == GAIN_A, ga, 0.0)
+    for v in more:
+        ga = ga + v[...]
+    sums[...] = ga
+    if places:
+        gwo = dot_tn(o[...], da[...]).astype(BF)
+        depth = gwo.shape[0]
+        for n in range(width // depth):
+            rs = slice(n * depth, (n + 1) * depth)
+            gw[rs, 2 * wid : 2 * wid + depth] = gwo[:, rs]
     else:
-        rest_cols = jnp.zeros((width, 128), F32)
-    gw[:, 2 * wid : 2 * wid + 128] = jnp.where(lanes == GAIN_A, ga, rest_cols).astype(BF)
-
-
-def attn_backward(first, count, tok, lengths, q, kd, vd, do, lse, h1, cos, sin, valid, wq, wkv, gain, extras=(), gwo=None):
+        gw[:, 2 * wid :] = ga.astype(BF)
+    size = width // len(pieces)
+    for k, piece in enumerate(pieces):
+        piece[...] = gw[pl.ds(pl.multiple_of((at[0] ^ k) * size, size), size), :]
+
+
+def placed(core, parts, i):
+    if len(parts) == 1:
+        return parts[0][i * BLK : (i + 1) * BLK, :].astype(F32)
+    n = len(parts) // 2
+    mine, other = parts[i % n][...].astype(F32), parts[n + i % n][...].astype(F32)
+    return jnp.where(core[0] == i // n, mine, other)
+
+
+def attn_backward(first, count, core, at, npiece, lengths, q, kd, vd, lse, h1, cos, sin, valid, wq, wkv, gain, sums, do=None, given=None):
     rows, width = h1.shape
     w = count * 128
-    cols = 2 * w + 128 + (0 if gwo is None else gwo.shape[0])
-    folded = gwo is not None
-    if folded:
-        extras = (*extras, gwo)
+    depth = given[1].shape[0] if given else 128
+    cols = 2 * w + depth
     shape = jax.ShapeDtypeStruct
     part = pl.BlockSpec((rows, w), lambda _: (0, first // count))
-    wpart = pl.BlockSpec((width, w), lambda _: (0, first // count))
+    full = lambda *s: pl.BlockSpec(s, lambda _: (0, 0))
+    there = pl.BlockSpec(memory_space=pl.ANY)
+    size = width // npiece
+    outs = [(rows, w)] * 2 + [(width, 128)] + [(size, cols)] * npiece
+    types = [BF, BF, F32] + [BF] * npiece
+    scratch = [
+        pltpu.VMEM((rows, w), F32),
+        pltpu.VMEM((rows, w), F32),
+        pltpu.VMEM((width, cols), BF),
+        pltpu.VMEM((rows, width), BF),
+        pltpu.VMEM((width, w), BF),
+        pltpu.VMEM((width, w), BF),
+        pltpu.SemaphoreType.DMA((4,)),
+    ]
+    if given:
+        cot, wo, o, *parts = given
+        last = [cot, wo, o, *parts]
+        last_specs = [whole_block(cot), whole_block(wo), there] + [whole_block(v) for v in parts]
+        outs += [(rows, depth), (rows, width)]
+        types += [BF, BF]
+        scratch += [pltpu.VMEM((rows, width), BF), pltpu.VMEM((rows, depth), BF)]
+    else:
+        parts, last, last_specs = (), [do], [part]
     return pl.pallas_call(
-        functools.partial(attn_backward_body, first, folded),
+        functools.partial(attn_backward_body, first, len(parts), len(sums), npiece, bool(given)),
         grid=(1,),
-        in_specs=[pl.BlockSpec(memory_space=pltpu.SMEM)] * 2
-        + [part] * 4
-        + [whole_block(v) for v in (lse, h1, cos, sin, valid)]
-        + [wpart] * 2
-        + [whole_block(v) for v in (gain, *extras)],
-        out_specs=[
-            pl.BlockSpec((rows, w), lambda _: (0, 0)),
-            pl.BlockSpec((rows, w), lambda _: (0, 0)),
-            pl.BlockSpec((width, cols), lambda _: (0, 0)),
-        ],
-        out_shape=[shape((rows, w), BF), shape((rows, w), BF), shape((width, cols), BF)],
-        scratch_shapes=[pltpu.VMEM((rows, w), F32), pltpu.VMEM((rows, w), F32)],
+        in_specs=[pl.BlockSpec(memory_space=pltpu.SMEM)] * 3
+        + [part] * 3
+        + [whole_block(v) for v in (lse, cos, sin, valid, gain)]
+        + [there] * 3
+        + [whole_block(v) for v in sums]
+        + last_specs,
+        out_specs=[full(*s) for s in outs],
+        out_shape=[shape(s, d) for s, d in zip(outs, types, strict=True)],
+        scratch_shapes=scratch,
         compiler_params=pltpu.CompilerParams(vmem_limit_bytes=VMEM_BYTES),
         cost_estimate=cost(4 * rows * width * w + 20 * rows * rows * w, 10 * rows * width),
         name="attention_backward",
-    )(tok, lengths, q, kd, vd, do, lse, h1, cos, sin, valid, wq, wkv, gain, *extras)
+    )(core, at, lengths, q, kd, vd, lse, cos, sin, valid, gain, h1, wq, wkv, *sums, *last)
 
 
 def on_device(
@@ -773,10 +830,12 @@
             acc = acc + term.astype(F32)
         return acc
 
-    def scatter_plane(v):
+    def scatter_plane(pieces):
+        return [pieces[0]] + [across(pieces[k], k) for k in range(1, inner)]
+
+    def cut_rows(v, k):
         size = v.shape[0] // inner
-        cut = lambda k: lax.dynamic_slice_in_dim(v, (me_in ^ k) * size, size)
-        return [cut(0)] + [across(cut(k), k) for k in range(1, inner)]
+        return lax.dynamic_slice_in_dim(v, (me_in ^ k) * size, size)
 
     def summed(terms):
         return total(terms).astype(BF)
@@ -898,21 +957,22 @@
         next_held()
     work([0], 0, near)
     finish(*h2s)
-    for b in close[1:]:
-        work([b], 0, near)
-        if b == 1:
-            if outer > 2:
-                finish(held[-1])
-                next_held()
-            for k in far:
-                pays.append(across(release(pay), k))
-                h2s.append(across(release(h2), k))
+    for k in far:
+        pays.append(across(release(pay), k))
+    if close[1:]:
+        work(close[1:], 0, near)
+    if outer > 2:
+        finish(held[-1])
+        next_held()
+    finish(*pays)
+    for k in far:
+        h2s.append(across(release(h2), k))
     for r in range(near, last):
         work(close, r, 1)
         if r + 1 < last:
             finish(held[-1])
             next_held()
-    finish(*h2s, *pays)
+    finish(*h2s)
     for b in far:
         work([b], 0, max(last, near))
     if last >= near:
@@ -937,6 +997,7 @@
     raws = [expert_grads(rs) for rs in later]
     finish(*dxs, *([ring] if outer > 1 else []))
     moes = [state[0][1]] + [across(release(state[k][1]), k) for k in range(1, inner)]
+    early = [swap(release(raw[1])) if pair and rs == [2] else None for rs, raw in zip(later, raws, strict=True)]
 
     def ring_step(r):
         nonlocal ring
@@ -947,43 +1008,39 @@
         finish(ring)
         ring = along(ring, 1)
 
-    gm_share, small = middle_back(tok, ids_all, h2, mid, gain_f, pay, wr, dxs, outer)
-    gm = [gm_share, swap(gm_share)] if pair else [lax.all_gather(gm_share, "tp", axis=0, tiled=True)]
-    finish(gm_share)
-    for rs, raw in zip(later, raws, strict=True):
-        if pair:
-            other = swap(release(raw[1]))
+    *gm, small = middle_back(tok, ids_all, h2, mid, gain_f, pay, wr, dxs, outer)
+    finish(small)
+    if pair:
+        gm = [*gm, *[swap(v) for v in gm]]
+    else:
+        gm = [lax.all_gather(jnp.concatenate(gm), "tp", axis=0, tiled=True)]
+    for rs, raw, other in zip(later, raws, early, strict=True):
+        if not pair:
+            parts.update({r: own_hidden([raw[0][n]]) for n, r in enumerate(rs)})
+        else:
+            other = release(other) if other is not None else swap(release(raw[1]))
             parts.update({r: raw[0][n].astype(F32) + other[n].astype(F32) for n, r in enumerate(rs)})
-            if rs == [2]:
-                finish(other)
-        else:
-            parts.update({r: own_hidden([raw[0][n]]) for n, r in enumerate(rs)})
     if outer > 2:
         ring_step(2)
-    do, gwo = out_back(tok, cotangent, w_out, o, gm)
-    finish(do)
-
     nkv = kd.shape[1] // 128
     groups = 2 if nkv % 2 == 0 else 1
     each = nkv // groups
-    dqs, dkvs, terms = [], [], []
+    w = each * 128
+    depth = w_out.shape[0]
+    dqs, dkvs, sums = [], [], small
+    at = me_in[None]
     for n in range(groups):
-        if n == groups - 1:
-            finish(*moes)
-            out_share, stats_out = layer_out_share(tok, mid, live, moes)
-            finish(out_share)
-            if outer > 3:
-                finish(ring)
-                ring_step(3)
-        dq, dkv, gw = attn_backward(
+        first_one = n == 0
+        out = attn_backward(
             n * each,
             each,
             tok,
+            at,
+            inner,
             doc_lengths,
             q,
             kd,
             vd,
-            do,
             lse,
             h1,
             cos,
@@ -992,36 +1049,62 @@
             query_weight_matrix,
             key_value_weight,
             gain_attn[:, None],
-            (small, stats, stats_out) if n == groups - 1 else (),
-            gwo if n == 0 else None,
+            [sums],
+            None if first_one else do,
+            (cotangent, w_out, o, *gm) if first_one else None,
         )
-        finish(gw)
+        dq, dkv, sums, *pieces = out[: 3 + inner]
+        if first_one:
+            do, gm_all = out[3 + inner :]
+        finish(pieces[0])
         dqs.append(dq)
         dkvs.append(dkv)
-        if n == 0:
-            terms.append(scatter_plane(gw))
-    finish(*terms[0])
-    ahead = column_steps(summed([release(t) for t in terms[0]]))
-    moving = next(ahead)
+        if first_one and groups > 1:
+            terms = scatter_plane(pieces)
+            if outer > 3:
+                finish(ring)
+                ring_step(3)
+    if groups == 1:
+        sums_only = [cut_rows(sums.astype(BF), k) for k in range(inner)]
+        terms = scatter_plane([jnp.concatenate(v, axis=1) for v in zip(pieces, sums_only, strict=True)])
+    finish(*moes)
+    out_share, stats_out = layer_out_share(tok, mid, live, moes)
+    finish(out_share)
+    spread = jnp.pad((stats + stats_out)[:1, :4], ((0, 0), (STATS, 128 - STATS - 4)))
+
+    def closing_sum(terms):
+        v = total([release(t) for t in terms])
+        row = lax.broadcasted_iota(jnp.int32, v.shape, 0)
+        lane = lax.broadcasted_iota(jnp.int32, v.shape, 1) - (v.shape[1] - 128)
+        place = (row == 0) & (lane >= STATS) & (lane < STATS + 4)
+        return jnp.where(place, jnp.pad(spread, ((0, 0), (v.shape[1] - 128, 0))), v).astype(BF)
+
+    def spread_plane(v):
+        return [v] + [across(v, k) for k in range(1, inner)]
+
     if groups > 1:
-        terms.append(scatter_plane(release(gw)))
+        finish(*terms)
+        ahead = column_steps(summed([release(t) for t in terms]))
+        moving = next(ahead)
+        terms = scatter_plane([release(v) for v in pieces])
     dh1 = input_back(tok, query_weight_matrix, key_value_weight, dqs, dkvs)
-    finish(dh1, moving, *([ring] if outer > 1 else []))
+    finish(dh1, *([ring] if outer > 1 else []), *([moving] if groups > 1 else []))
+    if groups > 1:
+        moving = next(ahead)
     if pair:
         dh_other = swap(release(dh1))
-        out_other = swap(release(out_share))
     else:
         dh1, dh_other = lax.psum(dh1.astype(F32), "tp"), jnp.zeros_like(dh1)
+    finish(dh_other)
+    grad_tokens = token_grads(tok, tokens, cotangent, dh1, dh_other, gm_all, gain_a)
+    finish(grad_tokens, *terms)
+    if pair:
+        out_other = swap(out_share)
+    closing = closing_sum(terms)
     if groups > 1:
-        moving = next(ahead)
-    finish(dh_other)
-    grad_tokens = token_grads(tok, tokens, cotangent, dh1, dh_other, gain_a, gm)
-    finish(grad_tokens)
-    gws = []
-    if groups > 1:
-        finish(*terms[1])
-        behind = column_steps(summed([release(t) for t in terms[1]]))
-        late = next(behind)
+        finish(moving)
+    behind = column_steps(release(closing))
+    late = next(behind)
     if pair:
         layer_out = jnp.where(
             core[0] == 0,
@@ -1031,37 +1114,38 @@
         finish(layer_out)
     else:
         layer_out = lax.all_gather(out_share, "tp", axis=0, tiled=True)
-    finish(moving)
-    for v in ahead:
-        whole = v
-    gws.append([whole] + [across(release(whole), k) for k in range(1, inner)])
-    if groups > 1:
-        finish(late)
-        for v in behind:
-            late = v
-        gws.append([late] + [across(release(late), k) for k in range(1, inner)])
     for r in range(4, outer):
         ring_step(r)
-    sums = ring_step(0) if outer > 1 else parts[0]
-    gu_grad, down_grad = unpacked(sums)
-    w = each * 128
-    depth = w_out.shape[0]
-    grad_w_query, grad_w_kv, extras, folded = gather_rows(
-        release(me_in[None]), gws, [(w, w, 128, depth if n == 0 else 0) for n in range(groups)]
-    )
+    expert_sums = ring_step(0) if outer > 1 else parts[0]
+    gu_grad, down_grad = unpacked(expert_sums)
+    spreads = []
+    if groups > 1:
+        for whole in ahead:
+            pass
+        spreads.append(spread_plane(release(whole)))
+    finish(late)
+    for whole in behind:
+        pass
+    spreads.append(spread_plane(release(whole)))
+    if groups > 1:
+        *grads, folded = gather_rows(at, spreads[0], (w, w, depth), groups, False)
+        finish(folded)
+        grad_w_query, grad_w_kv, extras = gather_rows(release(at), spreads[1], (w, w, 128), groups, True, grads)
+    else:
+        grad_w_query, grad_w_kv, folded, extras = gather_rows(release(at), spreads[0], (w, w, depth, 128), 1, True)
     grad_w_out = jnp.concatenate([folded[n * depth : (n + 1) * depth] for n in range(width // depth)], axis=1)
-    extras = sum(extras[:, n * 128 : (n + 1) * 128] for n in range(groups))
+    extras = extras[: STATS + 6]
     extras = extras + swap(extras) if pair else lax.psum(extras, "tp")
-    s = extras[:4, STATS]
+    s = jnp.sum(extras[STATS : STATS + 4, :: width // inner], axis=1)
     return (
         layer_out,
         grad_tokens,
-        extras[:, GAIN_A],
+        extras[GAIN_A],
         grad_w_query,
         grad_w_kv,
         grad_w_out,
-        extras[:, GAIN_F],
-        extras[:, :nexp],
+        extras[GAIN_F],
+        extras[:nexp].T,
         gu_grad[None],
         down_grad[None],
         jnp.sqrt(s[:3] / (s[3] * width)),

time: 496 us -> 441 us (0.89)
  waiting for transfers between devices: 113 us -> 67 us
  local copies, waits for them, and re-layouts: 24.3 us -> 18.6 us
  Pallas kernels: 278 us -> 273 us
    ppermute x24, waiting for transfers between devices: 59.7 us -> 29 us  [across(): return lax.ppermute(v, 'ep', [(i, i ^ k) for i in range(n_ep)])]
    ppermute x4, waiting for transfers between devices: 45.2 us -> 24.9 us  [column_steps(): other = lax.ppermute(v, 'ep', [(i, i ^ bit * inner) for i in range(n_ep)])]
    ppermute x6, waiting for transfers between devices: 0.04 us -> 7.45 us  [along(): lax.ppermute(v, 'ep', [(i, (i + k * inner) % n_ep) for i in range(n_ep)])]
    unnamed x68 -> x61, local copies, waits for them, and re-layouts: 10.4 us -> 5.44 us
    pallas_call x7 -> x6, Pallas kernels: 117 us -> 113 us  [experts(): pl.pallas_call(functools.partial(experts_body, nb, nchunk, halves, first,...]
  transfers between devices with their start and end apart: 46 -> 47, of which waited for: 17 -> 16; matrix products, arithmetic and copies ran while one was open for 8% -> 9% of each run, Pallas kernels for 50% -> 58%
where the time goes in v3:
time: 441 us; the launch traced here: 435 us
  Pallas kernels  273 us (62%)
  waiting for transfers between devices  67 us (15%)
  starting transfers between devices  44.7 us (10%)
  other arithmetic  29.4 us (7%)
  local copies, waits for them, and re-layouts  18.6 us (4%)
    pallas_call x6, Pallas kernels, experts(): pl.pallas_call(functools.partial(experts_body, nb, nchunk, halves, first,...  113 us
    pallas_call x3, Pallas kernels, weight_grads(): pl.pallas_call(functools.partial(weight_grads_body, nb, halves), grid=(ne...  50 us
    pallas_call x2, Pallas kernels, attn_backward(): pl.pallas_call(functools.partial(attn_backward_body, first, len(parts), l...  41.6 us
    ppermute x24, starting transfers between devices, across(): return lax.ppermute(v, 'ep', [(i, i ^ k) for i in range(n_ep)])  30.4 us
    ppermute x24, waiting for transfers between devices, across(): return lax.ppermute(v, 'ep', [(i, i ^ k) for i in range(n_ep)])  29 us
    pallas_call x1, Pallas kernels, attn_forward(): pl.pallas_call(attn_forward_body, in_specs=[pl.BlockSpec(memory_space=plt...  25.8 us
    ppermute x4, waiting for transfers between devices, column_steps(): other = lax.ppermute(v, 'ep', [(i, i ^ bit * inner) for i in range(n_ep)])  24.9 us
    pallas_call x1, Pallas kernels, middle_back(): pl.pallas_call(functools.partial(middle_back_body, len(dxs), nlocal), gri...  9.53 us
  transfers between devices with their start and end apart: 47, of which 16 were waited for; matrix products, arithmetic and copies ran while one was open for 9% of the time, Pallas kernels for 58%

profile of v3, /device:TPU:0, one launch (start us, length us, event | category | flops | bytes accessed | tf_op | source)
XLA Modules:
  0.0 434.8 jit_solution(15518251622953483338)
XLA Ops:
  10.6 25.8 %attention_forward.1 = (bf16[1024,1024]{1,0:T(8,128)(2,1)}, bf16[1024,512]{1,0:T(8,128)(2,1)}, bf16[1024,512]{1,0:T(8,128)(2,1)}, bf16[1024,512]{1,0:T(8,128)(2,...) custom-call(s32[1]{0:T(128)} %bitcast.core._, ...), custom_call_target="tpu_custom_call" | custom-call | flops 236223200 | bytes 251658 | tf_op jit(solution)/shard_map/attention_forward/pallas_call | solution.py:610
  49.2 13.6 %experts.6 = (bf16[528,1024]{1,0:T(8,128)(2,1)}, bf16[512,1024]{1,0:T(8,128)(2,1)}, bf16[4,256,512]{2,1,0:T(8,128)(2,1)}, bf16[4,512,512]{2,1,0:T(8,128)(2,1)}) custom-call(s32[4]{0:T(128)} %and_select_fusion.3.refs_0_, bf16[512,1024]{1,0:T(8,128)(2,1)} %get-tuple-element.204.refs_1_.refs_0_.h2, bf16[528,1024]{1,0:T(8,128)(2,1)} %get-tuple-element.194.refs_2_.refs_4_.tail, ...), custom_call_target="tpu_custom_call" | custom-call | flops 128849016 | bytes 251658 | tf_op jit(solution)/shard_map/experts/pallas_call | solution.py:187
  62.8 7.6 %collective-permute-done.6.refs_1_.refs_2_ = bf16[512,1024]{1,0:T(8,128)(2,1)S(1)} collective-permute-done((bf16[512,1024]{1,0:T(8,128)(2,1)}, bf16[512,1024]{1,0:T(8,128)(2,1)S(1)}, u32[]{:S(2)}, u32[]{:S(2)}) %collective-permute-start.6) | collective-permute-done | bytes 1048608 | tf_op jit(solution)/shard_map/ppermute | solution.py:816
  73.0 23.9 %experts.7 = (bf16[528,1024]{1,0:T(8,128)(2,1)}, bf16[512,1024]{1,0:T(8,128)(2,1)}, bf16[4,256,512]{2,1,0:T(8,128)(2,1)}, bf16[4,512,512]{2,1,0:T(8,128)(2,1)}, ...) custom-call(s32[4]{0:T(128)} %and_select_fusion.3.refs_0_, ...), custom_call_target="tpu_custom_call" | custom-call | flops 257698032 | bytes 377487 | tf_op jit(solution)/shard_map/experts/pallas_call | solution.py:187
  100.7 24.1 %experts.8 = (bf16[528,1024]{1,0:T(8,128)(2,1)}, bf16[512,1024]{1,0:T(8,128)(2,1)}, bf16[2,256,512]{2,1,0:T(8,128)(2,1)}, bf16[2,512,512]{2,1,0:T(8,128)(2,1)}, ...) custom-call(s32[4]{0:T(128)} %and_select_fusion.3.refs_0_, ...), custom_call_target="tpu_custom_call" | custom-call | flops 193273536 | bytes 440401 | tf_op jit(solution)/shard_map/experts/pallas_call | solution.py:187
  125.8 17.5 %experts.9 = (bf16[528,1024]{1,0:T(8,128)(2,1)}, bf16[512,1024]{1,0:T(8,128)(2,1)}, bf16[6,256,512]{2,1,0:T(8,128)(2,1)}, bf16[6,512,512]{2,1,0:T(8,128)(2,1)}) custom-call(s32[4]{0:T(128)} %and_select_fusion.3.refs_0_, bf16[512,1024]{1,0:T(8,128)(2,1)} %copy-done.5, bf16[528,1024]{1,0:T(8,128)(2,1)} %collective-permute-done.9.refs_2_.refs_7_.refs_6_, ...), custom_call_target="tpu_custom_call" | custom-call | flops 193273536 | bytes 314572 | tf_op jit(solution)/shard_map/experts/pallas_call | solution.py:187
  143.3 14.2 %expert_weight_grads.3 = (bf16[1,3,1024,256]{3,2,1,0:T(8,128)(2,1)}, bf16[1,3,1024,256]{3,2,1,0:T(8,128)(2,1)}) custom-call(s32[1]{0:T(128)} %bitcast.core._, bf16[512,1024]{1,0:T(8,128)(2,1)} %get-tuple-element.204.refs_1_.refs_0_.h2, bf16[512,1024]{1,0:T(8,128)(2,1)} %copy-done.4, bf16[512,1024]{1,0:T(8,128)(2,1)} %collective-permute-done.7.refs_2_.refs_3_, ...), custom_call_target="tpu_custom_call" | custom-call | flops 128849016 | bytes 230686 | tf_op jit(solution)/shard_map/expert_weight_grads/pallas_call | solution.py:260
  166.2 23.7 %experts.10 = (bf16[528,1024]{1,0:T(8,128)(2,1)}, bf16[512,1024]{1,0:T(8,128)(2,1)}, bf16[2,256,512]{2,1,0:T(8,128)(2,1)}, bf16[2,512,512]{2,1,0:T(8,128)(2,1)},...) custom-call(s32[4]{0:T(128)} %and_select_fusion.3.refs_0_, ...), custom_call_target="tpu_custom_call" | custom-call | flops 193273536 | bytes 440401 | tf_op jit(solution)/shard_map/experts/pallas_call | solution.py:187
  193.4 10.3 %experts.11 = (bf16[528,1024]{1,0:T(8,128)(2,1)}, bf16[512,1024]{1,0:T(8,128)(2,1)}, bf16[2,256,512]{2,1,0:T(8,128)(2,1)}, bf16[2,512,512]{2,1,0:T(8,128)(2,1)}) custom-call(s32[4]{0:T(128)} %and_select_fusion.3.refs_0_, bf16[512,1024]{1,0:T(8,128)(2,1)} %get-tuple-element.204.refs_1_.refs_0_.h2, bf16[528,1024]{1,0:T(8,128)(2,1)} %get-tuple-element.194.refs_2_.refs_4_.tail, ...), custom_call_target="tpu_custom_call" | custom-call | flops 64424508 | bytes 188743 | tf_op jit(solution)/shard_map/experts/pallas_call | solution.py:187
  203.7 13.8 %expert_weight_grads.4 = (bf16[1,3,1024,256]{3,2,1,0:T(8,128)(2,1)}, bf16[1,3,1024,256]{3,2,1,0:T(8,128)(2,1)}) custom-call(s32[1]{0:T(128)} %bitcast.core._, bf16[512,1024]{1,0:T(8,128)(2,1)} %get-tuple-element.204.refs_1_.refs_0_.h2, bf16[512,1024]{1,0:T(8,128)(2,1)} %copy-done.4, bf16[512,1024]{1,0:T(8,128)(2,1)} %collective-permute-done.7.refs_2_.refs_3_, ...), custom_call_target="tpu_custom_call" | custom-call | flops 128849016 | bytes 230686 | tf_op jit(solution)/shard_map/expert_weight_grads/pallas_call | solution.py:260
  217.6 22.0 %expert_weight_grads.5 = (bf16[2,3,1024,256]{3,2,1,0:T(8,128)(2,1)}, bf16[2,3,1024,256]{3,2,1,0:T(8,128)(2,1)}) custom-call(s32[1]{0:T(128)} %bitcast.core._, bf16[512,1024]{1,0:T(8,128)(2,1)} %get-tuple-element.204.refs_1_.refs_0_.h2, bf16[512,1024]{1,0:T(8,128)(2,1)} %copy-done.4, bf16[512,1024]{1,0:T(8,128)(2,1)} %collective-permute-done.7.refs_2_.refs_3_, ...), custom_call_target="tpu_custom_call" | custom-call | flops 128849016 | bytes 230686 | tf_op jit(solution)/shard_map/expert_weight_grads/pallas_call | solution.py:260
  241.3 9.5 %middle_back.1 = (bf16[256,1024]{1,0:T(8,128)(2,1)}, bf16[256,1024]{1,0:T(8,128)(2,1)}, f32[1024,128]{1,0:T(8,128)}) custom-call(s32[1]{0:T(128)} %bitcast.core._, s32[16]{0:T(128)} %pad_add_fusion.ids, bf16[512,1024]{1,0:T(8,128)(2,1)} %get-tuple-element.204.refs_1_.refs_0_.h2, f32[512,1024]{1,0:T(8,128)} %get-tuple-element.258.mid.refs_0_, ...), custom_call_target="tpu_custom_call" | custom-call | flops 419430 | bytes 209715 | tf_op jit(solution)/shard_map/middle_back/pallas_call | solution.py:326
  263.0 23.9 %attention_backward.2 = (bf16[1024,256]{1,0:T(8,128)(2,1)}, bf16[1024,256]{1,0:T(8,128)(2,1)}, f32[1024,128]{1,0:T(8,128)}, bf16[256,1024]{1,0:T(8,128)(2,1)}, b...) custom-call(s32[1]{0:T(128)} %bitcast.core._, ...), custom_call_target="tpu_custom_call" | custom-call | flops 128849016 | bytes 209715 | tf_op jit(solution)/shard_map/attention_backward/pallas_call | solution.py:771
  286.9 7.4 %collective-permute-done.22 = bf16[3,1024,256]{2,1,0:T(8,128)(2,1)} collective-permute-done((bf16[3,1024,256]{2,1,0:T(8,128)(2,1)}, bf16[3,1024,256]{2,1,0:T(8,128)(2,1)}, u32[]{:S(2)}, u32[]{:S(2)}) %collective-permute-start.22) | collective-permute-done | bytes 1572896 | tf_op jit(solution)/shard_map/ppermute | solution.py:819
  300.2 6.3 %collective-permute-done.25.refs_4_ = bf16[512,1024]{1,0:T(8,128)(2,1)} collective-permute-done((bf16[512,1024]{1,0:T(8,128)(2,1)}, bf16[512,1024]{1,0:T(8,128)(2,1)}, u32[]{:S(2)}, u32[]{:S(2)}) %collective-permute-start.25) | collective-permute-done | bytes 1048608 | tf_op jit(solution)/shard_map/ppermute | solution.py:816
  309.2 17.8 %attention_backward.3 = (bf16[1024,256]{1,0:T(8,128)(2,1)}, bf16[1024,256]{1,0:T(8,128)(2,1)}, f32[1024,128]{1,0:T(8,128)}, bf16[256,640]{1,0:T(8,128)(2,1)}, bf...) custom-call(s32[1]{0:T(128)} %bitcast.core._, s32[1]{0:T(128)} %bitcast.7.at.me, ...), custom_call_target="tpu_custom_call" | custom-call | flops 128849016 | bytes 209715 | tf_op jit(solution)/shard_map/attention_backward/pallas_call | solution.py:771
  326.9 5.2 %layer_out.1 = (bf16[512,1024]{1,0:T(8,128)(2,1)}, f32[8,128]{1,0:T(8,128)}) custom-call(s32[1]{0:T(128)} %bitcast.core._, f32[512,1024]{1,0:T(8,128)} %get-tuple-element.258.mid.refs_0_, f32[512,1]{1,0:T(8,128)} %copy.32.refs_1_, bf16[512,1024]{1,0:T(8,128)(2,1)} %get-tuple-element.233.refs_2_, bf16[512,1024]{1,0:T(8,128)(2,1)} %collective-permute-done.24.refs_3_, ...), custom_call_target="tpu_custom_call" | custom-call | flops 125829 | bytes 146800 | tf_op jit(solution)/shard_map/layer_out/pallas_call | solution.py:424
  334.8 6.2 %input_back.1.own = bf16[1024,1024]{1,0:T(8,128)(2,1)} custom-call(s32[1]{0:T(128)} %bitcast.core._, bf16[1024,512]{1,0:T(8,128)(2,1)} %wq.3, bf16[1024,512]{1,0:T(8,128)(2,1)} %wkv.3, bf16[1024,256]{1,0:T(8,128)(2,1)} %get-tuple-element.299.refs_0_, bf16[1024,256]{1,0:T(8,128)(2,1)} %get-tuple-element.300.refs_1_, ...), custom_call_target="tpu_custom_call" | custom-call | flops 42949672 | bytes 209715 | tf_op jit(solution)/shard_map/input_back/pallas_call | solution.py:363
  341.0 6.6 %collective-permute-done.31 = bf16[256,1024]{1,0:T(8,128)(2,1)} collective-permute-done((bf16[256,1024]{1,0:T(8,128)(2,1)S(1)}, bf16[256,1024]{1,0:T(8,128)(2,1)}, u32[]{:S(2)}, u32[]{:S(2)}) %collective-permute-start.31) | collective-permute-done | bytes 524320 | tf_op jit(solution)/shard_map/ppermute | solution.py:846
  355.6 7.5 %token_grads.1 = f32[1024,1024]{1,0:T(8,128)} custom-call(s32[1]{0:T(128)} %bitcast.core._, bf16[1024,1024]{1,0:T(8,128)(2,1)} %x.11, bf16[1024,1024]{1,0:T(8,128)(2,1)} %cot.3, bf16[1024,1024]{1,0:T(8,128)(2,1)} %input_back.1.own, bf16[1024,1024]{1,0:T(8,128)(2,1)} %collective-permute-done.32.other, bf16[1024,1024]{1,0:T(8,128)(2,1)} %get-tuple-element.310.gm, ...), custom_call_target="tpu_custom_call" | custom-call | flops 251658 | bytes 293601 | tf_op jit(solution)/shard_map/token_grads/pallas_call | solution.py:388
  363.7 5.8 %collective-permute-done.34 = bf16[256,640]{1,0:T(8,128)(2,1)} collective-permute-done((bf16[256,640]{1,0:T(8,128)(2,1)}, bf16[256,640]{1,0:T(8,128)(2,1)}, u32[]{:S(2)}, u32[]{:S(2)}) %collective-permute-start.34) | collective-permute-done | bytes 327712 | tf_op jit(solution)/shard_map/ppermute | solution.py:816
  369.7 6.8 %collective-permute-done.36 = bf16[256,1024]{1,0:T(8,128)(2,1)} collective-permute-done((bf16[256,1024]{1,0:T(8,128)(2,1)}, bf16[256,1024]{1,0:T(8,128)(2,1)}, u32[]{:S(2)}, u32[]{:S(2)}) %collective-permute-start.36) | collective-permute-done | bytes 524320 | tf_op jit(solution)/shard_map/ppermute | solution.py:846
  392.8 11.4 %collective-permute-done.39 = bf16[256,640]{1,0:T(8,128)(2,1)S(1)} collective-permute-done((bf16[256,640]{1,0:T(8,128)(2,1)S(1)}, bf16[256,640]{1,0:T(8,128)(2,1)S(1)}, u32[]{:S(2)}, u32[]{:S(2)}) %collective-permute-start.39) | collective-permute-done | bytes 327712 | tf_op jit(solution)/shard_map/ppermute | solution.py:846
  417.3 6.8 %collective-permute-done.41.refs_2_ = bf16[256,640]{1,0:T(8,128)(2,1)S(1)} collective-permute-done((bf16[256,640]{1,0:T(8,128)(2,1)S(1)}, bf16[256,640]{1,0:T(8,128)(2,1)S(1)}, u32[]{:S(2)}, u32[]{:S(2)}) %collective-permute-start.41) | collective-permute-done | bytes 327712 | tf_op jit(solution)/shard_map/ppermute | solution.py:816
  (193 shorter events, 115.0 us)
Async XLA Ops:
  4.0 35.4 %collective-permute-start.3 = (bf16[3,1024,256]{2,1,0:T(8,128)(2,1)}, bf16[3,1024,256]{2,1,0:T(8,128)(2,1)}, u32[]{:S(2)}, u32[]{:S(2)}) collective-permute-start(bf16[3,1024,256]{2,1,0:T(8,128)(2,1)} %get-tuple-element.177.refs_4_.refs_6_), channel_id=1, source_target_pairs={{0,1},{1,0},{2,3},{3,2},{4,5},{5,4},{6,7},{7,6},{8,9},{9,8},{10,11... | collective-permute-start | bytes 4718600 | tf_op jit(solution)/shard_map/ppermute | solution.py:822
  4.4 40.1 %collective-permute-start.4 = (bf16[3,1024,256]{2,1,0:T(8,128)(2,1)}, bf16[3,1024,256]{2,1,0:T(8,128)(2,1)}, u32[]{:S(2)}, u32[]{:S(2)}) collective-permute-start(bf16[3,1024,256]{2,1,0:T(8,128)(2,1)} %get-tuple-element.177.refs_4_.refs_6_), channel_id=1, source_target_pairs={{0,8},{2,10},{4,12},{6,14},{8,16},{10,18},{12,20},{14,22},{16,24},... | collective-permute-start | bytes 4718600 | tf_op jit(solution)/shard_map/ppermute | solution.py:819
  7.0 32.3 %collective-permute-start.1 = (bf16[528,1024]{1,0:T(8,128)(2,1)}, bf16[528,1024]{1,0:T(8,128)(2,1)S(1)}, u32[]{:S(2)}, u32[]{:S(2)}) collective-permute-start(bf16[528,1024]{1,0:T(8,128)(2,1)} %get-tuple-element.194.refs_2_.refs_4_.tail), channel_id=1, source_target_pairs={{0,2},{2,0},{4,6},{6,4},{8,10},{10,8},{12,14},{14,12},{16,18},{18,... | collective-permute-start | bytes 3244040 | tf_op jit(solution)/shard_map/ppermute | solution.py:816
  8.5 30.8 %collective-permute-start.2 = (bf16[528,1024]{1,0:T(8,128)(2,1)}, bf16[528,1024]{1,0:T(8,128)(2,1)S(1)}, u32[]{:S(2)}, u32[]{:S(2)}) collective-permute-start(bf16[528,1024]{1,0:T(8,128)(2,1)} %get-tuple-element.194.refs_2_.refs_4_.tail), channel_id=1, source_target_pairs={{0,4},{2,6},{4,0},{6,2},{8,12},{10,14},{12,8},{14,10},{16,20},{18,... | collective-permute-start | bytes 3244040 | tf_op jit(solution)/shard_map/ppermute | solution.py:816
  47.4 49.5 %collective-permute-start.8 = (bf16[3,1024,256]{2,1,0:T(8,128)(2,1)}, bf16[3,1024,256]{2,1,0:T(8,128)(2,1)}, u32[]{:S(2)}, u32[]{:S(2)}) collective-permute-start(bf16[3,1024,256]{2,1,0:T(8,128)(2,1)} %collective-permute-done.4.refs_6_.refs_8_), channel_id=1, source_target_pairs={{0,8},{2,10},{4,12},{6,14},{8,16},{10,18},{12,20},{14,22},{16,24},... | collective-permute-start | bytes 4718600 | tf_op jit(solution)/shard_map/ppermute | solution.py:819
  71.5 26.3 %collective-permute-start.9 = (bf16[528,1024]{1,0:T(8,128)(2,1)S(1)}, bf16[528,1024]{1,0:T(8,128)(2,1)}, u32[]{:S(2)}, u32[]{:S(2)}) collective-permute-start(bf16[528,1024]{1,0:T(8,128)(2,1)S(1)} %copy-done), channel_id=1, source_target_pairs={{0,6},{2,4},{4,2},{6,0},{8,14},{10,12},{12,10},{14,8},{16,22},{18,... | collective-permute-start | bytes 3244040 | tf_op jit(solution)/shard_map/ppermute | solution.py:816
  97.0 46.3 %collective-permute-start.12 = (bf16[3,1024,256]{2,1,0:T(8,128)(2,1)}, bf16[3,1024,256]{2,1,0:T(8,128)(2,1)}, u32[]{:S(2)}, u32[]{:S(2)}) collective-permute-start(bf16[3,1024,256]{2,1,0:T(8,128)(2,1)} %collective-permute-done.8.refs_14_.refs_8_), channel_id=1, source_target_pairs={{0,8},{2,10},{4,12},{6,14},{8,16},{10,18},{12,20},{14,22},{16,24},... | collective-permute-start | bytes 4718600 | tf_op jit(solution)/shard_map/ppermute | solution.py:819
  97.8 27.0 %collective-permute-start.11 = (bf16[512,1024]{1,0:T(8,128)(2,1)S(1)}, bf16[512,1024]{1,0:T(8,128)(2,1)S(1)}, u32[]{:S(2)}, u32[]{:S(2)}) collective-permute-start(bf16[512,1024]{1,0:T(8,128)(2,1)S(1)} %copy-done.1), channel_id=1, source_target_pairs={{0,6},{2,4},{4,2},{6,0},{8,14},{10,12},{12,10},{14,8},{16,22},{18,... | collective-permute-start | bytes 3145736 | tf_op jit(solution)/shard_map/ppermute | solution.py:816
  164.3 75.6 %collective-permute-start.18 = (bf16[3,1024,256]{2,1,0:T(8,128)(2,1)}, bf16[3,1024,256]{2,1,0:T(8,128)(2,1)}, u32[]{:S(2)}, u32[]{:S(2)}) collective-permute-start(bf16[3,1024,256]{2,1,0:T(8,128)(2,1)} %fusion), channel_id=1, source_target_pairs={{0,8},{2,10},{4,12},{6,14},{8,16},{10,18},{12,20},{14,22},{16,24},... | collective-permute-start | bytes 4718600 | tf_op jit(solution)/shard_map/ppermute | solution.py:819
  189.9 49.7 %collective-permute-start.15 = (bf16[528,1024]{1,0:T(8,128)(2,1)}, bf16[528,1024]{1,0:T(8,128)(2,1)S(1)}, u32[]{:S(2)}, u32[]{:S(2)}) collective-permute-start(bf16[528,1024]{1,0:T(8,128)(2,1)} %get-tuple-element.254), channel_id=1, source_target_pairs={{0,2},{2,0},{4,6},{6,4},{8,10},{10,8},{12,14},{14,12},{16,18},{18,... | collective-permute-start | bytes 3244040 | tf_op jit(solution)/shard_map/ppermute | solution.py:816
  190.8 48.8 %collective-permute-start.16 = (bf16[528,1024]{1,0:T(8,128)(2,1)}, bf16[528,1024]{1,0:T(8,128)(2,1)S(1)}, u32[]{:S(2)}, u32[]{:S(2)}) collective-permute-start(bf16[528,1024]{1,0:T(8,128)(2,1)} %get-tuple-element.255), channel_id=1, source_target_pairs={{0,4},{2,6},{4,0},{6,2},{8,12},{10,14},{12,8},{14,10},{16,20},{18,... | collective-permute-start | bytes 3244040 | tf_op jit(solution)/shard_map/ppermute | solution.py:816
  192.0 47.9 %collective-permute-start.17 = (bf16[528,1024]{1,0:T(8,128)(2,1)}, bf16[528,1024]{1,0:T(8,128)(2,1)S(1)}, u32[]{:S(2)}, u32[]{:S(2)}) collective-permute-start(bf16[528,1024]{1,0:T(8,128)(2,1)} %get-tuple-element.256), channel_id=1, source_target_pairs={{0,6},{2,4},{4,2},{6,0},{8,14},{10,12},{12,10},{14,8},{16,22},{18,... | collective-permute-start | bytes 3244040 | tf_op jit(solution)/shard_map/ppermute | solution.py:816
  250.8 43.5 %collective-permute-start.23 = (bf16[2,3,1024,256]{3,2,1,0:T(8,128)(2,1)}, bf16[2,3,1024,256]{3,2,1,0:T(8,128)(2,1)}, u32[]{:S(2)}, u32[]{:S(2)}) collective-permute-start(bf16[2,3,1024,256]{3,2,1,0:T(8,128)(2,1)} %get-tuple-element.281), channel_id=1, source_target_pairs={{0,1},{1,0},{2,3},{3,2},{4,5},{5,4},{6,7},{7,6},{8,9},{9,8},{10,11... | collective-permute-start | bytes 9437192 | tf_op jit(solution)/shard_map/ppermute | solution.py:822
  255.1 39.2 %collective-permute-start.22 = (bf16[3,1024,256]{2,1,0:T(8,128)(2,1)}, bf16[3,1024,256]{2,1,0:T(8,128)(2,1)}, u32[]{:S(2)}, u32[]{:S(2)}) collective-permute-start(bf16[3,1024,256]{2,1,0:T(8,128)(2,1)} %fusion.2), channel_id=1, source_target_pairs={{0,8},{2,10},{4,12},{6,14},{8,16},{10,18},{12,20},{14,22},{16,24},... | collective-permute-start | bytes 4718600 | tf_op jit(solution)/shard_map/ppermute | solution.py:819
  257.5 41.4 %collective-permute-start.26 = (bf16[512,1024]{1,0:T(8,128)(2,1)}, bf16[512,1024]{1,0:T(8,128)(2,1)}, u32[]{:S(2)}, u32[]{:S(2)}) collective-permute-start(bf16[512,1024]{1,0:T(8,128)(2,1)} %get-tuple-element.291), channel_id=1, source_target_pairs={{0,6},{2,4},{4,2},{6,0},{8,14},{10,12},{12,10},{14,8},{16,22},{18,... | collective-permute-start | bytes 3145736 | tf_op jit(solution)/shard_map/ppermute | solution.py:816
  260.1 46.5 %collective-permute-start.25 = (bf16[512,1024]{1,0:T(8,128)(2,1)}, bf16[512,1024]{1,0:T(8,128)(2,1)}, u32[]{:S(2)}, u32[]{:S(2)}) collective-permute-start(bf16[512,1024]{1,0:T(8,128)(2,1)} %get-tuple-element.289), channel_id=1, source_target_pairs={{0,4},{2,6},{4,0},{6,2},{8,12},{10,14},{12,8},{14,10},{16,20},{18,... | collective-permute-start | bytes 3145736 | tf_op jit(solution)/shard_map/ppermute | solution.py:816
  262.2 64.7 %collective-permute-start.24 = (bf16[512,1024]{1,0:T(8,128)(2,1)}, bf16[512,1024]{1,0:T(8,128)(2,1)}, u32[]{:S(2)}, u32[]{:S(2)}) collective-permute-start(bf16[512,1024]{1,0:T(8,128)(2,1)} %get-tuple-element.287), channel_id=1, source_target_pairs={{0,2},{2,0},{4,6},{6,4},{8,10},{10,8},{12,14},{14,12},{16,18},{18,... | collective-permute-start | bytes 3145736 | tf_op jit(solution)/shard_map/ppermute | solution.py:816
  297.9 49.7 %collective-permute-start.30 = (bf16[3,1024,256]{2,1,0:T(8,128)(2,1)}, bf16[3,1024,256]{2,1,0:T(8,128)(2,1)}, u32[]{:S(2)}, u32[]{:S(2)}) collective-permute-start(bf16[3,1024,256]{2,1,0:T(8,128)(2,1)} %fusion.1), channel_id=1, source_target_pairs={{0,8},{2,10},{4,12},{6,14},{8,16},{10,18},{12,20},{14,22},{16,24},... | collective-permute-start | bytes 4718600 | tf_op jit(solution)/shard_map/ppermute | solution.py:819
  297.9 34.2 %collective-permute-start.27 = (bf16[256,1024]{1,0:T(8,128)(2,1)}, bf16[256,1024]{1,0:T(8,128)(2,1)}, u32[]{:S(2)}, u32[]{:S(2)}) collective-permute-start(bf16[256,1024]{1,0:T(8,128)(2,1)} %get-tuple-element.295), channel_id=1, source_target_pairs={{0,2},{2,0},{4,6},{6,4},{8,10},{10,8},{12,14},{14,12},{16,18},{18,... | collective-permute-start | bytes 1572872 | tf_op jit(solution)/shard_map/ppermute | solution.py:816
  298.9 33.2 %collective-permute-start.28 = (bf16[256,1024]{1,0:T(8,128)(2,1)}, bf16[256,1024]{1,0:T(8,128)(2,1)}, u32[]{:S(2)}, u32[]{:S(2)}) collective-permute-start(bf16[256,1024]{1,0:T(8,128)(2,1)} %get-tuple-element.296), channel_id=1, source_target_pairs={{0,4},{2,6},{4,0},{6,2},{8,12},{10,14},{12,8},{14,10},{16,20},{18,... | collective-permute-start | bytes 1572872 | tf_op jit(solution)/shard_map/ppermute | solution.py:816
  347.7 30.2 %collective-permute-start.37 = (bf16[512,1024]{1,0:T(8,128)(2,1)}, bf16[512,1024]{1,0:T(8,128)(2,1)}, u32[]{:S(2)}, u32[]{:S(2)}) collective-permute-start(bf16[512,1024]{1,0:T(8,128)(2,1)} %get-tuple-element.321), channel_id=1, source_target_pairs={{0,1},{1,0},{2,3},{3,2},{4,5},{5,4},{6,7},{7,6},{8,9},{9,8},{10,11... | collective-permute-start | bytes 3145736 | tf_op jit(solution)/shard_map/ppermute | solution.py:822
  350.2 26.3 %collective-permute-start.36 = (bf16[256,1024]{1,0:T(8,128)(2,1)}, bf16[256,1024]{1,0:T(8,128)(2,1)}, u32[]{:S(2)}, u32[]{:S(2)}) collective-permute-start(bf16[256,1024]{1,0:T(8,128)(2,1)} %add_convert_fusion.1), channel_id=1, source_target_pairs={{0,16},{2,18},{4,20},{6,22},{8,24},{10,26},{12,28},{14,30},{16,0},... | collective-permute-start | bytes 1572872 | tf_op jit(solution)/shard_map/ppermute | solution.py:846
  385.1 26.6 %collective-permute-start.44 = (bf16[256,1024]{1,0:T(8,128)(2,1)}, bf16[256,1024]{1,0:T(8,128)(2,1)}, u32[]{:S(2)}, u32[]{:S(2)}) collective-permute-start(bf16[256,1024]{1,0:T(8,128)(2,1)} %add_convert_fusion.refs_0_), channel_id=1, source_target_pairs={{0,4},{2,6},{4,0},{6,2},{8,12},{10,14},{12,8},{14,10},{16,20},{18,... | collective-permute-start | bytes 1572872 | tf_op jit(solution)/shard_map/ppermute | solution.py:816
  385.8 25.8 %collective-permute-start.45 = (bf16[256,1024]{1,0:T(8,128)(2,1)}, bf16[256,1024]{1,0:T(8,128)(2,1)}, u32[]{:S(2)}, u32[]{:S(2)}) collective-permute-start(bf16[256,1024]{1,0:T(8,128)(2,1)} %add_convert_fusion.refs_0_), channel_id=1, source_target_pairs={{0,6},{2,4},{4,2},{6,0},{8,14},{10,12},{12,10},{14,8},{16,22},{18,... | collective-permute-start | bytes 1572872 | tf_op jit(solution)/shard_map/ppermute | solution.py:816
  (53 other events, 589.1 us)

commit v4 on v3

--- a/solution.py
+++ b/solution.py
@@ -93,21 +93,17 @@
     )(core, x, own, other, gain, live)
 
 
-def experts_body(nb, nchunk, halves, first, carried, *refs):
+def experts_body(nb, nchunk, halves, *refs):
     ids = refs[0]
     at = 1
     h2s, pays = refs[at : at + nb], refs[at + nb : at + 2 * nb]
     at += 2 * nb
-    prevs = [None] * nb
-    if carried:
-        prevs = [refs[at + 2 * b : at + 2 * b + 2] for b in range(nb)]
-        at += 2 * nb
     wr = refs[at]
     packs = refs[at + 1 : at + 1 + nchunk]
     at += 1 + nchunk
-    outs = [refs[at + 4 * b : at + 4 * b + 4] for b in range(nb)]
-    at += 4 * nb
-    gates, dgacc, macc, xacc, buf, sem = refs[at:]
+    outs = [refs[at + 5 * b : at + 5 * b + 5] for b in range(nb)]
+    at += 5 * nb
+    dgacc, macc, xacc, buf, sem = refs[at:]
     c = pl.program_id(0)
     rows, width = h2s[0].shape
     f = buf.shape[3]
@@ -117,13 +113,9 @@
     def _():
         pltpu.make_async_copy(packs[0], buf.at[0], sem.at[0]).start()
         for b in range(nb):
-            gates[b] = gate_table(h2s[b], pays[b], wr)
-            if carried:
-                macc[b] = prevs[b][1][...].astype(F32)
-                xacc[b] = prevs[b][0][:rows, :].astype(F32)
-            else:
-                macc[b] = jnp.zeros((rows, width), F32)
-                xacc[b] = jnp.zeros((rows, width), F32)
+            outs[b][4][...] = gate_table(h2s[b], pays[b], wr)
+        macc[...] = jnp.zeros_like(macc)
+        xacc[...] = jnp.zeros_like(xacc)
         dgacc[...] = jnp.zeros_like(dgacc)
 
     for k in range(1, nchunk):
@@ -134,7 +126,7 @@
 
     slot = lax.rem(c, 2)
     pltpu.make_async_copy(packs[0], buf.at[slot], sem.at[slot]).wait()
-    r = first + c // halves
+    r = c // halves
     e = ids[r]
     nd = width // f
     for b in range(nb):
@@ -143,7 +135,7 @@
         gp = dot(hb, buf[slot, 0])
         up = dot(hb, buf[slot, 1])
         u = sum(dot_nt(g[:rows, k * f : (k + 1) * f], buf[slot, 2, k * f : (k + 1) * f, :]) for k in range(nd))
-        gate = jnp.sum(jnp.where(lane == e, gates[b], 0.0), axis=1, keepdims=True)
+        gate = jnp.sum(jnp.where(lane == e, outs[b][4][...], 0.0), axis=1, keepdims=True)
         sg = jax.nn.sigmoid(gp)
         sl = gp * sg
         act = sl * up
@@ -165,40 +157,38 @@
             dx, moe = outs[b][:2]
             moe[...] = macc[b].astype(BF)
             dx[:rows, :] = xacc[b].astype(BF)
-            dg = dgacc[b].T[:8]
-            high = dg.astype(BF).astype(F32)
-            tail = jnp.concatenate([high, dg - high], axis=0)
-            if carried:
-                row = lax.broadcasted_iota(jnp.int32, (16, rows), 0) % 8
-                mine = (row >= first) & (row < first + nchunk // halves)
-                tail = jnp.where(mine, tail, prevs[b][0][rows:, :rows].astype(F32))
             dx[rows:, :] = jnp.zeros((16, width), BF)
-            dx[rows:, :rows] = tail.astype(BF)
-
-
-def experts(ids, h2s, pays, prevs, wr, packs, halves, first):
+            dx[rows:, :rows] = gate_tail(dgacc[b])
+
+
+def gate_tail(dg):
+    dg = dg.T[:8]
+    high = dg.astype(BF).astype(F32)
+    return jnp.concatenate([high, dg - high], axis=0).astype(BF)
+
+
+def experts(ids, h2s, pays, wr, packs, halves):
     rows, width = h2s[0].shape
     nb, nchunk = len(h2s), len(packs)
     f = packs[0].shape[2]
-    carried = prevs is not None
-    flat = [v for prev in prevs for v in prev] if carried else []
+    ne, hidden = nchunk // halves, halves * f
     shape = jax.ShapeDtypeStruct
     once = lambda v: pl.BlockSpec(v.shape, lambda *_: (0,) * len(v.shape), pipeline_mode=pl.Buffered(1))
     out = pl.pallas_call(
-        functools.partial(experts_body, nb, nchunk, halves, first, carried),
+        functools.partial(experts_body, nb, nchunk, halves),
         grid_spec=pltpu.PrefetchScalarGridSpec(
             num_scalar_prefetch=1,
             grid=(nchunk,),
-            in_specs=[once(v) for v in (*h2s, *pays, *flat, wr)] + [pl.BlockSpec(memory_space=pl.ANY)] * nchunk,
+            in_specs=[once(v) for v in (*h2s, *pays, wr)] + [pl.BlockSpec(memory_space=pl.ANY)] * nchunk,
             out_specs=[
                 pl.BlockSpec((rows + 16, width), lambda c, _: (0, 0)),
                 pl.BlockSpec((rows, width), lambda c, _: (0, 0)),
-                pl.BlockSpec((1, f, rows), lambda c, _: (c, 0, 0)),
-                pl.BlockSpec((1, rows, 2 * f), lambda c, _: (c, 0, 0)),
+                pl.BlockSpec((1, f, rows), lambda c, _: (c // halves, c % halves, 0)),
+                pl.BlockSpec((1, rows, 2 * f), lambda c, _: (c // halves, 0, c % halves)),
+                pl.BlockSpec((rows, 128), lambda c, _: (0, 0)),
             ]
             * nb,
             scratch_shapes=[
-                pltpu.VMEM((nb, rows, 128), F32),
                 pltpu.VMEM((nb, rows, 128), F32),
                 pltpu.VMEM((nb, rows, width), F32),
                 pltpu.VMEM((nb, rows, width), F32),
@@ -209,14 +199,108 @@
         out_shape=[
             shape((rows + 16, width), BF),
             shape((rows, width), BF),
-            shape((nchunk, f, rows), BF),
-            shape((nchunk, rows, 2 * f), BF),
+            shape((ne, hidden, rows), BF),
+            shape((ne, rows, 2 * hidden), BF),
+            shape((rows, 128), F32),
         ]
         * nb,
         compiler_params=pltpu.CompilerParams(vmem_limit_bytes=VMEM_BYTES),
         cost_estimate=cost(12 * rows * width * f * nchunk * nb, 6 * nchunk * width * f + 12 * rows * width * nb),
         name="experts",
-    )(ids, *h2s, *pays, *flat, wr, *packs)
+    )(ids, *h2s, *pays, wr, *packs)
+    return [out[5 * b : 5 * b + 5] for b in range(nb)]
+
+
+def weight_copies(packs, wgu, wd, sem, halves):
+    out = []
+    for h in range(halves):
+        pack = packs[h]
+        f = pack.shape[2]
+        for j in range(2):
+            cols = pl.ds((2 * h + j) * f, f)
+            out.append(pltpu.make_async_copy(pack.at[j], wgu.at[:, cols], sem.at[len(out)]))
+        for k in range(pack.shape[1] // f):
+            rows, cols = pl.ds(h * f, f), pl.ds(k * f, f)
+            out.append(pltpu.make_async_copy(pack.at[2, pl.ds(k * f, f), :], wd.at[rows, cols], sem.at[len(out)]))
+    return out
+
+
+def one_expert_body(nb, halves, r, ids, *refs):
+    it = iter(refs)
+    take = lambda n: [next(it) for _ in range(n)]
+    h2s, pays, gates = take(nb), take(nb), take(nb)
+    prevs = [take(2) for _ in range(nb)]
+    packs = take(halves)
+    outs = [take(4) for _ in range(nb)]
+    ga_all, wgu, wd, sem = it
+    rows, width = h2s[0].shape
+    f = wd.shape[0] // halves
+    copies = weight_copies(packs, wgu, wd, sem, halves)
+    for copy in copies:
+        copy.start()
+    lane = lax.broadcasted_iota(jnp.int32, (rows, 128), 1)
+    for copy in copies:
+        copy.wait()
+    for b in range(nb):
+        dx, moe, gat, dgu = outs[b]
+        gu = dot(h2s[b][...], wgu[...])
+        u = dot_nt(pays[b][:rows, :], wd[...])
+        gate = jnp.sum(jnp.where(lane == ids[r], gates[b][...], 0.0), axis=1, keepdims=True)
+        small = RESID_SCALE * gate
+        dg = jnp.zeros((rows, 1), F32)
+        for h in range(halves):
+            gp, up = gu[:, 2 * h * f : (2 * h + 1) * f], gu[:, (2 * h + 1) * f : (2 * h + 2) * f]
+            uh = u[:, h * f : (h + 1) * f]
+            sg = jax.nn.sigmoid(gp)
+            sl = gp * sg
+            act = sl * up
+            ga = (gate * act).astype(BF)
+            dg = dg + jnp.sum(act * uh, axis=1, keepdims=True)
+            da = small * uh
+            gat[0, h * f : (h + 1) * f, :] = ga.T
+            ga_all[:, h * f : (h + 1) * f] = ga
+            dgu[0, :, 2 * h * f : (2 * h + 1) * f] = (da * up * (sg + sl * (1.0 - sg))).astype(BF)
+            dgu[0, :, (2 * h + 1) * f : (2 * h + 2) * f] = (da * sl).astype(BF)
+        before = prevs[b]
+        moe[...] = (before[1][...].astype(F32) + dot(ga_all[...], wd[...])).astype(BF)
+        dx[:rows, :] = (before[0][:rows, :].astype(F32) + dot_nt(dgu[0], wgu[...])).astype(BF)
+        mine = lax.broadcasted_iota(jnp.int32, (16, rows), 0) % 8 == r
+        dx[rows:, :] = before[0][rows:, :]
+        tail = gate_tail(jnp.where(lane == r, dg * RESID_SCALE, 0.0))
+        dx[rows:, :rows] = jnp.where(mine, tail.astype(F32), before[0][rows:, :rows].astype(F32)).astype(BF)
+
+
+def one_expert(ids, h2s, pays, gates, prevs, packs, r):
+    rows, width = h2s[0].shape
+    nb, halves = len(h2s), len(packs)
+    f = packs[0].shape[2]
+    hidden = halves * f
+    flat = [v for prev in prevs for v in prev]
+    shape = jax.ShapeDtypeStruct
+    vmem = pl.BlockSpec(memory_space=pltpu.VMEM)
+    out = pl.pallas_call(
+        functools.partial(one_expert_body, nb, halves, r),
+        in_specs=[pl.BlockSpec(memory_space=pltpu.SMEM)]
+        + [vmem] * (5 * nb)
+        + [pl.BlockSpec(memory_space=pl.ANY)] * halves,
+        out_specs=[vmem] * (4 * nb),
+        scratch_shapes=[
+            pltpu.VMEM((rows, hidden), BF),
+            pltpu.VMEM((width, 2 * hidden), BF),
+            pltpu.VMEM((hidden, width), BF),
+            pltpu.SemaphoreType.DMA((halves * (2 + width // f),)),
+        ],
+        out_shape=[
+            shape((rows + 16, width), BF),
+            shape((rows, width), BF),
+            shape((1, hidden, rows), BF),
+            shape((1, rows, 2 * hidden), BF),
+        ]
+        * nb,
+        compiler_params=pltpu.CompilerParams(vmem_limit_bytes=VMEM_BYTES),
+        cost_estimate=cost(12 * rows * width * hidden * nb, 6 * width * hidden + 12 * rows * width * nb),
+        name="one_expert",
+    )(ids, *h2s, *pays, *gates, *flat, *packs)
     return [out[4 * b : 4 * b + 4] for b in range(nb)]
 
 
@@ -247,16 +331,20 @@
 def weight_grads(tok, h2s, pays, saved, halves):
     nb, ne = len(h2s), len(saved[0])
     rows, width = h2s[0].shape
-    f = saved[0][0][0].shape[1]
+    f = saved[0][0][0].shape[1] // halves
     shape = jax.ShapeDtypeStruct
     once = lambda v: pl.BlockSpec(v.shape, lambda *_: (0,) * len(v.shape), pipeline_mode=pl.Buffered(1))
     specs, args = [], []
     for n in range(ne):
         half = lambda e, c, n=n: jnp.where(e < n, 0, jnp.where(e == n, c, halves - 1))
-        for j, block in ((0, (1, f, rows)), (1, (1, rows, 2 * f))):
-            for b in range(nb):
-                args.append(saved[b][n][j])
-                specs.append(pl.BlockSpec(block, lambda e, c, o=saved[b][n][2], half=half: (o + half(e, c), 0, 0)))
+        for b in range(nb):
+            ga, dg, o = saved[b][n]
+            args.append(ga)
+            specs.append(pl.BlockSpec((1, f, rows), lambda e, c, o=o, half=half: (o, half(e, c), 0)))
+        for b in range(nb):
+            ga, dg, o = saved[b][n]
+            args.append(dg)
+            specs.append(pl.BlockSpec((1, rows, 2 * f), lambda e, c, o=o, half=half: (o, 0, half(e, c))))
     return pl.pallas_call(
         functools.partial(weight_grads_body, nb, halves),
         grid=(ne, halves),
@@ -269,14 +357,14 @@
     )(tok, *h2s, *pays, *args)
 
 
-def middle_back_body(nb, nlocal, _, ids, h2, mid, gain, tail, wr, *refs):
+def middle_back_body(nb, nlocal, _, ids, h2, mid, gain, gate, wr, *refs):
     dxs, tails = refs[:nb], refs[nb : 2 * nb]
-    *gms, small, acc = refs[2 * nb :]
+    gm, small, acc = refs[2 * nb :]
     rows, width = h2.shape
     at = pl.program_id(0)
     cols = pl.ds(pl.multiple_of(at * rows, rows), rows)
     lane = lax.broadcasted_iota(jnp.int32, (rows, 128), 1)
-    gates = gate_rows(h2[...], tail[:, cols], wr)
+    gates = gate[...]
     dgate = jnp.zeros((rows, 128), F32)
     for b in range(nb):
         part = tails[b][:, cols].astype(F32)
@@ -296,12 +384,8 @@
     col = jnp.broadcast_to(jnp.sum(dh * xhat, axis=0, keepdims=True), (8, width)).T[:, :1]
     su = dh * gain[...].astype(F32)
     grad = (r2 * (su - xhat * jnp.mean(su * xhat, axis=1, keepdims=True))).astype(BF)
-    for n, gm in enumerate(gms):
-
-        @pl.when(at == n)
-        def _(gm=gm):
-            gm[...] = grad
-
+    gm[0] = grad
+    gm[1] = grad
     small_here = jnp.where(lax.broadcasted_iota(jnp.int32, (width, 128), 1) == GAIN_F, col, router)
 
     @pl.when(at == 0)
@@ -315,7 +399,7 @@
     small[...] = acc[...]
 
 
-def middle_back(tok, ids, h2, mid, gain, pay, wr, dxs, nlocal):
+def middle_back(tok, ids, h2, mid, gain, gates, wr, dxs, nlocal):
     rows, width = h2.shape
     rt = rows // 2 if rows % 512 == 0 else rows
     shape = jax.ShapeDtypeStruct
@@ -327,16 +411,16 @@
         functools.partial(middle_back_body, len(dxs), nlocal),
         grid=(rows // rt,),
         in_specs=[pl.BlockSpec(memory_space=pltpu.SMEM)] * 2
-        + [block, block, whole(gain), tail, whole(wr)]
+        + [block, block, whole(gain), pl.BlockSpec((rt, 128), lambda i: (i, 0)), whole(wr)]
         + [block] * len(dxs)
         + [tail] * len(dxs),
-        out_specs=[pl.BlockSpec((rt, width), lambda i: (0, 0))] * (rows // rt) + [small],
-        out_shape=[shape((rt, width), BF)] * (rows // rt) + [shape((width, 128), F32)],
+        out_specs=[pl.BlockSpec((2, rt, width), lambda i: (0, i, 0)), small],
+        out_shape=[shape((2, rows, width), BF), shape((width, 128), F32)],
         scratch_shapes=[pltpu.VMEM((width, 128), F32)],
         compiler_params=pltpu.CompilerParams(vmem_limit_bytes=VMEM_BYTES),
         cost_estimate=cost(40 * rows * width, 20 * rows * width),
         name="middle_back",
-    )(tok, ids, h2, mid, gain, pay, wr, *dxs, *dxs)
+    )(tok, ids, h2, mid, gain, gates, wr, *dxs, *dxs)
 
 
 def input_back_body(nq, _, wq, wkv, *refs):
@@ -537,7 +621,19 @@
     )(core, gu, down, cot, routes)
 
 
-def attn_forward_body(core, lengths, x, gain, wq, wkv, wo, valid, h1, q, kd, vd, o, lse, cos, sin, own, *rest):
+def attn_forward_body(nout, core, lengths, x_hbm, gain, wq_hbm, wkv_hbm, wo_hbm, valid, *refs):
+    outs, bufs = refs[:nout], refs[nout : 2 * nout]
+    x, wq, wkv, wo, isem, osem = refs[2 * nout :]
+    h1, q, kd, vd, o, lse, cos, sin, own, *rest = bufs
+    nb = x.shape[0] // BLK
+    ins = [pltpu.make_async_copy(x_hbm.at[pl.ds(i * BLK, BLK), :], x.at[pl.ds(i * BLK, BLK), :], isem.at[i]) for i in range(nb)]
+    weights = [
+        pltpu.make_async_copy(source, to, isem.at[nb + n])
+        for n, (source, to) in enumerate(((wq_hbm, wq), (wkv_hbm, wkv), (wo_hbm, wo)))
+    ]
+    for copy in (ins[0], *weights, *ins[1:]):
+        copy.start()
+    leaving = []
     nkv = wkv.shape[1] // 128
     lane = lax.broadcasted_iota(jnp.int32, (BLK, 128), 1)
     low = lane < HD
@@ -555,10 +651,14 @@
         sb = jnp.where(lane % HD < HD // 2, -sb, sb)
         cos[rs, :] = cb
         sin[rs, :] = sb
+        ins[i].wait()
         xb = x[rs, :].astype(F32)
         r = lax.rsqrt(jnp.mean(xb * xb, axis=1, keepdims=True) + NORM_EPS)
         hb = (xb * r * ga).astype(BF)
         h1[rs, :] = hb
+        if i == 0:
+            weights[0].wait()
+            weights[1].wait()
         qp = dot(hb, wq[...])
         kvp = dot(hb, wkv[...])
         for n in range(nkv):
@@ -569,6 +669,9 @@
             rot = kv * cb + swap_halves(kv, lane) * sb
             kd[rs, ns] = jnp.where(low, rot, pltpu.roll(rot, HD, 1)).astype(BF)
             vd[rs, ns] = jnp.where(low, pltpu.roll(kv, HD, 1), kv).astype(BF)
+        for j in (0, 1, 2, 3, 6, 7):
+            leaving.append(pltpu.make_async_copy(bufs[j].at[rs, :], outs[j].at[rs, :], osem.at[i, j]))
+            leaving[-1].start()
         bias = mask_bias(start, valid, i, keys)
         bias2 = jnp.concatenate([bias, bias], axis=0)
         lse_all = jnp.zeros((BLK, 128), F32)
@@ -586,19 +689,34 @@
             l2 = m + jnp.log(total)
             lse_all = jnp.where(lane == 2 * n, l2[:BLK], jnp.where(lane == 2 * n + 1, l2[BLK:], lse_all))
         lse[rs, :] = lse_all
+        for j in (4, 5):
+            leaving.append(pltpu.make_async_copy(bufs[j].at[rs, :], outs[j].at[rs, :], osem.at[i, j]))
+            leaving[-1].start()
+        if i == 0:
+            weights[2].wait()
         term = dot(o[rs, :], wo[...]).astype(BF)
+        at = pl.ds(i * BLK % half, BLK)
         if not rest:
             own[rs, :] = term
+            leaving.append(pltpu.make_async_copy(own.at[rs, :], outs[8].at[rs, :], osem.at[i, 8]))
+            leaving[-1].start()
         else:
-            at = pl.ds(i * BLK % half, BLK)
+            mine = pltpu.make_async_copy(own.at[at, :], outs[8].at[at, :], osem.at[i, 8])
+            other = pltpu.make_async_copy(rest[0].at[at, :], outs[9].at[at, :], osem.at[i, 8])
 
             @pl.when(core[0] == i * BLK // half)
             def _():
                 own[at, :] = term
+                mine.start()
 
             @pl.when(core[0] != i * BLK // half)
             def _():
                 rest[0][at, :] = term
+                other.start()
+
+            leaving.append(mine)
+    for copy in leaving:
+        copy.wait()
 
 
 def attn_forward(core, lengths, x, gain, wq, wkv, wo, valid, split):
@@ -606,20 +724,33 @@
     wid = wq.shape[1]
     kvw = wkv.shape[1]
     shape = jax.ShapeDtypeStruct
-    part = [shape((rows // 2, width), BF)] * 2 if split else [shape((rows, width), BF)]
+    part = [((rows // 2, width), BF)] * 2 if split else [((rows, width), BF)]
+    outs = [
+        ((rows, width), BF),
+        ((rows, wid), BF),
+        ((rows, kvw), BF),
+        ((rows, kvw), BF),
+        ((rows, wid), BF),
+        ((rows, 128), F32),
+        ((rows, 128), F32),
+        ((rows, 128), F32),
+        *part,
+    ]
+    nb = rows // BLK
+    smem, vmem, there = (pl.BlockSpec(memory_space=m) for m in (pltpu.SMEM, pltpu.VMEM, pl.ANY))
     return pl.pallas_call(
-        attn_forward_body,
-        in_specs=[pl.BlockSpec(memory_space=pltpu.SMEM)] * 2 + [pl.BlockSpec(memory_space=pltpu.VMEM)] * 6,
-        out_shape=[
-            shape((rows, width), BF),
-            shape((rows, wid), BF),
-            shape((rows, kvw), BF),
-            shape((rows, kvw), BF),
-            shape((rows, wid), BF),
-            shape((rows, 128), F32),
-            shape((rows, 128), F32),
-            shape((rows, 128), F32),
-            *part,
+        functools.partial(attn_forward_body, len(outs)),
+        in_specs=[smem, smem, there, vmem, there, there, there, vmem],
+        out_specs=[there] * len(outs),
+        out_shape=[shape(*s) for s in outs],
+        scratch_shapes=[pltpu.VMEM(*s) for s in outs]
+        + [
+            pltpu.VMEM((rows, width), BF),
+            pltpu.VMEM((width, wid), BF),
+            pltpu.VMEM((width, kvw), BF),
+            pltpu.VMEM((wid, width), BF),
+            pltpu.SemaphoreType.DMA((nb + 3,)),
+            pltpu.SemaphoreType.DMA((nb, 9)),
         ],
         compiler_params=pltpu.CompilerParams(vmem_limit_bytes=VMEM_BYTES),
         cost_estimate=cost(2 * rows * width * 3 * wid + 4 * rows * rows * 4 * wid, 12 * rows * width),
@@ -924,22 +1055,21 @@
     state = [None] * inner
     saved = [dict() for _ in range(inner)]
 
+    gates = [None] * inner
+
     def work(blocks, first, count):
-        prevs = None if state[blocks[0]] is None else [state[b] for b in blocks]
-        out = experts(
-            release(ids),
-            [h2s[b] for b in blocks],
-            [pays[b] for b in blocks],
-            prevs,
-            wr,
-            [c for r in range(first, first + count) for c in chunks[r]],
-            halves,
-            first,
-        )
-        for b, (dx, moe, gat, dgu) in zip(blocks, out, strict=True):
+        rows_in = [h2s[b] for b in blocks], [pays[b] for b in blocks]
+        packs = [c for r in range(first, first + count) for c in chunks[r]]
+        if state[blocks[0]] is None:
+            out = experts(release(ids), *rows_in, wr, packs, halves)
+        else:
+            held_gates, before = [gates[b] for b in blocks], [state[b] for b in blocks]
+            out = one_expert(release(ids), *rows_in, held_gates, before, packs, first)
+        for b, (dx, moe, gat, dgu, *gate) in zip(blocks, out, strict=True):
             state[b] = (dx, moe)
+            gates[b] = gate[0] if gate else gates[b]
             for r in range(count):
-                saved[b][first + r] = (gat, dgu, r * halves)
+                saved[b][first + r] = (gat, dgu, r)
         finish(out[0][1])
 
     def expert_grads(experts_of):
@@ -995,10 +1125,6 @@
         work([0], last, 1)
     dxs[0] = state[0][0]
     raws = [expert_grads(rs) for rs in later]
-    finish(*dxs, *([ring] if outer > 1 else []))
-    moes = [state[0][1]] + [across(release(state[k][1]), k) for k in range(1, inner)]
-    early = [swap(release(raw[1])) if pair and rs == [2] else None for rs, raw in zip(later, raws, strict=True)]
-
     def ring_step(r):
         nonlocal ring
         term = release(ring).astype(F32) + parts[r]
@@ -1008,20 +1134,30 @@
         finish(ring)
         ring = along(ring, 1)
 
-    *gm, small = middle_back(tok, ids_all, h2, mid, gain_f, pay, wr, dxs, outer)
-    finish(small)
-    if pair:
-        gm = [*gm, *[swap(v) for v in gm]]
-    else:
-        gm = [lax.all_gather(jnp.concatenate(gm), "tp", axis=0, tiled=True)]
-    for rs, raw, other in zip(later, raws, early, strict=True):
+    def take_part(rs, raw):
         if not pair:
             parts.update({r: own_hidden([raw[0][n]]) for n, r in enumerate(rs)})
-        else:
-            other = release(other) if other is not None else swap(release(raw[1]))
-            parts.update({r: raw[0][n].astype(F32) + other[n].astype(F32) for n, r in enumerate(rs)})
+            return
+        other = swap(release(raw[1]))
+        parts.update({r: raw[0][n].astype(F32) + other[n].astype(F32) for n, r in enumerate(rs)})
+        if rs == [2]:
+            finish(other)
+
+    finish(*dxs, *([ring] if outer > 1 else []))
     if outer > 2:
+        take_part(later[0], raws[0])
         ring_step(2)
+    for rs, raw in zip(later, raws, strict=True):
+        if rs != [2]:
+            take_part(rs, raw)
+    moes = [state[0][1]] + [across(release(state[k][1]), k) for k in range(1, inner)]
+    gm, small = middle_back(tok, ids_all, h2, mid, gain_f, gates[0], wr, dxs, outer)
+    if pair:
+        gm = lax.all_to_all(gm, "tp", 0, 0).reshape(rows, width)
+    else:
+        gm = lax.all_gather(gm[0], "tp", axis=0, tiled=True)
+    finish(gm)
+
     nkv = kd.shape[1] // 128
     groups = 2 if nkv % 2 == 0 else 1
     each = nkv // groups
@@ -1051,7 +1187,7 @@
             gain_attn[:, None],
             [sums],
             None if first_one else do,
-            (cotangent, w_out, o, *gm) if first_one else None,
+            (cotangent, w_out, o, gm) if first_one else None,
         )
         dq, dkv, sums, *pieces = out[: 3 + inner]
         if first_one:
@@ -1088,23 +1224,18 @@
         moving = next(ahead)
         terms = scatter_plane([release(v) for v in pieces])
     dh1 = input_back(tok, query_weight_matrix, key_value_weight, dqs, dkvs)
-    finish(dh1, *([ring] if outer > 1 else []), *([moving] if groups > 1 else []))
+    finish(dh1, *([ring] if outer > 1 else []), *([moving] if groups > 1 else []), *terms)
     if groups > 1:
         moving = next(ahead)
+    closing = closing_sum(terms)
     if pair:
         dh_other = swap(release(dh1))
+        out_other = swap(out_share)
     else:
         dh1, dh_other = lax.psum(dh1.astype(F32), "tp"), jnp.zeros_like(dh1)
-    finish(dh_other)
-    grad_tokens = token_grads(tok, tokens, cotangent, dh1, dh_other, gm_all, gain_a)
-    finish(grad_tokens, *terms)
-    if pair:
-        out_other = swap(out_share)
-    closing = closing_sum(terms)
-    if groups > 1:
-        finish(moving)
-    behind = column_steps(release(closing))
-    late = next(behind)
+    finish(dh_other, closing)
+    grad_tokens = token_grads(tok, tokens, cotangent, dh1, dh_other, gm, gain_a)
+    finish(grad_tokens)
     if pair:
         layer_out = jnp.where(
             core[0] == 0,
@@ -1114,15 +1245,20 @@
         finish(layer_out)
     else:
         layer_out = lax.all_gather(out_share, "tp", axis=0, tiled=True)
+    spreads = []
+    if groups > 1:
+        finish(moving)
+    behind = column_steps(release(closing))
+    late = next(behind)
+    if groups > 1:
+        for whole in ahead:
+            pass
+        finish(whole)
+        spreads.append(spread_plane(whole))
     for r in range(4, outer):
         ring_step(r)
     expert_sums = ring_step(0) if outer > 1 else parts[0]
     gu_grad, down_grad = unpacked(expert_sums)
-    spreads = []
-    if groups > 1:
-        for whole in ahead:
-            pass
-        spreads.append(spread_plane(release(whole)))
     finish(late)
     for whole in behind:
         pass

time: 441 us -> 433 us (0.982)
  Pallas kernels: 273 us -> 258 us
  blocking collectives: 0 us -> 8.61 us
    pallas_call x7, Pallas kernels: 139 us -> 126 us  [the longest x3 55.5 us: experts(): pl.pallas_call(functools.partial(experts_body, nb, nchunk, halves), grid_...]
    all_to_all x0 -> x1, blocking collectives: none -> 8.61 us  [on_device(): gm = lax.all_to_all(gm, 'tp', 0, 0).reshape(rows, width)]
    ppermute x4, waiting for transfers between devices: 24.9 us -> 31.6 us  [column_steps(): other = lax.ppermute(v, 'ep', [(i, i ^ bit * inner) for i in range(n_ep)])]
    ppermute x6, waiting for transfers between devices: 7.45 us -> 3.03 us  [along(): lax.ppermute(v, 'ep', [(i, (i + k * inner) % n_ep) for i in range(n_ep)])]
    ppermute x13 -> x11, waiting for transfers between devices: 5.74 us -> 9.61 us  [swap(): return lax.ppermute(v, 'tp', [(0, 1), (1, 0)])]
  transfers between devices with their start and end apart: 47 -> 45, of which waited for: 16 -> 17; matrix products, arithmetic and copies ran while one was open for 9% -> 8% of each run, Pallas kernels for 58% -> 56%
where the time goes in v4:
time: 433 us; the launch traced here: 426 us
  Pallas kernels  258 us (60%)
  waiting for transfers between devices  69.3 us (16%)
  starting transfers between devices  41.5 us (10%)
  other arithmetic  29.4 us (7%)
  local copies, waits for them, and re-layouts  17.4 us (4%)
  blocking collectives  8.61 us (2%)
    pallas_call x3, Pallas kernels, experts(): pl.pallas_call(functools.partial(experts_body, nb, nchunk, halves), grid_...  55.5 us
    pallas_call x3, Pallas kernels, weight_grads(): pl.pallas_call(functools.partial(weight_grads_body, nb, halves), grid=(ne...  49.6 us
    pallas_call x3, Pallas kernels, one_expert(): pl.pallas_call(functools.partial(one_expert_body, nb, halves, r), in_spec...  47.7 us
    pallas_call x2, Pallas kernels, attn_backward(): pl.pallas_call(functools.partial(attn_backward_body, first, len(parts), l...  40.8 us
    ppermute x4, waiting for transfers between devices, column_steps(): other = lax.ppermute(v, 'ep', [(i, i ^ bit * inner) for i in range(n_ep)])  31.6 us
    ppermute x24, starting transfers between devices, across(): return lax.ppermute(v, 'ep', [(i, i ^ k) for i in range(n_ep)])  30.2 us
    ppermute x24, waiting for transfers between devices, across(): return lax.ppermute(v, 'ep', [(i, i ^ k) for i in range(n_ep)])  25 us
    pallas_call x1, Pallas kernels, attn_forward(): pl.pallas_call(functools.partial(attn_forward_body, len(outs)), in_specs=...  22.6 us
  transfers between devices with their start and end apart: 45, of which 17 were waited for; matrix products, arithmetic and copies ran while one was open for 8% of the time, Pallas kernels for 56%

profile of v4, /device:TPU:0, one launch (start us, length us, event | category | flops | bytes accessed | tf_op | source)
XLA Modules:
  0.0 426.1 jit_solution(189591805417965397)
XLA Ops:
  10.7 22.6 %attention_forward.1 = (bf16[1024,1024]{1,0:T(8,128)(2,1)}, bf16[1024,512]{1,0:T(8,128)(2,1)}, bf16[1024,512]{1,0:T(8,128)(2,1)}, bf16[1024,512]{1,0:T(8,128)(2,...) custom-call(s32[1]{0:T(128)} %bitcast.core._, ...), custom_call_target="tpu_custom_call" | custom-call | flops 236223200 | bytes 251658 | tf_op jit(solution)/shard_map/attention_forward/pallas_call | solution.py:741
  37.2 4.3 %middle_norm.1 = (f32[512,1024]{1,0:T(8,128)}, bf16[512,1024]{1,0:T(8,128)(2,1)}, f32[8,128]{1,0:T(8,128)}) custom-call(s32[1]{0:T(128)} %bitcast.core._, bf16[1024,1024]{1,0:T(8,128)(2,1)} %x.9, bf16[512,1024]{1,0:T(8,128)(2,1)} %get-tuple-element.181.own, bf16[512,1024]{1,0:T(8,128)(2,1)} %copy-done.12, bf16[1,1024]{1,0:T(2,128)(2,1)} %broadcast_in_dim.38.gain, ...), custom_call_target="tpu_custom_call" | custom-call | flops 104857 | bytes 125829 | tf_op jit(solution)/shard_map/middle_norm/pallas_call | solution.py:81
  49.5 13.7 %experts.3 = (bf16[528,1024]{1,0:T(8,128)(2,1)}, bf16[512,1024]{1,0:T(8,128)(2,1)}, bf16[2,512,512]{2,1,0:T(8,128)(2,1)}, bf16[2,512,1024]{2,1,0:T(8,128)(2,1)}, f32[512,128]{1,0:T(8,128)}) custom-call(s32[4]{0:T(128)} %and_select_fusion.3.refs_0_.ids, bf16[512,1024]{1,0:T(8,128)(2,1)} %get-tuple-element.209.refs_1_.refs_0_.h2, ...), custom_call_target="tpu_custom_call" | custom-call | flops 128849016 | bytes 251658 | tf_op jit(solution)/shard_map/experts/pallas_call | solution.py:177
  63.3 7.1 %collective-permute-done.6.refs_1_.refs_0_ = bf16[512,1024]{1,0:T(8,128)(2,1)S(1)} collective-permute-done((bf16[512,1024]{1,0:T(8,128)(2,1)}, bf16[512,1024]{1,0:T(8,128)(2,1)S(1)}, u32[]{:S(2)}, u32[]{:S(2)}) %collective-permute-start.6) | collective-permute-done | bytes 1048608 | tf_op jit(solution)/shard_map/ppermute | solution.py:947
  73.1 24.1 %experts.4 = (bf16[528,1024]{1,0:T(8,128)(2,1)}, bf16[512,1024]{1,0:T(8,128)(2,1)}, bf16[2,512,512]{2,1,0:T(8,128)(2,1)}, bf16[2,512,1024]{2,1,0:T(8,128)(2,1)},...) custom-call(s32[4]{0:T(128)} %and_select_fusion.3.refs_0_.ids, ...), custom_call_target="tpu_custom_call" | custom-call | flops 257698032 | bytes 377487 | tf_op jit(solution)/shard_map/experts/pallas_call | solution.py:177
  101.1 19.3 %one_expert.3 = (bf16[528,1024]{1,0:T(8,128)(2,1)}, bf16[512,1024]{1,0:T(8,128)(2,1)}, bf16[1,512,512]{2,1,0:T(8,128)(2,1)}, bf16[1,512,1024]{2,1,0:T(8,128)(2,1...) custom-call(s32[4]{0:T(128)} %and_select_fusion.3.refs_0_.ids, ...), custom_call_target="tpu_custom_call" | custom-call | flops 193273536 | bytes 440401 | tf_op jit(solution)/shard_map/one_expert/pallas_call | solution.py:281
  125.2 17.6 %experts.5 = (bf16[528,1024]{1,0:T(8,128)(2,1)}, bf16[512,1024]{1,0:T(8,128)(2,1)}, bf16[3,512,512]{2,1,0:T(8,128)(2,1)}, bf16[3,512,1024]{2,1,0:T(8,128)(2,1)}, f32[512,128]{1,0:T(8,128)}) custom-call(s32[4]{0:T(128)} %and_select_fusion.3.refs_0_.ids, bf16[512,1024]{1,0:T(8,128)(2,1)} %copy-done.5, ...), custom_call_target="tpu_custom_call" | custom-call | flops 193273536 | bytes 314572 | tf_op jit(solution)/shard_map/experts/pallas_call | solution.py:177
  142.8 13.7 %expert_weight_grads.3 = (bf16[1,3,1024,256]{3,2,1,0:T(8,128)(2,1)}, bf16[1,3,1024,256]{3,2,1,0:T(8,128)(2,1)}) custom-call(s32[1]{0:T(128)} %bitcast.core._, bf16[512,1024]{1,0:T(8,128)(2,1)} %get-tuple-element.209.refs_1_.refs_0_.h2, bf16[512,1024]{1,0:T(8,128)(2,1)} %copy-done.4, bf16[512,1024]{1,0:T(8,128)(2,1)} %collective-permute-done.7.refs_2_.refs_1_, ...), custom_call_target="tpu_custom_call" | custom-call | flops 128849016 | bytes 230686 | tf_op jit(solution)/shard_map/expert_weight_grads/pallas_call | solution.py:348
  165.7 19.3 %one_expert.4 = (bf16[528,1024]{1,0:T(8,128)(2,1)}, bf16[512,1024]{1,0:T(8,128)(2,1)}, bf16[1,512,512]{2,1,0:T(8,128)(2,1)}, bf16[1,512,1024]{2,1,0:T(8,128)(2,1...) custom-call(s32[4]{0:T(128)} %and_select_fusion.3.refs_0_.ids, ...), custom_call_target="tpu_custom_call" | custom-call | flops 193273536 | bytes 440401 | tf_op jit(solution)/shard_map/one_expert/pallas_call | solution.py:281
  188.6 9.1 %one_expert.5 = (bf16[528,1024]{1,0:T(8,128)(2,1)}, bf16[512,1024]{1,0:T(8,128)(2,1)}, bf16[1,512,512]{2,1,0:T(8,128)(2,1)}, bf16[1,512,1024]{2,1,0:T(8,128)(2,1)}) custom-call(s32[4]{0:T(128)} %and_select_fusion.3.refs_0_.ids, bf16[512,1024]{1,0:T(8,128)(2,1)} %get-tuple-element.209.refs_1_.refs_0_.h2, ...), custom_call_target="tpu_custom_call" | custom-call | flops 64424508 | bytes 188743 | tf_op jit(solution)/shard_map/one_expert/pallas_call | solution.py:281
  197.7 13.8 %expert_weight_grads.4 = (bf16[1,3,1024,256]{3,2,1,0:T(8,128)(2,1)}, bf16[1,3,1024,256]{3,2,1,0:T(8,128)(2,1)}) custom-call(s32[1]{0:T(128)} %bitcast.core._, bf16[512,1024]{1,0:T(8,128)(2,1)} %get-tuple-element.209.refs_1_.refs_0_.h2, bf16[512,1024]{1,0:T(8,128)(2,1)} %copy-done.4, bf16[512,1024]{1,0:T(8,128)(2,1)} %collective-permute-done.7.refs_2_.refs_1_, ...), custom_call_target="tpu_custom_call" | custom-call | flops 128849016 | bytes 230686 | tf_op jit(solution)/shard_map/expert_weight_grads/pallas_call | solution.py:348
  211.5 22.1 %expert_weight_grads.5 = (bf16[2,3,1024,256]{3,2,1,0:T(8,128)(2,1)}, bf16[2,3,1024,256]{3,2,1,0:T(8,128)(2,1)}) custom-call(s32[1]{0:T(128)} %bitcast.core._, bf16[512,1024]{1,0:T(8,128)(2,1)} %get-tuple-element.209.refs_1_.refs_0_.h2, bf16[512,1024]{1,0:T(8,128)(2,1)} %copy-done.4, bf16[512,1024]{1,0:T(8,128)(2,1)} %collective-permute-done.7.refs_2_.refs_1_, ...), custom_call_target="tpu_custom_call" | custom-call | flops 128849016 | bytes 230686 | tf_op jit(solution)/shard_map/expert_weight_grads/pallas_call | solution.py:348
  249.5 8.4 %middle_back.1 = (bf16[2,512,1024]{2,1,0:T(8,128)(2,1)}, f32[1024,128]{1,0:T(8,128)}) custom-call(s32[1]{0:T(128)} %bitcast.core._, s32[16]{0:T(128)} %pad_add_fusion.ids, bf16[512,1024]{1,0:T(8,128)(2,1)} %get-tuple-element.209.refs_1_.refs_0_.h2, f32[512,1024]{1,0:T(8,128)} %get-tuple-element.269.mid.refs_0_, bf16[1,1024]{1,0:T(2,128)(2,1)} %broadcast_in_dim.38.gain, ...), custom_call_target="tpu_custom_call" | custom-call | flops 419430 | bytes 209715 | tf_op jit(solution)/shard_map/middle_back/pallas_call | solution.py:410
  257.9 8.6 %all_to_all.5 = bf16[2,512,1024]{2,1,0:T(8,128)(2,1)} all-to-all(bf16[2,512,1024]{2,1,0:T(8,128)(2,1)} %get-tuple-element.270), channel_id=1, replica_groups=mesh['ep'=16,'tp'=2] {'tp'}, dimensions={0} | all-to-all | bytes 4194304 | tf_op jit(solution)/shard_map/all_to_all | solution.py:1156
  266.5 23.2 %attention_backward.2 = (bf16[1024,256]{1,0:T(8,128)(2,1)}, bf16[1024,256]{1,0:T(8,128)(2,1)}, f32[1024,128]{1,0:T(8,128)}, bf16[256,1024]{1,0:T(8,128)(2,1)}, b...) custom-call(s32[1]{0:T(128)} %bitcast.core._, ...), custom_call_target="tpu_custom_call" | custom-call | flops 128849016 | bytes 209715 | tf_op jit(solution)/shard_map/attention_backward/pallas_call | solution.py:902
  299.9 17.7 %attention_backward.3 = (bf16[1024,256]{1,0:T(8,128)(2,1)}, bf16[1024,256]{1,0:T(8,128)(2,1)}, f32[1024,128]{1,0:T(8,128)}, bf16[256,640]{1,0:T(8,128)(2,1)}, bf...) custom-call(s32[1]{0:T(128)} %bitcast.core._, s32[1]{0:T(128)} %bitcast.8.at.me, ...), custom_call_target="tpu_custom_call" | custom-call | flops 128849016 | bytes 209715 | tf_op jit(solution)/shard_map/attention_backward/pallas_call | solution.py:902
  317.6 5.2 %layer_out.1 = (bf16[512,1024]{1,0:T(8,128)(2,1)}, f32[8,128]{1,0:T(8,128)}) custom-call(s32[1]{0:T(128)} %bitcast.core._, f32[512,1024]{1,0:T(8,128)} %get-tuple-element.269.mid.refs_0_, f32[512,1]{1,0:T(8,128)} %copy.32.refs_1_, bf16[512,1024]{1,0:T(8,128)(2,1)} %get-tuple-element.239.refs_2_, bf16[512,1024]{1,0:T(8,128)(2,1)} %collective-permute-done.22.refs_3_, ...), custom_call_target="tpu_custom_call" | custom-call | flops 125829 | bytes 146800 | tf_op jit(solution)/shard_map/layer_out/pallas_call | solution.py:508
  328.6 6.3 %input_back.1.own = bf16[1024,1024]{1,0:T(8,128)(2,1)} custom-call(s32[1]{0:T(128)} %bitcast.core._, bf16[1024,512]{1,0:T(8,128)(2,1)} %wq.1, bf16[1024,512]{1,0:T(8,128)(2,1)} %wkv.1, bf16[1024,256]{1,0:T(8,128)(2,1)} %get-tuple-element.304.refs_0_, bf16[1024,256]{1,0:T(8,128)(2,1)} %get-tuple-element.305.refs_1_, ...), custom_call_target="tpu_custom_call" | custom-call | flops 42949672 | bytes 209715 | tf_op jit(solution)/shard_map/input_back/pallas_call | solution.py:447
  336.9 4.7 %collective-permute-done.31 = bf16[256,640]{1,0:T(8,128)(2,1)} collective-permute-done((bf16[256,640]{1,0:T(8,128)(2,1)}, bf16[256,640]{1,0:T(8,128)(2,1)}, u32[]{:S(2)}, u32[]{:S(2)}) %collective-permute-start.31) | collective-permute-done | bytes 327712 | tf_op jit(solution)/shard_map/ppermute | solution.py:947
  347.8 7.5 %token_grads.1 = f32[1024,1024]{1,0:T(8,128)} custom-call(s32[1]{0:T(128)} %bitcast.core._, bf16[1024,1024]{1,0:T(8,128)(2,1)} %x.9, bf16[1024,1024]{1,0:T(8,128)(2,1)} %cot.3, bf16[1024,1024]{1,0:T(8,128)(2,1)} %input_back.1.own, bf16[1024,1024]{1,0:T(8,128)(2,1)} %collective-permute-done.33.other, bf16[1024,1024]{1,0:T(8,128)(2,1)} %bitcast.32, ...), custom_call_target="tpu_custom_call" | custom-call | flops 251658 | bytes 293601 | tf_op jit(solution)/shard_map/token_grads/pallas_call | solution.py:472
  355.3 4.7 %maximum_select_fusion = bf16[1024,1024]{1,0:T(8,128)(2,1)} fusion(bf16[512,1024]{1,0:T(8,128)(2,1)} %collective-permute-done.34, bf16[512,1024]{1,0:T(8,128)(2,1)} %get-tuple-element.329, pred[]{:T(512)S(6)} %eq.18), kind=kLoop, calls=%fused_computation.8 | loop fusion | flops 9437184 | bytes 4194305 | tf_op jit(solution)/shard_map/jit(_where)/select_n | solution.py:1240
  360.0 11.7 %collective-permute-done.35 = bf16[256,1024]{1,0:T(8,128)(2,1)} collective-permute-done((bf16[256,1024]{1,0:T(8,128)(2,1)}, bf16[256,1024]{1,0:T(8,128)(2,1)}, u32[]{:S(2)}, u32[]{:S(2)}) %collective-permute-start.35) | collective-permute-done | bytes 524320 | tf_op jit(solution)/shard_map/ppermute | solution.py:977
  383.9 14.4 %collective-permute-done.37 = bf16[256,640]{1,0:T(8,128)(2,1)S(1)} collective-permute-done((bf16[256,640]{1,0:T(8,128)(2,1)S(1)}, bf16[256,640]{1,0:T(8,128)(2,1)S(1)}, u32[]{:S(2)}, u32[]{:S(2)}) %collective-permute-start.37) | collective-permute-done | bytes 327712 | tf_op jit(solution)/shard_map/ppermute | solution.py:977
  411.2 4.2 collective-permute-done.39.refs_2_
  (180 shorter events, 120.9 us)
Async XLA Ops:
  4.1 32.2 %collective-permute-start.3 = (bf16[3,1024,256]{2,1,0:T(8,128)(2,1)}, bf16[3,1024,256]{2,1,0:T(8,128)(2,1)}, u32[]{:S(2)}, u32[]{:S(2)}) collective-permute-start(bf16[3,1024,256]{2,1,0:T(8,128)(2,1)} %get-tuple-element.179.refs_4_.refs_6_), channel_id=1, source_target_pairs={{0,1},{1,0},{2,3},{3,2},{4,5},{5,4},{6,7},{7,6},{8,9},{9,8},{10,11... | collective-permute-start | bytes 4718600 | tf_op jit(solution)/shard_map/ppermute | solution.py:953
  4.5 40.0 %collective-permute-start.4 = (bf16[3,1024,256]{2,1,0:T(8,128)(2,1)}, bf16[3,1024,256]{2,1,0:T(8,128)(2,1)}, u32[]{:S(2)}, u32[]{:S(2)}) collective-permute-start(bf16[3,1024,256]{2,1,0:T(8,128)(2,1)} %get-tuple-element.179.refs_4_.refs_6_), channel_id=1, source_target_pairs={{0,8},{2,10},{4,12},{6,14},{8,16},{10,18},{12,20},{14,22},{16,24},... | collective-permute-start | bytes 4718600 | tf_op jit(solution)/shard_map/ppermute | solution.py:950
  7.1 29.1 %collective-permute-start.1 = (bf16[528,1024]{1,0:T(8,128)(2,1)}, bf16[528,1024]{1,0:T(8,128)(2,1)S(1)}, u32[]{:S(2)}, u32[]{:S(2)}) collective-permute-start(bf16[528,1024]{1,0:T(8,128)(2,1)} %get-tuple-element.196.refs_2_.refs_3_.refs_4_.refs_1_), channel_id=1, source_target_pairs={{0,2},{2,0},{4,6},{6,4},{8,10},{10,8},{12,14},{14,12},{16,18},{18,... | collective-permute-start | bytes 3244040 | tf_op jit(solution)/shard_map/ppermute | solution.py:947
  8.6 27.7 %collective-permute-start.2 = (bf16[528,1024]{1,0:T(8,128)(2,1)}, bf16[528,1024]{1,0:T(8,128)(2,1)S(1)}, u32[]{:S(2)}, u32[]{:S(2)}) collective-permute-start(bf16[528,1024]{1,0:T(8,128)(2,1)} %get-tuple-element.196.refs_2_.refs_3_.refs_4_.refs_1_), channel_id=1, source_target_pairs={{0,4},{2,6},{4,0},{6,2},{8,12},{10,14},{12,8},{14,10},{16,20},{18,... | collective-permute-start | bytes 3244040 | tf_op jit(solution)/shard_map/ppermute | solution.py:947
  47.5 49.7 %collective-permute-start.8 = (bf16[3,1024,256]{2,1,0:T(8,128)(2,1)}, bf16[3,1024,256]{2,1,0:T(8,128)(2,1)}, u32[]{:S(2)}, u32[]{:S(2)}) collective-permute-start(bf16[3,1024,256]{2,1,0:T(8,128)(2,1)} %collective-permute-done.4.refs_6_.refs_8_), channel_id=1, source_target_pairs={{0,8},{2,10},{4,12},{6,14},{8,16},{10,18},{12,20},{14,22},{16,24},... | collective-permute-start | bytes 4718600 | tf_op jit(solution)/shard_map/ppermute | solution.py:950
  71.6 26.2 %collective-permute-start.9 = (bf16[528,1024]{1,0:T(8,128)(2,1)S(1)}, bf16[528,1024]{1,0:T(8,128)(2,1)}, u32[]{:S(2)}, u32[]{:S(2)}) collective-permute-start(bf16[528,1024]{1,0:T(8,128)(2,1)S(1)} %copy-done.1), channel_id=1, source_target_pairs={{0,6},{2,4},{4,2},{6,0},{8,14},{10,12},{12,10},{14,8},{16,22},{18,... | collective-permute-start | bytes 3244040 | tf_op jit(solution)/shard_map/ppermute | solution.py:947
  97.4 45.4 %collective-permute-start.12 = (bf16[3,1024,256]{2,1,0:T(8,128)(2,1)}, bf16[3,1024,256]{2,1,0:T(8,128)(2,1)}, u32[]{:S(2)}, u32[]{:S(2)}) collective-permute-start(bf16[3,1024,256]{2,1,0:T(8,128)(2,1)} %collective-permute-done.8.refs_15_.refs_8_), channel_id=1, source_target_pairs={{0,8},{2,10},{4,12},{6,14},{8,16},{10,18},{12,20},{14,22},{16,24},... | collective-permute-start | bytes 4718600 | tf_op jit(solution)/shard_map/ppermute | solution.py:950
  97.8 26.3 %collective-permute-start.11 = (bf16[512,1024]{1,0:T(8,128)(2,1)S(1)}, bf16[512,1024]{1,0:T(8,128)(2,1)S(1)}, u32[]{:S(2)}, u32[]{:S(2)}) collective-permute-start(bf16[512,1024]{1,0:T(8,128)(2,1)S(1)} %copy-done), channel_id=1, source_target_pairs={{0,6},{2,4},{4,2},{6,0},{8,14},{10,12},{12,10},{14,8},{16,22},{18,... | collective-permute-start | bytes 3145736 | tf_op jit(solution)/shard_map/ppermute | solution.py:947
  163.2 72.1 %collective-permute-start.18 = (bf16[3,1024,256]{2,1,0:T(8,128)(2,1)}, bf16[3,1024,256]{2,1,0:T(8,128)(2,1)}, u32[]{:S(2)}, u32[]{:S(2)}) collective-permute-start(bf16[3,1024,256]{2,1,0:T(8,128)(2,1)} %fusion), channel_id=1, source_target_pairs={{0,8},{2,10},{4,12},{6,14},{8,16},{10,18},{12,20},{14,22},{16,24},... | collective-permute-start | bytes 4718600 | tf_op jit(solution)/shard_map/ppermute | solution.py:950
  185.0 48.5 %collective-permute-start.15 = (bf16[528,1024]{1,0:T(8,128)(2,1)}, bf16[528,1024]{1,0:T(8,128)(2,1)S(1)}, u32[]{:S(2)}, u32[]{:S(2)}) collective-permute-start(bf16[528,1024]{1,0:T(8,128)(2,1)} %get-tuple-element.260), channel_id=1, source_target_pairs={{0,2},{2,0},{4,6},{6,4},{8,10},{10,8},{12,14},{14,12},{16,18},{18,... | collective-permute-start | bytes 3244040 | tf_op jit(solution)/shard_map/ppermute | solution.py:947
  186.6 48.7 %collective-permute-start.16 = (bf16[528,1024]{1,0:T(8,128)(2,1)}, bf16[528,1024]{1,0:T(8,128)(2,1)S(1)}, u32[]{:S(2)}, u32[]{:S(2)}) collective-permute-start(bf16[528,1024]{1,0:T(8,128)(2,1)} %get-tuple-element.261), channel_id=1, source_target_pairs={{0,4},{2,6},{4,0},{6,2},{8,12},{10,14},{12,8},{14,10},{16,20},{18,... | collective-permute-start | bytes 3244040 | tf_op jit(solution)/shard_map/ppermute | solution.py:947
  187.1 48.2 %collective-permute-start.17 = (bf16[528,1024]{1,0:T(8,128)(2,1)}, bf16[528,1024]{1,0:T(8,128)(2,1)S(1)}, u32[]{:S(2)}, u32[]{:S(2)}) collective-permute-start(bf16[528,1024]{1,0:T(8,128)(2,1)} %get-tuple-element.262), channel_id=1, source_target_pairs={{0,6},{2,4},{4,2},{6,0},{8,14},{10,12},{12,10},{14,8},{16,22},{18,... | collective-permute-start | bytes 3244040 | tf_op jit(solution)/shard_map/ppermute | solution.py:947
  242.7 47.0 %collective-permute-start.21 = (bf16[2,3,1024,256]{3,2,1,0:T(8,128)(2,1)}, bf16[2,3,1024,256]{3,2,1,0:T(8,128)(2,1)}, u32[]{:S(2)}, u32[]{:S(2)}) collective-permute-start(bf16[2,3,1024,256]{3,2,1,0:T(8,128)(2,1)} %get-tuple-element.286), channel_id=1, source_target_pairs={{0,1},{1,0},{2,3},{3,2},{4,5},{5,4},{6,7},{7,6},{8,9},{9,8},{10,11... | collective-permute-start | bytes 9437192 | tf_op jit(solution)/shard_map/ppermute | solution.py:953
  242.9 46.8 %collective-permute-start.20 = (bf16[3,1024,256]{2,1,0:T(8,128)(2,1)}, bf16[3,1024,256]{2,1,0:T(8,128)(2,1)}, u32[]{:S(2)}, u32[]{:S(2)}) collective-permute-start(bf16[3,1024,256]{2,1,0:T(8,128)(2,1)} %fusion.2), channel_id=1, source_target_pairs={{0,8},{2,10},{4,12},{6,14},{8,16},{10,18},{12,20},{14,22},{16,24},... | collective-permute-start | bytes 4718600 | tf_op jit(solution)/shard_map/ppermute | solution.py:950
  244.5 51.5 %collective-permute-start.24 = (bf16[512,1024]{1,0:T(8,128)(2,1)}, bf16[512,1024]{1,0:T(8,128)(2,1)}, u32[]{:S(2)}, u32[]{:S(2)}) collective-permute-start(bf16[512,1024]{1,0:T(8,128)(2,1)} %get-tuple-element.296), channel_id=1, source_target_pairs={{0,6},{2,4},{4,2},{6,0},{8,14},{10,12},{12,10},{14,8},{16,22},{18,... | collective-permute-start | bytes 3145736 | tf_op jit(solution)/shard_map/ppermute | solution.py:947
  245.6 51.5 %collective-permute-start.23 = (bf16[512,1024]{1,0:T(8,128)(2,1)}, bf16[512,1024]{1,0:T(8,128)(2,1)}, u32[]{:S(2)}, u32[]{:S(2)}) collective-permute-start(bf16[512,1024]{1,0:T(8,128)(2,1)} %get-tuple-element.294), channel_id=1, source_target_pairs={{0,4},{2,6},{4,0},{6,2},{8,12},{10,14},{12,8},{14,10},{16,20},{18,... | collective-permute-start | bytes 3145736 | tf_op jit(solution)/shard_map/ppermute | solution.py:947
  248.0 69.5 %collective-permute-start.22 = (bf16[512,1024]{1,0:T(8,128)(2,1)}, bf16[512,1024]{1,0:T(8,128)(2,1)}, u32[]{:S(2)}, u32[]{:S(2)}) collective-permute-start(bf16[512,1024]{1,0:T(8,128)(2,1)} %get-tuple-element.292), channel_id=1, source_target_pairs={{0,2},{2,0},{4,6},{6,4},{8,10},{10,8},{12,14},{14,12},{16,18},{18,... | collective-permute-start | bytes 3145736 | tf_op jit(solution)/shard_map/ppermute | solution.py:947
  293.3 49.8 %collective-permute-start.28 = (bf16[3,1024,256]{2,1,0:T(8,128)(2,1)}, bf16[3,1024,256]{2,1,0:T(8,128)(2,1)}, u32[]{:S(2)}, u32[]{:S(2)}) collective-permute-start(bf16[3,1024,256]{2,1,0:T(8,128)(2,1)} %fusion.1), channel_id=1, source_target_pairs={{0,8},{2,10},{4,12},{6,14},{8,16},{10,18},{12,20},{14,22},{16,24},... | collective-permute-start | bytes 4718600 | tf_op jit(solution)/shard_map/ppermute | solution.py:950
  295.4 27.3 %collective-permute-start.25 = (bf16[256,1024]{1,0:T(8,128)(2,1)}, bf16[256,1024]{1,0:T(8,128)(2,1)}, u32[]{:S(2)}, u32[]{:S(2)}) collective-permute-start(bf16[256,1024]{1,0:T(8,128)(2,1)} %get-tuple-element.300), channel_id=1, source_target_pairs={{0,2},{2,0},{4,6},{6,4},{8,10},{10,8},{12,14},{14,12},{16,18},{18,... | collective-permute-start | bytes 1572872 | tf_op jit(solution)/shard_map/ppermute | solution.py:947
  296.0 26.8 %collective-permute-start.26 = (bf16[256,1024]{1,0:T(8,128)(2,1)}, bf16[256,1024]{1,0:T(8,128)(2,1)}, u32[]{:S(2)}, u32[]{:S(2)}) collective-permute-start(bf16[256,1024]{1,0:T(8,128)(2,1)} %get-tuple-element.301), channel_id=1, source_target_pairs={{0,4},{2,6},{4,0},{6,2},{8,12},{10,14},{12,8},{14,10},{16,20},{18,... | collective-permute-start | bytes 1572872 | tf_op jit(solution)/shard_map/ppermute | solution.py:947
  345.7 26.0 %collective-permute-start.35 = (bf16[256,1024]{1,0:T(8,128)(2,1)}, bf16[256,1024]{1,0:T(8,128)(2,1)}, u32[]{:S(2)}, u32[]{:S(2)}) collective-permute-start(bf16[256,1024]{1,0:T(8,128)(2,1)} %add_convert_fusion.1), channel_id=1, source_target_pairs={{0,16},{2,18},{4,20},{6,22},{8,24},{10,26},{12,28},{14,30},{16,0},... | collective-permute-start | bytes 1572872 | tf_op jit(solution)/shard_map/ppermute | solution.py:977
  373.9 26.3 %collective-permute-start.41 = (bf16[256,1024]{1,0:T(8,128)(2,1)}, bf16[256,1024]{1,0:T(8,128)(2,1)S(1)}, u32[]{:S(2)}, u32[]{:S(2)}) collective-permute-start(bf16[256,1024]{1,0:T(8,128)(2,1)} %add_convert_fusion.refs_0_), channel_id=1, source_target_pairs={{0,2},{2,0},{4,6},{6,4},{8,10},{10,8},{12,14},{14,12},{16,18},{18,... | collective-permute-start | bytes 1572872 | tf_op jit(solution)/shard_map/ppermute | solution.py:947
  374.5 31.3 %collective-permute-start.42 = (bf16[256,1024]{1,0:T(8,128)(2,1)}, bf16[256,1024]{1,0:T(8,128)(2,1)}, u32[]{:S(2)}, u32[]{:S(2)}) collective-permute-start(bf16[256,1024]{1,0:T(8,128)(2,1)} %add_convert_fusion.refs_0_), channel_id=1, source_target_pairs={{0,4},{2,6},{4,0},{6,2},{8,12},{10,14},{12,8},{14,10},{16,20},{18,... | collective-permute-start | bytes 1572872 | tf_op jit(solution)/shard_map/ppermute | solution.py:947
  375.6 30.1 %collective-permute-start.43 = (bf16[256,1024]{1,0:T(8,128)(2,1)}, bf16[256,1024]{1,0:T(8,128)(2,1)}, u32[]{:S(2)}, u32[]{:S(2)}) collective-permute-start(bf16[256,1024]{1,0:T(8,128)(2,1)} %add_convert_fusion.refs_0_), channel_id=1, source_target_pairs={{0,6},{2,4},{4,2},{6,0},{8,14},{10,12},{12,10},{14,8},{16,22},{18,... | collective-permute-start | bytes 1572872 | tf_op jit(solution)/shard_map/ppermute | solution.py:947
  (46 other events, 520.0 us)

commit v5 on v4

--- a/solution.py
+++ b/solution.py
@@ -1234,6 +1234,8 @@
     else:
         dh1, dh_other = lax.psum(dh1.astype(F32), "tp"), jnp.zeros_like(dh1)
     finish(dh_other, closing)
+    behind = column_steps(release(closing))
+    late = next(behind)
     grad_tokens = token_grads(tok, tokens, cotangent, dh1, dh_other, gm, gain_a)
     finish(grad_tokens)
     if pair:
@@ -1248,7 +1250,7 @@
     spreads = []
     if groups > 1:
         finish(moving)
-    behind = column_steps(release(closing))
+    finish(late)
     late = next(behind)
     if groups > 1:
         for whole in ahead:
@@ -1260,9 +1262,9 @@
     expert_sums = ring_step(0) if outer > 1 else parts[0]
     gu_grad, down_grad = unpacked(expert_sums)
     finish(late)
-    for whole in behind:
+    for late in behind:
         pass
-    spreads.append(spread_plane(release(whole)))
+    spreads.append(spread_plane(release(late)))
     if groups > 1:
         *grads, folded = gather_rows(at, spreads[0], (w, w, depth), groups, False)
         finish(folded)

time: 433 us -> 432 us (level)
    ppermute x4, waiting for transfers between devices: 31.6 us -> 24.3 us  [column_steps(): other = lax.ppermute(v, 'ep', [(i, i ^ bit * inner) for i in range(n_ep)])]
  transfers between devices with their start and end apart: 45 -> 45, of which waited for: 17 -> 18; matrix products, arithmetic and copies ran while one was open for 8% -> 8% of each run, Pallas kernels for 56% -> 56%
where the time goes in v5:
time: 432 us; the launch traced here: 424 us
  Pallas kernels  258 us (60%)
  waiting for transfers between devices  65.9 us (15%)
  starting transfers between devices  42 us (10%)
  other arithmetic  30.5 us (7%)
  local copies, waits for them, and re-layouts  17.4 us (4%)
  blocking collectives  8.61 us (2%)
    pallas_call x3, Pallas kernels, experts(): pl.pallas_call(functools.partial(experts_body, nb, nchunk, halves), grid_...  55.5 us
    pallas_call x3, Pallas kernels, weight_grads(): pl.pallas_call(functools.partial(weight_grads_body, nb, halves), grid=(ne...  49.6 us
    pallas_call x3, Pallas kernels, one_expert(): pl.pallas_call(functools.partial(one_expert_body, nb, halves, r), in_spec...  47.7 us
    pallas_call x2, Pallas kernels, attn_backward(): pl.pallas_call(functools.partial(attn_backward_body, first, len(parts), l...  40.8 us
    ppermute x24, starting transfers between devices, across(): return lax.ppermute(v, 'ep', [(i, i ^ k) for i in range(n_ep)])  30.2 us
    ppermute x24, waiting for transfers between devices, across(): return lax.ppermute(v, 'ep', [(i, i ^ k) for i in range(n_ep)])  29 us
    ppermute x4, waiting for transfers between devices, column_steps(): other = lax.ppermute(v, 'ep', [(i, i ^ bit * inner) for i in range(n_ep)])  24.3 us
    pallas_call x1, Pallas kernels, attn_forward(): pl.pallas_call(functools.partial(attn_forward_body, len(outs)), in_specs=...  22.6 us
  transfers between devices with their start and end apart: 45, of which 18 were waited for; matrix products, arithmetic and copies ran while one was open for 8% of the time, Pallas kernels for 56%

profile of v5, /device:TPU:0, one launch (start us, length us, event | category | flops | bytes accessed | tf_op | source)
XLA Modules:
  0.0 424.3 jit_solution(2936763675221040613)
XLA Ops:
  10.7 22.6 %attention_forward.1 = (bf16[1024,1024]{1,0:T(8,128)(2,1)}, bf16[1024,512]{1,0:T(8,128)(2,1)}, bf16[1024,512]{1,0:T(8,128)(2,1)}, bf16[1024,512]{1,0:T(8,128)(2,...) custom-call(s32[1]{0:T(128)} %bitcast.core._, ...), custom_call_target="tpu_custom_call" | custom-call | flops 236223200 | bytes 251658 | tf_op jit(solution)/shard_map/attention_forward/pallas_call | solution.py:741
  37.2 4.3 %middle_norm.1 = (f32[512,1024]{1,0:T(8,128)}, bf16[512,1024]{1,0:T(8,128)(2,1)}, f32[8,128]{1,0:T(8,128)}) custom-call(s32[1]{0:T(128)} %bitcast.core._, bf16[1024,1024]{1,0:T(8,128)(2,1)} %x.9, bf16[512,1024]{1,0:T(8,128)(2,1)} %get-tuple-element.182.own, bf16[512,1024]{1,0:T(8,128)(2,1)} %copy-done.12, bf16[1,1024]{1,0:T(2,128)(2,1)} %broadcast_in_dim.38.gain, ...), custom_call_target="tpu_custom_call" | custom-call | flops 104857 | bytes 125829 | tf_op jit(solution)/shard_map/middle_norm/pallas_call | solution.py:81
  49.5 13.7 %experts.3 = (bf16[528,1024]{1,0:T(8,128)(2,1)}, bf16[512,1024]{1,0:T(8,128)(2,1)}, bf16[2,512,512]{2,1,0:T(8,128)(2,1)}, bf16[2,512,1024]{2,1,0:T(8,128)(2,1)}, f32[512,128]{1,0:T(8,128)}) custom-call(s32[4]{0:T(128)} %and_select_fusion.3.refs_0_.ids, bf16[512,1024]{1,0:T(8,128)(2,1)} %get-tuple-element.210.refs_1_.refs_0_.h2, ...), custom_call_target="tpu_custom_call" | custom-call | flops 128849016 | bytes 251658 | tf_op jit(solution)/shard_map/experts/pallas_call | solution.py:177
  63.3 7.1 %collective-permute-done.6.refs_1_.refs_0_ = bf16[512,1024]{1,0:T(8,128)(2,1)S(1)} collective-permute-done((bf16[512,1024]{1,0:T(8,128)(2,1)}, bf16[512,1024]{1,0:T(8,128)(2,1)S(1)}, u32[]{:S(2)}, u32[]{:S(2)}) %collective-permute-start.6) | collective-permute-done | bytes 1048608 | tf_op jit(solution)/shard_map/ppermute | solution.py:947
  73.1 24.1 %experts.4 = (bf16[528,1024]{1,0:T(8,128)(2,1)}, bf16[512,1024]{1,0:T(8,128)(2,1)}, bf16[2,512,512]{2,1,0:T(8,128)(2,1)}, bf16[2,512,1024]{2,1,0:T(8,128)(2,1)},...) custom-call(s32[4]{0:T(128)} %and_select_fusion.3.refs_0_.ids, ...), custom_call_target="tpu_custom_call" | custom-call | flops 257698032 | bytes 377487 | tf_op jit(solution)/shard_map/experts/pallas_call | solution.py:177
  101.1 19.3 %one_expert.3 = (bf16[528,1024]{1,0:T(8,128)(2,1)}, bf16[512,1024]{1,0:T(8,128)(2,1)}, bf16[1,512,512]{2,1,0:T(8,128)(2,1)}, bf16[1,512,1024]{2,1,0:T(8,128)(2,1...) custom-call(s32[4]{0:T(128)} %and_select_fusion.3.refs_0_.ids, ...), custom_call_target="tpu_custom_call" | custom-call | flops 193273536 | bytes 440401 | tf_op jit(solution)/shard_map/one_expert/pallas_call | solution.py:281
  125.2 17.6 %experts.5 = (bf16[528,1024]{1,0:T(8,128)(2,1)}, bf16[512,1024]{1,0:T(8,128)(2,1)}, bf16[3,512,512]{2,1,0:T(8,128)(2,1)}, bf16[3,512,1024]{2,1,0:T(8,128)(2,1)}, f32[512,128]{1,0:T(8,128)}) custom-call(s32[4]{0:T(128)} %and_select_fusion.3.refs_0_.ids, bf16[512,1024]{1,0:T(8,128)(2,1)} %copy-done.5, ...), custom_call_target="tpu_custom_call" | custom-call | flops 193273536 | bytes 314572 | tf_op jit(solution)/shard_map/experts/pallas_call | solution.py:177
  142.8 13.7 %expert_weight_grads.3 = (bf16[1,3,1024,256]{3,2,1,0:T(8,128)(2,1)}, bf16[1,3,1024,256]{3,2,1,0:T(8,128)(2,1)}) custom-call(s32[1]{0:T(128)} %bitcast.core._, bf16[512,1024]{1,0:T(8,128)(2,1)} %get-tuple-element.210.refs_1_.refs_0_.h2, bf16[512,1024]{1,0:T(8,128)(2,1)} %copy-done.4, bf16[512,1024]{1,0:T(8,128)(2,1)} %collective-permute-done.7.refs_2_.refs_1_, ...), custom_call_target="tpu_custom_call" | custom-call | flops 128849016 | bytes 230686 | tf_op jit(solution)/shard_map/expert_weight_grads/pallas_call | solution.py:348
  165.7 19.3 %one_expert.4 = (bf16[528,1024]{1,0:T(8,128)(2,1)}, bf16[512,1024]{1,0:T(8,128)(2,1)}, bf16[1,512,512]{2,1,0:T(8,128)(2,1)}, bf16[1,512,1024]{2,1,0:T(8,128)(2,1...) custom-call(s32[4]{0:T(128)} %and_select_fusion.3.refs_0_.ids, ...), custom_call_target="tpu_custom_call" | custom-call | flops 193273536 | bytes 440401 | tf_op jit(solution)/shard_map/one_expert/pallas_call | solution.py:281
  188.6 9.1 %one_expert.5 = (bf16[528,1024]{1,0:T(8,128)(2,1)}, bf16[512,1024]{1,0:T(8,128)(2,1)}, bf16[1,512,512]{2,1,0:T(8,128)(2,1)}, bf16[1,512,1024]{2,1,0:T(8,128)(2,1)}) custom-call(s32[4]{0:T(128)} %and_select_fusion.3.refs_0_.ids, bf16[512,1024]{1,0:T(8,128)(2,1)} %get-tuple-element.210.refs_1_.refs_0_.h2, ...), custom_call_target="tpu_custom_call" | custom-call | flops 64424508 | bytes 188743 | tf_op jit(solution)/shard_map/one_expert/pallas_call | solution.py:281
  197.7 13.8 %expert_weight_grads.4 = (bf16[1,3,1024,256]{3,2,1,0:T(8,128)(2,1)}, bf16[1,3,1024,256]{3,2,1,0:T(8,128)(2,1)}) custom-call(s32[1]{0:T(128)} %bitcast.core._, bf16[512,1024]{1,0:T(8,128)(2,1)} %get-tuple-element.210.refs_1_.refs_0_.h2, bf16[512,1024]{1,0:T(8,128)(2,1)} %copy-done.4, bf16[512,1024]{1,0:T(8,128)(2,1)} %collective-permute-done.7.refs_2_.refs_1_, ...), custom_call_target="tpu_custom_call" | custom-call | flops 128849016 | bytes 230686 | tf_op jit(solution)/shard_map/expert_weight_grads/pallas_call | solution.py:348
  211.5 22.1 %expert_weight_grads.5 = (bf16[2,3,1024,256]{3,2,1,0:T(8,128)(2,1)}, bf16[2,3,1024,256]{3,2,1,0:T(8,128)(2,1)}) custom-call(s32[1]{0:T(128)} %bitcast.core._, bf16[512,1024]{1,0:T(8,128)(2,1)} %get-tuple-element.210.refs_1_.refs_0_.h2, bf16[512,1024]{1,0:T(8,128)(2,1)} %copy-done.4, bf16[512,1024]{1,0:T(8,128)(2,1)} %collective-permute-done.7.refs_2_.refs_1_, ...), custom_call_target="tpu_custom_call" | custom-call | flops 128849016 | bytes 230686 | tf_op jit(solution)/shard_map/expert_weight_grads/pallas_call | solution.py:348
  249.5 8.4 %middle_back.1 = (bf16[2,512,1024]{2,1,0:T(8,128)(2,1)}, f32[1024,128]{1,0:T(8,128)}) custom-call(s32[1]{0:T(128)} %bitcast.core._, s32[16]{0:T(128)} %pad_add_fusion.ids, bf16[512,1024]{1,0:T(8,128)(2,1)} %get-tuple-element.210.refs_1_.refs_0_.h2, f32[512,1024]{1,0:T(8,128)} %get-tuple-element.270.mid.refs_0_, bf16[1,1024]{1,0:T(2,128)(2,1)} %broadcast_in_dim.38.gain, ...), custom_call_target="tpu_custom_call" | custom-call | flops 419430 | bytes 209715 | tf_op jit(solution)/shard_map/middle_back/pallas_call | solution.py:410
  257.9 8.6 %all_to_all.5 = bf16[2,512,1024]{2,1,0:T(8,128)(2,1)} all-to-all(bf16[2,512,1024]{2,1,0:T(8,128)(2,1)} %get-tuple-element.271), channel_id=1, replica_groups=mesh['ep'=16,'tp'=2] {'tp'}, dimensions={0} | all-to-all | bytes 4194304 | tf_op jit(solution)/shard_map/all_to_all | solution.py:1156
  266.5 23.2 %attention_backward.2 = (bf16[1024,256]{1,0:T(8,128)(2,1)}, bf16[1024,256]{1,0:T(8,128)(2,1)}, f32[1024,128]{1,0:T(8,128)}, bf16[256,1024]{1,0:T(8,128)(2,1)}, b...) custom-call(s32[1]{0:T(128)} %bitcast.core._, ...), custom_call_target="tpu_custom_call" | custom-call | flops 128849016 | bytes 209715 | tf_op jit(solution)/shard_map/attention_backward/pallas_call | solution.py:902
  299.9 17.7 %attention_backward.3 = (bf16[1024,256]{1,0:T(8,128)(2,1)}, bf16[1024,256]{1,0:T(8,128)(2,1)}, f32[1024,128]{1,0:T(8,128)}, bf16[256,640]{1,0:T(8,128)(2,1)}, bf...) custom-call(s32[1]{0:T(128)} %bitcast.core._, s32[1]{0:T(128)} %bitcast.8.at.me, ...), custom_call_target="tpu_custom_call" | custom-call | flops 128849016 | bytes 209715 | tf_op jit(solution)/shard_map/attention_backward/pallas_call | solution.py:902
  317.6 5.2 %layer_out.1 = (bf16[512,1024]{1,0:T(8,128)(2,1)}, f32[8,128]{1,0:T(8,128)}) custom-call(s32[1]{0:T(128)} %bitcast.core._, f32[512,1024]{1,0:T(8,128)} %get-tuple-element.270.mid.refs_0_, f32[512,1]{1,0:T(8,128)} %copy.32.refs_1_, bf16[512,1024]{1,0:T(8,128)(2,1)} %get-tuple-element.240.refs_2_, bf16[512,1024]{1,0:T(8,128)(2,1)} %collective-permute-done.22.refs_3_, ...), custom_call_target="tpu_custom_call" | custom-call | flops 125829 | bytes 146800 | tf_op jit(solution)/shard_map/layer_out/pallas_call | solution.py:508
  328.6 6.2 %input_back.1.own = bf16[1024,1024]{1,0:T(8,128)(2,1)} custom-call(s32[1]{0:T(128)} %bitcast.core._, bf16[1024,512]{1,0:T(8,128)(2,1)} %wq.1, bf16[1024,512]{1,0:T(8,128)(2,1)} %wkv.1, bf16[1024,256]{1,0:T(8,128)(2,1)} %get-tuple-element.305.refs_0_, bf16[1024,256]{1,0:T(8,128)(2,1)} %get-tuple-element.306.refs_1_, ...), custom_call_target="tpu_custom_call" | custom-call | flops 42949672 | bytes 209715 | tf_op jit(solution)/shard_map/input_back/pallas_call | solution.py:447
  336.8 4.8 %collective-permute-done.31 = bf16[256,640]{1,0:T(8,128)(2,1)} collective-permute-done((bf16[256,640]{1,0:T(8,128)(2,1)}, bf16[256,640]{1,0:T(8,128)(2,1)}, u32[]{:S(2)}, u32[]{:S(2)}) %collective-permute-start.31) | collective-permute-done | bytes 327712 | tf_op jit(solution)/shard_map/ppermute | solution.py:947
  348.4 7.5 %token_grads.1 = f32[1024,1024]{1,0:T(8,128)} custom-call(s32[1]{0:T(128)} %bitcast.core._, bf16[1024,1024]{1,0:T(8,128)(2,1)} %x.9, bf16[1024,1024]{1,0:T(8,128)(2,1)} %cot.3, bf16[1024,1024]{1,0:T(8,128)(2,1)} %input_back.1.own, bf16[1024,1024]{1,0:T(8,128)(2,1)} %collective-permute-done.33.other, bf16[1024,1024]{1,0:T(8,128)(2,1)} %bitcast.32, ...), custom_call_target="tpu_custom_call" | custom-call | flops 251658 | bytes 293601 | tf_op jit(solution)/shard_map/token_grads/pallas_call | solution.py:472
  356.0 4.7 %maximum_select_fusion = bf16[1024,1024]{1,0:T(8,128)(2,1)} fusion(bf16[512,1024]{1,0:T(8,128)(2,1)} %collective-permute-done.34, bf16[512,1024]{1,0:T(8,128)(2,1)} %get-tuple-element.330, pred[]{:T(512)S(6)} %eq.18), kind=kLoop, calls=%fused_computation.8 | loop fusion | flops 9437184 | bytes 4194305 | tf_op jit(solution)/shard_map/jit(_where)/select_n | solution.py:1242
  360.6 11.2 %collective-permute-done.36 = bf16[256,1024]{1,0:T(8,128)(2,1)} collective-permute-done((bf16[256,1024]{1,0:T(8,128)(2,1)}, bf16[256,1024]{1,0:T(8,128)(2,1)}, u32[]{:S(2)}, u32[]{:S(2)}) %collective-permute-start.36) | collective-permute-done | bytes 524320 | tf_op jit(solution)/shard_map/ppermute | solution.py:977
  381.1 11.6 %collective-permute-done.37 = bf16[256,640]{1,0:T(8,128)(2,1)S(1)} collective-permute-done((bf16[256,640]{1,0:T(8,128)(2,1)S(1)}, bf16[256,640]{1,0:T(8,128)(2,1)S(1)}, u32[]{:S(2)}, u32[]{:S(2)}) %collective-permute-start.37) | collective-permute-done | bytes 327712 | tf_op jit(solution)/shard_map/ppermute | solution.py:977
  407.4 6.3 %collective-permute-done.39.refs_2_ = bf16[256,640]{1,0:T(8,128)(2,1)S(1)} collective-permute-done((bf16[256,640]{1,0:T(8,128)(2,1)S(1)}, bf16[256,640]{1,0:T(8,128)(2,1)S(1)}, u32[]{:S(2)}, u32[]{:S(2)}) %collective-permute-start.39) | collective-permute-done | bytes 327712 | tf_op jit(solution)/shard_map/ppermute | solution.py:947
  (180 shorter events, 120.3 us)
Async XLA Ops:
  4.1 32.2 %collective-permute-start.3 = (bf16[3,1024,256]{2,1,0:T(8,128)(2,1)}, bf16[3,1024,256]{2,1,0:T(8,128)(2,1)}, u32[]{:S(2)}, u32[]{:S(2)}) collective-permute-start(bf16[3,1024,256]{2,1,0:T(8,128)(2,1)} %get-tuple-element.180.refs_4_.refs_6_), channel_id=1, source_target_pairs={{0,1},{1,0},{2,3},{3,2},{4,5},{5,4},{6,7},{7,6},{8,9},{9,8},{10,11... | collective-permute-start | bytes 4718600 | tf_op jit(solution)/shard_map/ppermute | solution.py:953
  4.5 40.0 %collective-permute-start.4 = (bf16[3,1024,256]{2,1,0:T(8,128)(2,1)}, bf16[3,1024,256]{2,1,0:T(8,128)(2,1)}, u32[]{:S(2)}, u32[]{:S(2)}) collective-permute-start(bf16[3,1024,256]{2,1,0:T(8,128)(2,1)} %get-tuple-element.180.refs_4_.refs_6_), channel_id=1, source_target_pairs={{0,8},{2,10},{4,12},{6,14},{8,16},{10,18},{12,20},{14,22},{16,24},... | collective-permute-start | bytes 4718600 | tf_op jit(solution)/shard_map/ppermute | solution.py:950
  7.1 29.1 %collective-permute-start.1 = (bf16[528,1024]{1,0:T(8,128)(2,1)}, bf16[528,1024]{1,0:T(8,128)(2,1)S(1)}, u32[]{:S(2)}, u32[]{:S(2)}) collective-permute-start(bf16[528,1024]{1,0:T(8,128)(2,1)} %get-tuple-element.197.refs_2_.refs_3_.refs_4_.refs_1_), channel_id=1, source_target_pairs={{0,2},{2,0},{4,6},{6,4},{8,10},{10,8},{12,14},{14,12},{16,18},{18,... | collective-permute-start | bytes 3244040 | tf_op jit(solution)/shard_map/ppermute | solution.py:947
  8.6 27.7 %collective-permute-start.2 = (bf16[528,1024]{1,0:T(8,128)(2,1)}, bf16[528,1024]{1,0:T(8,128)(2,1)S(1)}, u32[]{:S(2)}, u32[]{:S(2)}) collective-permute-start(bf16[528,1024]{1,0:T(8,128)(2,1)} %get-tuple-element.197.refs_2_.refs_3_.refs_4_.refs_1_), channel_id=1, source_target_pairs={{0,4},{2,6},{4,0},{6,2},{8,12},{10,14},{12,8},{14,10},{16,20},{18,... | collective-permute-start | bytes 3244040 | tf_op jit(solution)/shard_map/ppermute | solution.py:947
  44.5 25.8 %collective-permute-start.6 = (bf16[512,1024]{1,0:T(8,128)(2,1)}, bf16[512,1024]{1,0:T(8,128)(2,1)S(1)}, u32[]{:S(2)}, u32[]{:S(2)}) collective-permute-start(bf16[512,1024]{1,0:T(8,128)(2,1)} %get-tuple-element.210.refs_1_.refs_0_.h2), channel_id=1, source_target_pairs={{0,2},{2,0},{4,6},{6,4},{8,10},{10,8},{12,14},{14,12},{16,18},{18,... | collective-permute-start | bytes 3145736 | tf_op jit(solution)/shard_map/ppermute | solution.py:947
  46.0 25.6 %collective-permute-start.7 = (bf16[512,1024]{1,0:T(8,128)(2,1)}, bf16[512,1024]{1,0:T(8,128)(2,1)}, u32[]{:S(2)}, u32[]{:S(2)}) collective-permute-start(bf16[512,1024]{1,0:T(8,128)(2,1)} %get-tuple-element.210.refs_1_.refs_0_.h2), channel_id=1, source_target_pairs={{0,4},{2,6},{4,0},{6,2},{8,12},{10,14},{12,8},{14,10},{16,20},{18,... | collective-permute-start | bytes 3145736 | tf_op jit(solution)/shard_map/ppermute | solution.py:947
  47.5 49.7 %collective-permute-start.8 = (bf16[3,1024,256]{2,1,0:T(8,128)(2,1)}, bf16[3,1024,256]{2,1,0:T(8,128)(2,1)}, u32[]{:S(2)}, u32[]{:S(2)}) collective-permute-start(bf16[3,1024,256]{2,1,0:T(8,128)(2,1)} %collective-permute-done.4.refs_6_.refs_8_), channel_id=1, source_target_pairs={{0,8},{2,10},{4,12},{6,14},{8,16},{10,18},{12,20},{14,22},{16,24},... | collective-permute-start | bytes 4718600 | tf_op jit(solution)/shard_map/ppermute | solution.py:950
  71.6 26.2 %collective-permute-start.9 = (bf16[528,1024]{1,0:T(8,128)(2,1)S(1)}, bf16[528,1024]{1,0:T(8,128)(2,1)}, u32[]{:S(2)}, u32[]{:S(2)}) collective-permute-start(bf16[528,1024]{1,0:T(8,128)(2,1)S(1)} %copy-done.1), channel_id=1, source_target_pairs={{0,6},{2,4},{4,2},{6,0},{8,14},{10,12},{12,10},{14,8},{16,22},{18,... | collective-permute-start | bytes 3244040 | tf_op jit(solution)/shard_map/ppermute | solution.py:947
  97.4 45.4 %collective-permute-start.12 = (bf16[3,1024,256]{2,1,0:T(8,128)(2,1)}, bf16[3,1024,256]{2,1,0:T(8,128)(2,1)}, u32[]{:S(2)}, u32[]{:S(2)}) collective-permute-start(bf16[3,1024,256]{2,1,0:T(8,128)(2,1)} %collective-permute-done.8.refs_15_.refs_8_), channel_id=1, source_target_pairs={{0,8},{2,10},{4,12},{6,14},{8,16},{10,18},{12,20},{14,22},{16,24},... | collective-permute-start | bytes 4718600 | tf_op jit(solution)/shard_map/ppermute | solution.py:950
  97.8 26.3 %collective-permute-start.11 = (bf16[512,1024]{1,0:T(8,128)(2,1)S(1)}, bf16[512,1024]{1,0:T(8,128)(2,1)S(1)}, u32[]{:S(2)}, u32[]{:S(2)}) collective-permute-start(bf16[512,1024]{1,0:T(8,128)(2,1)S(1)} %copy-done), channel_id=1, source_target_pairs={{0,6},{2,4},{4,2},{6,0},{8,14},{10,12},{12,10},{14,8},{16,22},{18,... | collective-permute-start | bytes 3145736 | tf_op jit(solution)/shard_map/ppermute | solution.py:947
  163.2 72.1 %collective-permute-start.18 = (bf16[3,1024,256]{2,1,0:T(8,128)(2,1)}, bf16[3,1024,256]{2,1,0:T(8,128)(2,1)}, u32[]{:S(2)}, u32[]{:S(2)}) collective-permute-start(bf16[3,1024,256]{2,1,0:T(8,128)(2,1)} %fusion), channel_id=1, source_target_pairs={{0,8},{2,10},{4,12},{6,14},{8,16},{10,18},{12,20},{14,22},{16,24},... | collective-permute-start | bytes 4718600 | tf_op jit(solution)/shard_map/ppermute | solution.py:950
  185.0 48.5 %collective-permute-start.15 = (bf16[528,1024]{1,0:T(8,128)(2,1)}, bf16[528,1024]{1,0:T(8,128)(2,1)S(1)}, u32[]{:S(2)}, u32[]{:S(2)}) collective-permute-start(bf16[528,1024]{1,0:T(8,128)(2,1)} %get-tuple-element.261), channel_id=1, source_target_pairs={{0,2},{2,0},{4,6},{6,4},{8,10},{10,8},{12,14},{14,12},{16,18},{18,... | collective-permute-start | bytes 3244040 | tf_op jit(solution)/shard_map/ppermute | solution.py:947
  186.6 48.7 %collective-permute-start.16 = (bf16[528,1024]{1,0:T(8,128)(2,1)}, bf16[528,1024]{1,0:T(8,128)(2,1)S(1)}, u32[]{:S(2)}, u32[]{:S(2)}) collective-permute-start(bf16[528,1024]{1,0:T(8,128)(2,1)} %get-tuple-element.262), channel_id=1, source_target_pairs={{0,4},{2,6},{4,0},{6,2},{8,12},{10,14},{12,8},{14,10},{16,20},{18,... | collective-permute-start | bytes 3244040 | tf_op jit(solution)/shard_map/ppermute | solution.py:947
  187.1 48.2 %collective-permute-start.17 = (bf16[528,1024]{1,0:T(8,128)(2,1)}, bf16[528,1024]{1,0:T(8,128)(2,1)S(1)}, u32[]{:S(2)}, u32[]{:S(2)}) collective-permute-start(bf16[528,1024]{1,0:T(8,128)(2,1)} %get-tuple-element.263), channel_id=1, source_target_pairs={{0,6},{2,4},{4,2},{6,0},{8,14},{10,12},{12,10},{14,8},{16,22},{18,... | collective-permute-start | bytes 3244040 | tf_op jit(solution)/shard_map/ppermute | solution.py:947
  242.7 47.0 %collective-permute-start.21 = (bf16[2,3,1024,256]{3,2,1,0:T(8,128)(2,1)}, bf16[2,3,1024,256]{3,2,1,0:T(8,128)(2,1)}, u32[]{:S(2)}, u32[]{:S(2)}) collective-permute-start(bf16[2,3,1024,256]{3,2,1,0:T(8,128)(2,1)} %get-tuple-element.287), channel_id=1, source_target_pairs={{0,1},{1,0},{2,3},{3,2},{4,5},{5,4},{6,7},{7,6},{8,9},{9,8},{10,11... | collective-permute-start | bytes 9437192 | tf_op jit(solution)/shard_map/ppermute | solution.py:953
  242.9 46.8 %collective-permute-start.20 = (bf16[3,1024,256]{2,1,0:T(8,128)(2,1)}, bf16[3,1024,256]{2,1,0:T(8,128)(2,1)}, u32[]{:S(2)}, u32[]{:S(2)}) collective-permute-start(bf16[3,1024,256]{2,1,0:T(8,128)(2,1)} %fusion.2), channel_id=1, source_target_pairs={{0,8},{2,10},{4,12},{6,14},{8,16},{10,18},{12,20},{14,22},{16,24},... | collective-permute-start | bytes 4718600 | tf_op jit(solution)/shard_map/ppermute | solution.py:950
  244.5 51.5 %collective-permute-start.24 = (bf16[512,1024]{1,0:T(8,128)(2,1)}, bf16[512,1024]{1,0:T(8,128)(2,1)}, u32[]{:S(2)}, u32[]{:S(2)}) collective-permute-start(bf16[512,1024]{1,0:T(8,128)(2,1)} %get-tuple-element.297), channel_id=1, source_target_pairs={{0,6},{2,4},{4,2},{6,0},{8,14},{10,12},{12,10},{14,8},{16,22},{18,... | collective-permute-start | bytes 3145736 | tf_op jit(solution)/shard_map/ppermute | solution.py:947
  245.6 51.5 %collective-permute-start.23 = (bf16[512,1024]{1,0:T(8,128)(2,1)}, bf16[512,1024]{1,0:T(8,128)(2,1)}, u32[]{:S(2)}, u32[]{:S(2)}) collective-permute-start(bf16[512,1024]{1,0:T(8,128)(2,1)} %get-tuple-element.295), channel_id=1, source_target_pairs={{0,4},{2,6},{4,0},{6,2},{8,12},{10,14},{12,8},{14,10},{16,20},{18,... | collective-permute-start | bytes 3145736 | tf_op jit(solution)/shard_map/ppermute | solution.py:947
  248.0 69.5 %collective-permute-start.22 = (bf16[512,1024]{1,0:T(8,128)(2,1)}, bf16[512,1024]{1,0:T(8,128)(2,1)}, u32[]{:S(2)}, u32[]{:S(2)}) collective-permute-start(bf16[512,1024]{1,0:T(8,128)(2,1)} %get-tuple-element.293), channel_id=1, source_target_pairs={{0,2},{2,0},{4,6},{6,4},{8,10},{10,8},{12,14},{14,12},{16,18},{18,... | collective-permute-start | bytes 3145736 | tf_op jit(solution)/shard_map/ppermute | solution.py:947
  293.3 49.8 %collective-permute-start.28 = (bf16[3,1024,256]{2,1,0:T(8,128)(2,1)}, bf16[3,1024,256]{2,1,0:T(8,128)(2,1)}, u32[]{:S(2)}, u32[]{:S(2)}) collective-permute-start(bf16[3,1024,256]{2,1,0:T(8,128)(2,1)} %fusion.1), channel_id=1, source_target_pairs={{0,8},{2,10},{4,12},{6,14},{8,16},{10,18},{12,20},{14,22},{16,24},... | collective-permute-start | bytes 4718600 | tf_op jit(solution)/shard_map/ppermute | solution.py:950
  295.4 27.3 %collective-permute-start.25 = (bf16[256,1024]{1,0:T(8,128)(2,1)}, bf16[256,1024]{1,0:T(8,128)(2,1)}, u32[]{:S(2)}, u32[]{:S(2)}) collective-permute-start(bf16[256,1024]{1,0:T(8,128)(2,1)} %get-tuple-element.301), channel_id=1, source_target_pairs={{0,2},{2,0},{4,6},{6,4},{8,10},{10,8},{12,14},{14,12},{16,18},{18,... | collective-permute-start | bytes 1572872 | tf_op jit(solution)/shard_map/ppermute | solution.py:947
  296.0 26.8 %collective-permute-start.26 = (bf16[256,1024]{1,0:T(8,128)(2,1)}, bf16[256,1024]{1,0:T(8,128)(2,1)}, u32[]{:S(2)}, u32[]{:S(2)}) collective-permute-start(bf16[256,1024]{1,0:T(8,128)(2,1)} %get-tuple-element.302), channel_id=1, source_target_pairs={{0,4},{2,6},{4,0},{6,2},{8,12},{10,14},{12,8},{14,10},{16,20},{18,... | collective-permute-start | bytes 1572872 | tf_op jit(solution)/shard_map/ppermute | solution.py:947
  297.2 25.6 %collective-permute-start.27 = (bf16[256,1024]{1,0:T(8,128)(2,1)}, bf16[256,1024]{1,0:T(8,128)(2,1)}, u32[]{:S(2)}, u32[]{:S(2)}) collective-permute-start(bf16[256,1024]{1,0:T(8,128)(2,1)} %get-tuple-element.303), channel_id=1, source_target_pairs={{0,6},{2,4},{4,2},{6,0},{8,14},{10,12},{12,10},{14,8},{16,22},{18,... | collective-permute-start | bytes 1572872 | tf_op jit(solution)/shard_map/ppermute | solution.py:947
  345.8 26.0 %collective-permute-start.36 = (bf16[256,1024]{1,0:T(8,128)(2,1)}, bf16[256,1024]{1,0:T(8,128)(2,1)}, u32[]{:S(2)}, u32[]{:S(2)}) collective-permute-start(bf16[256,1024]{1,0:T(8,128)(2,1)} %add_convert_fusion.1), channel_id=1, source_target_pairs={{0,16},{2,18},{4,20},{6,22},{8,24},{10,26},{12,28},{14,30},{16,0},... | collective-permute-start | bytes 1572872 | tf_op jit(solution)/shard_map/ppermute | solution.py:977
  (46 other events, 523.8 us)
